TPU v7x, 32 devices: a whole 2x2x4 slice. The times are simulated.
32 devices in a mesh: ctx: 16 (over z, x, core), fsdp: 2 (over y).
Axes of the slice: x: 2, y: 2, z: 4, core: 2. Of those that a mesh axis runs over, the one named last changes fastest.
Arguments:
- tokens: bfloat16 [12, 2048, 576], P('fsdp', 'ctx'), may hold values from -6 to 6
- cotangent: bfloat16 [12, 2048, 576], P('fsdp', 'ctx'), may hold values from -8 to 8
- pair_order: int32 [12, 16], P('fsdp'), may hold values from 0 to 15, each once within a row
- query_weight: float32 [576, 576], P('fsdp', 'ctx'), may hold values from -0.5 to 0.5
- key_master_weight: float32 [576, 192], P('fsdp', 'ctx'), may hold values from -0.25 to 0.25
- value_master_weight: float32 [576, 192], P('fsdp', 'ctx'), may hold values from -0.25 to 0.25
- output_weight: float32 [576, 576], P('fsdp', 'ctx'), may hold values from -1.5 to 1.5
- gate_weight: float32 [576, 1536], P('fsdp', 'ctx'), may hold values from -0.25 to 0.25
- up_weight: float32 [576, 1536], P('fsdp', 'ctx'), may hold values from -0.25 to 0.25
- down_weight: float32 [1536, 576], P('fsdp', 'ctx'), may hold values from -0.21875 to 0.21875
- norm_gains: float32 [576, 2], P('fsdp'), may hold values from 0.5 to 1.5
- query_first: float32 [576, 576], P('fsdp', 'ctx'), may hold values from -224 to 224
- key_first_moment: float32 [576, 192], P('fsdp', 'ctx'), may hold values from -448 to 448
- value_first_moment: float32 [576, 192], P('fsdp', 'ctx'), may hold values from -320 to 320
- output_first: float32 [576, 576], P('fsdp', 'ctx'), may hold values from -20 to 20
- gate_first: float32 [576, 1536], P('fsdp', 'ctx'), may hold values from -56 to 56
- up_first: float32 [576, 1536], P('fsdp', 'ctx'), may hold values from -56 to 56
- down_first: float32 [1536, 576], P('fsdp', 'ctx'), may hold values from -64 to 64
- gains_first: float32 [576, 2], P('fsdp'), may hold values from -256 to 256
- query_second: float32 [576, 576], P('fsdp', 'ctx'), may hold values from 5160.96 to 20643.84
- key_second_moment: float32 [576, 192], P('fsdp', 'ctx'), may hold values from 20643.84 to 82821.12
- value_second_moment: float32 [576, 192], P('fsdp', 'ctx'), may hold values from 11550.72 to 46448.64
- output_second: float32 [576, 576], P('fsdp', 'ctx'), may hold values from 51.6096 to 206.4384
- gate_second: float32 [576, 1536], P('fsdp', 'ctx'), may hold values from 321.9456 to 1292.6976
- up_second: float32 [576, 1536], P('fsdp', 'ctx'), may hold values from 321.9456 to 1292.6976
- down_second: float32 [1536, 576], P('fsdp', 'ctx'), may hold values from 464.4864 to 1862.8608
- gains_second: float32 [576, 2], P('fsdp'), may hold values from 454.656 to 1818.624
Outputs:
- block_output: float32 [12, 2048, 576], P('fsdp', 'ctx')
- input_gradient: float32 [12, 2048, 576], P('fsdp', 'ctx')
- query_next: float32 [576, 576], P('fsdp', 'ctx')
- key_next: float32 [576, 192], P('fsdp', 'ctx')
- value_next: float32 [576, 192], P('fsdp', 'ctx')
- output_next: float32 [576, 576], P('fsdp', 'ctx')
- gate_next: float32 [576, 1536], P('fsdp', 'ctx')
- up_next: float32 [576, 1536], P('fsdp', 'ctx')
- down_next: float32 [1536, 576], P('fsdp', 'ctx')
- gains_next: float32 [576, 2], P('fsdp')
- query_first_next: float32 [576, 576], P('fsdp', 'ctx')
- key_first_next: float32 [576, 192], P('fsdp', 'ctx')
- value_first_next: float32 [576, 192], P('fsdp', 'ctx')
- output_first_next: float32 [576, 576], P('fsdp', 'ctx')
- gate_first_next: float32 [576, 1536], P('fsdp', 'ctx')
- up_first_next: float32 [576, 1536], P('fsdp', 'ctx')
- down_first_next: float32 [1536, 576], P('fsdp', 'ctx')
- gains_first_next: float32 [576, 2], P('fsdp')
- query_second_next: float32 [576, 576], P('fsdp', 'ctx')
- key_second_next: float32 [576, 192], P('fsdp', 'ctx')
- value_second_next: float32 [576, 192], P('fsdp', 'ctx')
- output_second_next: float32 [576, 576], P('fsdp', 'ctx')
- gate_second_next: float32 [576, 1536], P('fsdp', 'ctx')
- up_second_next: float32 [576, 1536], P('fsdp', 'ctx')
- down_second_next: float32 [1536, 576], P('fsdp', 'ctx')
- gains_second_next: float32 [576, 2], P('fsdp')
Inputs may be any that keep to these rules, and one draw needn't show every extreme that they name: `pair_order`: each row is a permutation of 0 to 15.
All inputs are finite; a program needn't handle non-finite values.
Results may differ from a plain program's by a relative error of at most 0.024.
Values may be sent and summed in bfloat16 or wider, within the bound.
No kernel may reach another device: no remote copies, remote signals or barrier semaphores. Data moves between devices by JAX's collectives and lax.ppermute only.
A program may use at most 192 MiB of HBM per device.

v0:
```python
import functools

import jax
import jax.numpy as jnp
from jax import lax
from jax.experimental import pallas as pl
from jax.experimental.pallas import tpu as pltpu
from jax.sharding import PartitionSpec as P

MODEL_WIDTH = 576
FF = 1536
HEADS = 9
KV_HEADS = 3
HEAD_DIM = 64
STEP = 10
GROUP = HEADS // KV_HEADS
KEY_WIDTH = KV_HEADS * HEAD_DIM
QUERY_WIDTH = HEADS * HEAD_DIM
PACK = 2 * HEAD_DIM
KV_PACKED = KV_HEADS * PACK
TILE = 256
FF_CHUNK = 640
LANES = 640
INNER = 1024
REST = FF // 2 - LANES

NORM_EPS = 1e-05
ROPE_BASE = 100000.0
BETA_ONE = 0.9
BETA_TWO = 0.95
ADAM_EPS = 1e-08
DECAY = 0.1
GAIN_RATE = 0.5
MASKED = -1e30
FLOPS_PER_US = 1153.5e6
VMEM_BYTES = 56 * 1024 * 1024

f32 = jnp.float32
bf16 = jnp.bfloat16


def dot_nt(a, b):
    return lax.dot_general(a, b, (((1,), (1,)), ((), ())), preferred_element_type=f32)


def dot_nn(a, b):
    return lax.dot_general(a, b, (((1,), (0,)), ((), ())), preferred_element_type=f32)


def lanes_of(shape):
    return lax.broadcasted_iota(jnp.int32, shape, len(shape) - 1)


def turned(v, first):
    lane = lanes_of(v.shape) % HEAD_DIM
    ahead = pltpu.roll(v, PACK - HEAD_DIM // 2, 1)
    behind = pltpu.roll(v, HEAD_DIM // 2, 1)
    if first:
        return jnp.where(lane < HEAD_DIM // 2, -ahead, behind)
    return jnp.where(lane < HEAD_DIM // 2, ahead, -behind)


def project_kernel(x_ref, gain_ref, weight_ref, cos_ref, sin_ref, normed_ref, query_ref, kv_ref):
    rows = x_ref.shape[1]
    blk = query_ref.shape[3] // GROUP
    x = x_ref[0].astype(f32)
    inv = lax.rsqrt(jnp.mean(x * x, axis=-1, keepdims=True) + NORM_EPS)
    normed = (x * inv * gain_ref[...]).astype(bf16)
    normed_ref[0] = normed
    raw = dot_nt(normed, weight_ref[...])
    cosine, sine = cos_ref[0], sin_ref[0]
    low_half = lanes_of((rows, PACK)) < HEAD_DIM
    for j in range(KV_HEADS):
        part = raw[:, j * PACK : (j + 1) * PACK]
        spun = part * cosine + turned(part, True) * sine
        kv_ref[0, :, j * PACK : (j + 1) * PACK] = jnp.where(low_half, spun, part).astype(bf16)
    for i in range((HEADS + 1) // 2):
        begin = KV_PACKED + i * PACK
        if 2 * i + 1 < HEADS:
            part = raw[:, begin : begin + PACK]
        else:
            tail = raw[:, begin : begin + HEAD_DIM]
            part = jnp.concatenate([tail, tail], axis=1)
        spun = part * cosine + turned(part, True) * sine
        spun = spun.astype(bf16).astype(f32) * (HEAD_DIM**-0.5)
        pair = [jnp.where(low_half, spun, 0.0)]
        if 2 * i + 1 < HEADS:
            pair.append(jnp.where(low_half, pltpu.roll(spun, HEAD_DIM, 1), 0.0))
        for offset, value in enumerate(pair):
            head = 2 * i + offset
            j, member = head // GROUP, head % GROUP
            value = value.astype(bf16)
            for b in range(rows // blk):
                query_ref[0, b, j, member * blk : (member + 1) * blk, :] = value[
                    b * blk : (b + 1) * blk
                ]


def sort_blocks(blocks_ref, s, kv_refs, sorted_ref, blk):
    per = kv_refs[0].shape[1] // blk
    for g, kv_ref in enumerate(kv_refs):
        for b in range(per):
            place = pl.multiple_of(blocks_ref[s, g * per + b] * blk, blk)
            sorted_ref[pl.ds(place, blk), :] = kv_ref[0, b * blk : (b + 1) * blk, :]


def allowed_mask(place, tile_begin, blk, rows):
    row = lax.broadcasted_iota(jnp.int32, (rows, TILE), 0) % blk
    col = lax.broadcasted_iota(jnp.int32, (rows, TILE), 1)
    return col <= row + (place * blk - tile_begin)


def attend_kernel(chunks, blocks_ref, query_ref, *refs):
    s = pl.program_id(0)
    kv_refs = refs[:chunks]
    out_ref, log_ref, sorted_ref, score_ref, top_ref, acc_ref = refs[chunks:]
    per, rows = query_ref.shape[1], query_ref.shape[3]
    blk = rows // GROUP
    sort_blocks(blocks_ref, s, kv_refs, sorted_ref, blk)
    lane = lanes_of((TILE, PACK))
    for b in range(per):
        place = blocks_ref[s, b]
        full = (place * blk) // TILE

        def score_tile(t, masked):
            begin = pl.multiple_of(t * TILE, TILE)
            for j in range(KV_HEADS):
                kv = sorted_ref[pl.ds(begin, TILE), j * PACK : (j + 1) * PACK]
                score = dot_nt(query_ref[0, b, j], kv)
                if masked:
                    score = jnp.where(allowed_mask(place, begin, blk, rows), score, MASKED)
                score_ref[j, t] = score
                best = jnp.maximum(score[:, :PACK], score[:, PACK:])
                top_ref[j] = jnp.maximum(top_ref[j], best)

        top_ref[...] = jnp.full(top_ref.shape, MASKED, f32)
        acc_ref[...] = jnp.zeros(acc_ref.shape, f32)

        @pl.loop(0, full)
        def _(t):
            score_tile(t, False)

        score_tile(full, True)
        for j in range(KV_HEADS):
            top = jnp.max(top_ref[j], axis=-1, keepdims=True)
            top_ref[j] = jnp.broadcast_to(top, (rows, PACK))

        @pl.loop(0, full + 1)
        def _(t):
            begin = pl.multiple_of(t * TILE, TILE)
            for j in range(KV_HEADS):
                kv = sorted_ref[pl.ds(begin, TILE), j * PACK : (j + 1) * PACK]
                ones_v = jnp.where(lane < HEAD_DIM, jnp.ones((), bf16), kv)
                top = top_ref[j]
                score = score_ref[j, t]
                prob = jnp.concatenate(
                    [jnp.exp(score[:, :PACK] - top), jnp.exp(score[:, PACK:] - top)], axis=1
                )
                acc_ref[j] += dot_nn(prob.astype(bf16), ones_v)

        for j in range(KV_HEADS):
            acc = acc_ref[j]
            low_half = lanes_of(acc.shape) < HEAD_DIM
            total = jnp.where(low_half, acc, pltpu.roll(acc, HEAD_DIM, 1))
            log_ref[0, b, j] = top_ref[j] + jnp.log(total)
            attended = (acc / total).astype(bf16)
            for member in range(GROUP):
                head = j * GROUP + member
                out_ref[0, b * blk : (b + 1) * blk, head * HEAD_DIM : (head + 1) * HEAD_DIM] = (
                    attended[member * blk : (member + 1) * blk, HEAD_DIM:]
                )


def unpack_second(place_ref, part_refs, pack_ref, sems, out_w_ref, gate_w_ref, up_w_ref, down_w_ref):
    ctx = pack_ref.shape[1]
    f_cols, o_cols, half = FF // ctx, MODEL_WIDTH // ctx, MODEL_WIDTH // 2
    copies = []
    for part, part_ref in enumerate(part_refs):
        core = jnp.abs(place_ref[0] - part // 2)
        plane = jnp.abs(place_ref[1] - part % 2)
        for k in range(part_ref.shape[0]):
            index = 2 * place_ref[2 + k] + core
            copies.append(
                pltpu.make_async_copy(
                    part_ref.at[k], pack_ref.at[plane, index], sems.at[part, k]
                )
            )
    for copy in copies:
        copy.start()
    for copy in copies:
        copy.wait()
    for c in range(ctx):
        here = slice(c * f_cols, (c + 1) * f_cols)
        low, high = pack_ref[0, c, :f_cols, :], pack_ref[1, c, :f_cols, :]
        gate_w_ref[here, :] = jnp.concatenate([low[:, :half], high[:, :half]], axis=1)
        up_w_ref[here, :] = jnp.concatenate(
            [low[:, half:MODEL_WIDTH], high[:, half:MODEL_WIDTH]], axis=1
        )

    def natural(plane, base, lanes):
        pieces = [
            pack_ref[plane, c, base : base + o_cols, lanes].astype(f32) for c in range(ctx)
        ]
        return jnp.concatenate(pieces, axis=0).astype(bf16)

    base = f_cols + o_cols
    for plane in range(2):
        begin = plane * (FF // 2)
        down_w_ref[:, begin : begin + LANES] = natural(plane, f_cols, slice(0, LANES))
        down_w_ref[:, begin + LANES : begin + FF // 2] = natural(plane, base, slice(0, REST))
    out_w_ref[...] = jnp.concatenate(
        [natural(plane, base, slice(REST, REST + half)) for plane in range(2)], axis=1
    )


def middle_kernel(
    place_ref,
    x_ref,
    attn_ref,
    cot_ref,
    gain_ref,
    part_a_ref,
    part_b_ref,
    part_c_ref,
    part_d_ref,
    block_ref,
    normed_ref,
    hidden_ref,
    dgate_ref,
    dup_ref,
    dattn_ref,
    dout_ref,
    dresid_ref,
    gain_grad_ref,
    out_w_ref,
    gate_w_ref,
    up_w_ref,
    down_w_ref,
    pack_ref,
    sems,
):
    @pl.when(pl.program_id(0) == 0)
    def _():
        parts = (part_a_ref, part_b_ref, part_c_ref, part_d_ref)
        unpack_second(
            place_ref, parts, pack_ref, sems, out_w_ref, gate_w_ref, up_w_ref, down_w_ref
        )

    attn = attn_ref[0]
    cot = cot_ref[0]
    resid = x_ref[0].astype(f32) + dot_nt(attn, out_w_ref[...])
    inv = lax.rsqrt(jnp.mean(resid * resid, axis=-1, keepdims=True) + NORM_EPS)
    hat = resid * inv
    gain = gain_ref[...]
    normed = (hat * gain).astype(bf16)
    normed_ref[0] = normed
    block = resid
    dnormed = jnp.zeros(resid.shape, f32)
    for begin in range(0, FF, FF_CHUNK):
        span = slice(begin, min(begin + FF_CHUNK, FF))
        gate = dot_nt(normed, gate_w_ref[span, :])
        up = dot_nt(normed, up_w_ref[span, :])
        sig = 1.0 / (1.0 + jnp.exp(-gate))
        act = gate * sig
        hidden = (act * up).astype(bf16)
        hidden_ref[0, :, span] = hidden
        block = block + dot_nt(hidden, down_w_ref[:, span])
        dhidden = dot_nn(cot, down_w_ref[:, span])
        dgate = (dhidden * up * (sig * (1.0 + gate * (1.0 - sig)))).astype(bf16)
        dup = (dhidden * act).astype(bf16)
        dgate_ref[0, :, span] = dgate
        dup_ref[0, :, span] = dup
        dnormed = dnormed + dot_nn(dgate, gate_w_ref[span, :]) + dot_nn(dup, up_w_ref[span, :])
    block_ref[0] = block
    gain_grad_ref[0] = jnp.sum(dnormed * hat, axis=0, keepdims=True)
    scaled = dnormed * gain
    dresid = cot.astype(f32) + inv * (scaled - hat * jnp.mean(scaled * hat, axis=-1, keepdims=True))
    dresid_ref[0] = dresid
    dattn = dresid.astype(bf16)
    dattn_ref[0] = dattn
    dout_ref[0] = dot_nn(dattn, out_w_ref[...]).astype(bf16)


def attend_back_kernel(chunks, first, blocks_ref, query_ref, *refs):
    s = first + pl.program_id(0)
    kv_refs = refs[:chunks]
    out_ref, dout_ref, log_ref, cos_ref, sin_ref, dquery_ref = refs[chunks : chunks + 6]
    dkv_refs = refs[chunks + 6 : 2 * chunks + 6]
    sorted_ref, both_ref, flip_ref, delta_ref, dq_ref, dkv_t_ref, dkv_s_ref = refs[2 * chunks + 6 :]
    per, rows = query_ref.shape[1], query_ref.shape[3]
    blk = rows // GROUP
    length = sorted_ref.shape[0]
    sort_blocks(blocks_ref, s, kv_refs, sorted_ref, blk)
    dkv_t_ref[...] = jnp.zeros(dkv_t_ref.shape, f32)
    for b in range(per):
        place = blocks_ref[s, b]
        full = (place * blk) // TILE
        span = slice(b * blk, (b + 1) * blk)
        for j in range(KV_HEADS):
            both_ref[j, :rows] = query_ref[0, b, j]
            for member in range(GROUP):
                head = j * GROUP + member
                lanes = slice(head * HEAD_DIM, (head + 1) * HEAD_DIM)
                dout = dout_ref[0, span, lanes]
                delta = jnp.sum(
                    dout.astype(f32) * out_ref[0, span, lanes].astype(f32), axis=-1, keepdims=True
                )
                here = slice(member * blk, (member + 1) * blk)
                delta_ref[j, here] = jnp.broadcast_to(delta, (blk, PACK))
                both_ref[j, rows + member * blk : rows + (member + 1) * blk] = jnp.concatenate(
                    [jnp.zeros_like(dout), dout], axis=1
                )
            flip_ref[j] = both_ref[j].T
        dq_ref[...] = jnp.zeros(dq_ref.shape, f32)

        def tile_step(t, masked):
            begin = pl.multiple_of(t * TILE, TILE)
            kvs = [
                sorted_ref[pl.ds(begin, TILE), j * PACK : (j + 1) * PACK] for j in range(KV_HEADS)
            ]
            joined = [dot_nt(both_ref[j], kvs[j]) for j in range(KV_HEADS)]
            dscores, joints = [], []
            for j in range(KV_HEADS):
                score, dprob = joined[j][:rows], joined[j][rows:]
                log_total = log_ref[0, b, j]
                delta = delta_ref[j]
                prob = jnp.concatenate(
                    [jnp.exp(score[:, :PACK] - log_total), jnp.exp(score[:, PACK:] - log_total)],
                    axis=1,
                )
                if masked:
                    prob = jnp.where(allowed_mask(place, begin, blk, rows), prob, 0.0)
                dscore = prob * jnp.concatenate(
                    [dprob[:, :PACK] - delta, dprob[:, PACK:] - delta], axis=1
                )
                dscores.append(dscore.astype(bf16))
                joints.append(jnp.concatenate([dscores[j], prob.astype(bf16)], axis=0))
            dqs = [dot_nn(dscores[j], kvs[j]) for j in range(KV_HEADS)]
            dkvs = [dot_nn(flip_ref[j], joints[j]) for j in range(KV_HEADS)]
            for j in range(KV_HEADS):
                dq_ref[j] += dqs[j]
                dkv_t_ref[j * PACK : (j + 1) * PACK, pl.ds(begin, TILE)] += dkvs[j]

        @pl.loop(0, full)
        def _(t):
            tile_step(t, False)

        tile_step(full, True)
        cosine, sine = cos_ref[0, span, :], sin_ref[0, span, :]
        for j in range(KV_HEADS):
            for member in range(GROUP):
                head = j * GROUP + member
                grad = dq_ref[j, member * blk : (member + 1) * blk]
                back = (grad * cosine + turned(grad, False) * sine) * (HEAD_DIM**-0.5)
                dquery_ref[0, span, head * HEAD_DIM : (head + 1) * HEAD_DIM] = back[
                    :, :HEAD_DIM
                ].astype(bf16)
    for begin in range(0, length, TILE):
        dkv_s_ref[begin : begin + TILE, :] = dkv_t_ref[:, begin : begin + TILE].T.astype(bf16)
    for g, dkv_ref in enumerate(dkv_refs):
        for b in range(per):
            place = pl.multiple_of(blocks_ref[s, g * per + b] * blk, blk)
            dkv_ref[0, b * blk : (b + 1) * blk, :] = dkv_s_ref[pl.ds(place, blk), :]


def final_kernel(
    x_ref,
    gain_ref,
    dquery_ref,
    dkv_ref,
    dresid_ref,
    cos_ref,
    sin_ref,
    weight_ref,
    dinput_ref,
    dall_ref,
    gain_grad_ref,
):
    rows = x_ref.shape[1]
    cosine, sine = cos_ref[0], sin_ref[0]
    low_half = lanes_of((rows, PACK)) < HEAD_DIM
    for j in range(KV_HEADS):
        part = dkv_ref[0, :, j * PACK : (j + 1) * PACK].astype(f32)
        back = part * cosine + turned(part, False) * sine
        dall_ref[0, :, j * PACK : (j + 1) * PACK] = jnp.where(low_half, back, part).astype(bf16)
    used = KV_PACKED + QUERY_WIDTH
    dall_ref[0, :, KV_PACKED:used] = dquery_ref[0]
    dall_ref[0, :, used:] = jnp.zeros((rows, INNER - used), bf16)
    dnormed = dot_nn(dall_ref[0, :, :used], weight_ref[...])
    x = x_ref[0].astype(f32)
    inv = lax.rsqrt(jnp.mean(x * x, axis=-1, keepdims=True) + NORM_EPS)
    hat = x * inv
    gain_grad_ref[0] = jnp.sum(dnormed * hat, axis=0, keepdims=True)
    scaled = dnormed * gain_ref[...]
    dinput_ref[0] = dresid_ref[0] + inv * (
        scaled - hat * jnp.mean(scaled * hat, axis=-1, keepdims=True)
    )


def natural_pieces(where_ref, own_ref, other_ref, begin, size):
    zero = where_ref[0] == 0
    pieces = []
    for g in range(own_ref.shape[0]):
        slot = where_ref[1 + g]
        mine = own_ref[slot, begin : begin + size, :].astype(f32)
        theirs = other_ref[slot, begin : begin + size, :].astype(f32)
        pieces.append(jnp.where(zero, mine, theirs))
        pieces.append(jnp.where(zero, theirs, mine))
    return jnp.concatenate(pieces, axis=0).astype(bf16)


def unpack_first_kernel(q_cols, kv_cols, where_ref, own_ref, other_ref, inward_ref):
    width = inward_ref.shape[1]
    query = natural_pieces(where_ref, own_ref, other_ref, 0, q_cols)
    inward_ref[KV_PACKED:, :] = query[:, :width]
    for offset in range(2):
        part = natural_pieces(where_ref, own_ref, other_ref, q_cols + offset * kv_cols, kv_cols)
        for j in range(KV_HEADS):
            begin = j * PACK + offset * HEAD_DIM
            inward_ref[begin : begin + HEAD_DIM, :] = part[
                j * HEAD_DIM : (j + 1) * HEAD_DIM, :width
            ]


def pack_rows(where_ref, own_ref, other_ref, source, begin, size):
    zero = where_ref[0] == 0
    lanes = source.shape[1]
    for g in range(own_ref.shape[0]):
        slot = where_ref[1 + g]
        even = source[2 * g * size : (2 * g + 1) * size]
        odd = source[(2 * g + 1) * size : (2 * g + 2) * size]
        own_ref[slot, begin : begin + size, :lanes] = jnp.where(zero, even, odd).astype(bf16)
        other_ref[slot, begin : begin + size, :lanes] = jnp.where(zero, odd, even).astype(bf16)


def pack_first_kernel(q_cols, kv_cols, parts, where_ref, normed_ref, *refs):
    dall_refs, (gains_ref, own_ref, other_ref, grad_ref) = refs[:parts], refs[parts:]
    width = grad_ref.shape[1]
    seq = 0
    for dall_ref in dall_refs:
        for s in range(dall_ref.shape[0]):
            term = dot_nn(dall_ref[s].T, normed_ref[seq])
            grad_ref[...] = term if seq == 0 else grad_ref[...] + term
            seq += 1
    query = grad_ref[KV_PACKED : KV_PACKED + QUERY_WIDTH, :]
    pack_rows(where_ref, own_ref, other_ref, query, 0, q_cols)
    for offset in range(2):
        part = jnp.concatenate(
            [
                grad_ref[j * PACK + offset * HEAD_DIM : j * PACK + (offset + 1) * HEAD_DIM, :]
                for j in range(KV_HEADS)
            ],
            axis=0,
        )
        pack_rows(where_ref, own_ref, other_ref, part, q_cols + offset * kv_cols, kv_cols)
    begin = q_cols + 2 * kv_cols
    for g in range(own_ref.shape[0]):
        own_ref[g, begin : begin + 2, :width] = gains_ref[...].astype(bf16)
        other_ref[g, begin : begin + 2, :width] = gains_ref[...].astype(bf16)


def pack_second_kernel(
    place_ref, out_g_ref, gate_g_ref, up_g_ref, down_g_ref, a_ref, b_ref, c_ref, d_ref, pack_ref, sems
):
    ctx = pack_ref.shape[1]
    f_cols, o_cols, half = FF // ctx, MODEL_WIDTH // ctx, MODEL_WIDTH // 2
    base = f_cols + o_cols
    for plane in range(2):
        lanes = slice(plane * half, (plane + 1) * half)
        for c in range(ctx):
            here = slice(c * f_cols, (c + 1) * f_cols)
            pack_ref[plane, c, :f_cols, :MODEL_WIDTH] = jnp.concatenate(
                [gate_g_ref[here, lanes], up_g_ref[here, lanes]], axis=1
            )
        begin = plane * (FF // 2)
        first = down_g_ref[:, begin : begin + LANES].astype(f32)
        rest = down_g_ref[:, begin + LANES : begin + FF // 2]
        second = jnp.concatenate([rest, out_g_ref[:, lanes]], axis=1).astype(f32)
        for c in range(ctx):
            here = slice(c * o_cols, (c + 1) * o_cols)
            pack_ref[plane, c, f_cols:base, :] = first[here].astype(bf16)
            pack_ref[plane, c, base : base + o_cols, : REST + half] = second[here].astype(bf16)
    copies = []
    for part, part_ref in enumerate((a_ref, b_ref, c_ref, d_ref)):
        core = jnp.abs(place_ref[0] - part // 2)
        plane = jnp.abs(place_ref[1] - part % 2)
        for k in range(part_ref.shape[0]):
            index = 2 * place_ref[2 + k] + core
            copies.append(
                pltpu.make_async_copy(
                    pack_ref.at[plane, index], part_ref.at[k], sems.at[part, k]
                )
            )
    for copy in copies:
        copy.start()
    for copy in copies:
        copy.wait()


def one(shape):
    rest = tuple(shape[1:])
    return pl.BlockSpec((1,) + rest, lambda s, *_: (s,) + (0,) * len(rest))


def whole(shape):
    return pl.BlockSpec(tuple(shape), lambda s, *_: (0,) * len(shape))


def anywhere(shape):
    return pl.BlockSpec(memory_space=pl.ANY)


def since(first):
    def make(shape):
        rest = tuple(shape[1:])
        return pl.BlockSpec((1,) + rest, lambda s, *_: (first + s,) + (0,) * len(rest))

    return make


def call(kernel, seqs, inputs, outputs, scalars=(), scratch=(), us=1.0, after=()):
    begin = len(scalars) + len(inputs)

    def body_of(*refs):
        kernel(*refs[:begin], *refs[begin + len(after) :])

    in_specs = [make(array.shape) for make, array in inputs]
    in_specs += [anywhere(array.shape) for array in after]
    out_specs = [make(shape) for make, shape, _ in outputs]
    moved = sum(array.size * array.dtype.itemsize for _, array in inputs)
    for _, shape, kind in outputs:
        count = 1
        for size in shape:
            count *= size
        moved += count * jnp.dtype(kind).itemsize
    return pl.pallas_call(
        body_of,
        grid_spec=pltpu.PrefetchScalarGridSpec(
            num_scalar_prefetch=len(scalars),
            grid=(seqs,),
            in_specs=in_specs,
            out_specs=out_specs,
            scratch_shapes=list(scratch),
        ),
        out_shape=[jax.ShapeDtypeStruct(shape, kind) for _, shape, kind in outputs],
        compiler_params=pltpu.CompilerParams(vmem_limit_bytes=VMEM_BYTES),
        cost_estimate=pl.CostEstimate(
            flops=int(us * FLOPS_PER_US), bytes_accessed=int(moved), transcendentals=0
        ),
    )(*scalars, *[array for _, array in inputs], *after)


def join_kernel(*refs):
    del refs


def join(arrays, *after):
    return pl.pallas_call(
        join_kernel,
        in_specs=[pl.BlockSpec(memory_space=pl.ANY)] * (len(arrays) + len(after)),
        out_specs=[pl.BlockSpec(memory_space=pl.ANY)] * len(arrays),
        out_shape=[jax.ShapeDtypeStruct(array.shape, array.dtype) for array in arrays],
        input_output_aliases={i: i for i in range(len(arrays))},
    )(*arrays, *after)


def adam_update(weight, first, second, grad, rate, decay):
    first_next = BETA_ONE * first + (1.0 - BETA_ONE) * grad
    second_next = BETA_TWO * second + (1.0 - BETA_TWO) * grad * grad
    first_fix = first_next / (1.0 - BETA_ONE**STEP)
    second_fix = second_next / (1.0 - BETA_TWO**STEP)
    update = first_fix / (jnp.sqrt(second_fix) + ADAM_EPS) + decay * weight
    return (weight - rate * update, first_next, second_next)


def ring_of(chips):
    if chips == 8:
        return [0, 2, 4, 6, 7, 5, 3, 1]
    return list(range(chips))


def ring_pairs(chips, step):
    ring = ring_of(chips)
    return [
        (2 * ring[p] + core, 2 * ring[(p + step) % chips] + core)
        for p in range(chips)
        for core in range(2)
    ]


def ring_gather(mine, flip, pins=None, trace=None):
    chips = lax.axis_size("ctx") // 2
    steps = (chips // 2, (chips - 1) // 2)
    if flip:
        steps = steps[::-1]
    result = [mine] * chips
    ahead = behind = mine
    for t in range(1, max(steps) + 1):
        if t <= steps[0]:
            ahead = lax.ppermute(ahead, "ctx", ring_pairs(chips, 1))
            result[-t % chips] = ahead
        if t <= steps[1]:
            behind = lax.ppermute(behind, "ctx", ring_pairs(chips, -1))
            result[t] = behind
        if pins and t in pins and t <= min(steps):
            ahead, behind = join([ahead, behind], *pins[t])
            result[-t % chips], result[t] = ahead, behind
        if trace is not None:
            trace.append([ahead, behind])
    return result


def plus(*terms):
    total = terms[0].astype(f32)
    for term in terms[1:]:
        total = total + term.astype(f32)
    return total


def ring_scatter(terms, flip):
    chips = lax.axis_size("ctx") // 2
    steps = (chips // 2, (chips - 1) // 2)
    if flip:
        steps = steps[::-1]
    moving = [terms[steps[0]]().astype(bf16), terms[-steps[1] % chips]().astype(bf16)]
    trace = []
    for t in range(max(steps)):
        for way in range(2):
            left = steps[way] - 1 - t
            if left < 0:
                continue
            sign = 1 - 2 * way
            got = lax.ppermute(moving[way], "ctx", ring_pairs(chips, sign))
            if left:
                got = plus(got, terms[sign * left % chips]()).astype(bf16)
            moving[way] = got
        trace.append(list(moving))
    return plus(terms[0](), moving[0], moving[1]), trace


def rows_gather(part):
    if lax.axis_size("fsdp") != 2:
        return lax.all_gather(part, "fsdp", axis=1, tiled=True)
    first = lax.axis_index("fsdp") == 0
    got = lax.ppermute(part, "fsdp", [(0, 1), (1, 0)])
    return jnp.concatenate([jnp.where(first, part, got), jnp.where(first, got, part)], axis=1)


def rows_scatter(grads):
    fsdp = lax.axis_size("fsdp")
    if fsdp != 2:
        return lax.psum_scatter(
            grads.astype(bf16), "fsdp", scatter_dimension=1, tiled=True
        ).astype(f32)
    first = lax.axis_index("fsdp") == 0
    half = grads.shape[1] // 2
    low, high = grads[:, :half], grads[:, half:]
    got = lax.ppermute(jnp.where(first, high, low).astype(bf16), "fsdp", [(0, 1), (1, 0)])
    return jnp.where(first, low, high) + got.astype(f32)


def widen(array):
    return jnp.pad(array, ((0, 0), (0, LANES - array.shape[1])))


def weight_grad(left, right):
    return lax.dot_general(left, right, (((0, 1), (0, 1)), ((), ())), preferred_element_type=f32)


def body(
    tokens,
    cotangent,
    pair_order,
    query_weight,
    key_master_weight,
    value_master_weight,
    output_weight,
    gate_weight,
    up_weight,
    down_weight,
    norm_gains,
    query_first,
    key_first_moment,
    value_first_moment,
    output_first,
    gate_first,
    up_first,
    down_first,
    gains_first,
    query_second,
    key_second_moment,
    value_second_moment,
    output_second,
    gate_second,
    up_second,
    down_second,
    gains_second,
):
    masters = (
        query_weight,
        key_master_weight,
        value_master_weight,
        output_weight,
        gate_weight,
        up_weight,
        down_weight,
    )
    ctx = lax.axis_size("ctx")
    index = lax.axis_index("ctx")
    chunks = ctx // 2
    core = index % 2
    seqs = tokens.shape[0] // 2
    part_rows = tokens.shape[1]
    rows = 2 * part_rows
    blk = part_rows // 2
    per = rows // blk
    length = part_rows * ctx
    mine, other = core * seqs, (1 - core) * seqs
    partners = [(i, i ^ 1) for i in range(ctx)]

    def take(array):
        own = lax.dynamic_slice_in_dim(array, mine, seqs, 0)
        got = lax.ppermute(lax.dynamic_slice_in_dim(array, other, seqs, 0), "ctx", partners)
        return jnp.concatenate([own, got], axis=1)

    def give(array):
        got = lax.ppermute(array[:, part_rows:], "ctx", partners)
        result = jnp.zeros((2 * seqs, part_rows) + array.shape[2:], array.dtype)
        result = lax.dynamic_update_slice_in_dim(result, array[:, :part_rows], mine, 0)
        return lax.dynamic_update_slice_in_dim(result, got, other, 0)

    ring = ring_of(chunks)
    position_of = [ring.index(g) for g in range(chunks)]
    position = jnp.array(position_of, jnp.int32)[index // 2]
    slots = (jnp.array(position_of, jnp.int32) - position) % chunks
    where = jnp.concatenate([core[None].astype(jnp.int32), slots])
    reached = jnp.array(ring, jnp.int32)[(position + jnp.arange(chunks)) % chunks]
    two_planes = lax.axis_size("fsdp") == 2
    plane = lax.axis_index("fsdp") if two_planes else jnp.zeros((), jnp.int32)
    place = jnp.concatenate([core[None].astype(jnp.int32), plane[None].astype(jnp.int32), reached])
    planes = [(0, 1), (1, 0)]

    turned_low = [matrix.astype(bf16).T for matrix in masters]
    q_cols, kv_cols = QUERY_WIDTH // ctx, KEY_WIDTH // ctx
    o_cols, f_cols = MODEL_WIDTH // ctx, FF // ctx

    def both_packs(pack, flip):
        stack = jnp.stack(ring_gather(pack, flip), axis=0)
        return stack, lax.ppermute(stack, "ctx", partners)

    first_part = rows_gather(jnp.concatenate(turned_low[:3] + [norm_gains.astype(bf16).T], axis=0))
    first_used = first_part.shape[0]
    first_part = jnp.pad(first_part, ((0, -first_used % 16), (0, 0)))
    gains = first_part[q_cols + 2 * kv_cols : first_used].astype(f32)
    gain_one, gain_two = gains[0:1], gains[1:2]
    first_own, first_other = both_packs(widen(first_part), False)
    (inward,) = call(
        functools.partial(unpack_first_kernel, q_cols, kv_cols),
        1,
        [(whole, first_own), (whole, first_other)],
        [(whole, (KV_PACKED + QUERY_WIDTH, MODEL_WIDTH), bf16)],
        scalars=(where,),
        us=3.3,
    )
    half = MODEL_WIDTH // 2

    def second_part(gate, up, output, down):
        return jnp.concatenate(
            [
                widen(jnp.concatenate([gate, up], axis=1)),
                down[:, :LANES],
                widen(jnp.concatenate([down[:, LANES:], output], axis=1)),
            ],
            axis=0,
        )

    def later(part):
        return lax.optimization_barrier((part, first_other))[0]

    x = take(tokens)
    cot = take(cotangent)
    order = lax.dynamic_slice_in_dim(pair_order, mine, seqs, 0)
    ends = jnp.stack([order, 2 * ctx - 1 - order], axis=2).reshape(seqs, chunks, 2, 2)
    ends = jnp.where(core == 0, ends, ends[:, :, ::-1])
    ends = ends.reshape(seqs, chunks, per)
    blocks = jnp.take(ends, reached, axis=1).reshape(seqs, chunks * per)
    own = blocks[:, :per]
    places = (own[:, :, None] * blk + jnp.arange(blk, dtype=jnp.int32)).reshape(seqs, rows)
    half_dim = HEAD_DIM // 2
    inverse = ROPE_BASE ** (-jnp.arange(half_dim, dtype=f32) * 2.0 / HEAD_DIM)
    angle = places.astype(f32)[..., None] * inverse
    cosine = jnp.tile(jnp.cos(angle), (1, 1, PACK // half_dim))
    sine = jnp.tile(jnp.sin(angle), (1, 1, PACK // half_dim))

    wide = (seqs, rows, MODEL_WIDTH)
    heads = (seqs, per, KV_HEADS, GROUP * blk, PACK)
    normed_one, query, kv = call(
        project_kernel,
        seqs,
        [(one, x), (whole, gain_one), (whole, inward), (one, cosine), (one, sine)],
        [(one, wide, bf16), (one, heads, bf16), (one, (seqs, rows, KV_PACKED), bf16)],
        us=6.2,
    )
    load = length / 2048
    tile_rows = (KV_HEADS, GROUP * blk, PACK)
    kv_trace = []
    kv_all = ring_gather(kv, False, trace=kv_trace)
    outer = (turned_low[4], turned_low[5], turned_low[3], turned_low[6])
    if two_planes:
        same = jnp.stack(ring_gather(later(second_part(*outer)), True, {1: [inward], 2: kv_trace[0], 3: kv_trace[1]}), axis=0)
        cross = lax.ppermute(same, "fsdp", planes)
    else:
        outer = [rows_gather(part) for part in outer]
        same, cross = [
            jnp.stack(
                ring_gather(
                    second_part(*[jnp.split(part, 2, axis=1)[side] for part in outer]), True
                ),
                axis=0,
            )
            for side in range(2)
        ]
    second_parts = [same, cross] + [lax.ppermute(part, "ctx", partners) for part in (same, cross)]

    attn, logs = call(
        functools.partial(attend_kernel, chunks),
        seqs,
        [(one, query)] + [(one, chunk) for chunk in kv_all],
        [(one, wide, bf16), (one, heads, f32)],
        scalars=(blocks,),
        scratch=[
            pltpu.VMEM((length, KV_PACKED), bf16),
            pltpu.VMEM((KV_HEADS, length // TILE, GROUP * blk, TILE), f32),
            pltpu.VMEM(tile_rows, f32),
            pltpu.VMEM(tile_rows, f32),
        ],
        us=11.0 * seqs * load,
    )
    ff_wide = (seqs, rows, FF)
    (
        block_local,
        normed_two,
        hidden,
        dgate,
        dup,
        dattn,
        dout,
        dresid,
        gain_two_grad,
    ) = call(
        middle_kernel,
        seqs,
        [
            (one, x),
            (one, attn),
            (one, cot),
            (whole, gain_two),
        ]
        + [(anywhere, part) for part in second_parts],
        [
            (one, wide, f32),
            (one, wide, bf16),
            (one, ff_wide, bf16),
            (one, ff_wide, bf16),
            (one, ff_wide, bf16),
            (one, wide, bf16),
            (one, wide, bf16),
            (one, wide, f32),
            (one, (seqs, 1, MODEL_WIDTH), f32),
        ],
        scratch=[
            pltpu.VMEM((MODEL_WIDTH, QUERY_WIDTH), bf16),
            pltpu.VMEM((FF, MODEL_WIDTH), bf16),
            pltpu.VMEM((FF, MODEL_WIDTH), bf16),
            pltpu.VMEM((MODEL_WIDTH, FF), bf16),
            pltpu.VMEM((2, ctx) + same.shape[1:], bf16),
            pltpu.SemaphoreType.DMA((4, chunks)),
        ],
        scalars=(place,),
        us=26.0,
    )
    block_output = give(block_local)
    def reduced_packs(own_packs, other_packs, flip):
        got = lax.ppermute(other_packs, "ctx", partners)
        terms = [lambda k=k: plus(own_packs[k], got[k]) for k in range(chunks)]
        return ring_scatter(terms, flip)

    def outer_sums(earlier):
        behind = traces[-1]
        dattn_, dgate_ = join([dattn, dgate], earlier)
        (dup_,) = join([dup], *behind[0])
        (hidden_,) = join([hidden], *behind[1])
        packs = call(
            pack_second_kernel,
            1,
            [
                (whole, weight_grad(dattn_, attn).astype(bf16)),
                (whole, weight_grad(dgate_, normed_two).astype(bf16)),
                (whole, weight_grad(dup_, normed_two).astype(bf16)),
                (whole, weight_grad(cot, hidden_).astype(bf16)),
            ],
            [(anywhere, same.shape, bf16)] * 4,
            scalars=(place,),
            scratch=[
                pltpu.VMEM((2, ctx) + same.shape[1:], bf16),
                pltpu.SemaphoreType.DMA((4, chunks)),
            ],
            us=7.7,
            after=behind[2],
        )
        got = [lax.ppermute(part, "ctx", partners) for part in packs[2:]]
        if two_planes:
            sent = lax.ppermute(plus(packs[1], got[1]).astype(bf16), "fsdp", planes)
            terms = [lambda k=k: plus(packs[0][k], got[0][k], sent[k]) for k in range(chunks)]
            sums, trace = ring_scatter(terms, True)
            sums, before_last, before_final = [sums], got, [sent]
        else:
            sums = [
                ring_scatter(
                    [lambda k=k, i=i: plus(packs[i][k], got[i][k]) for k in range(chunks)], True
                )[0]
                for i in range(2)
            ]
            before_last, before_final, trace = got, [], [[], []]
        base = f_cols + o_cols
        result = []
        for pick in (
            lambda part: part[base:, REST : REST + half],
            lambda part: part[:f_cols, :half],
            lambda part: part[:f_cols, half:MODEL_WIDTH],
            lambda part: jnp.concatenate([part[f_cols:base], part[base:, :REST]], axis=1),
        ):
            if two_planes:
                result.append(pick(sums[0]))
            else:
                result.append(rows_scatter(jnp.concatenate([pick(part) for part in sums], axis=1)))
        return result, before_last, before_final, trace[1]

    dinputs, dalls, gain_one_grads, traces = [], [], [], []
    last = seqs - 1
    for first, count in ((0, last), (last, 1)):
        these = since(first)
        waits = []
        if first == last:
            outer_reduced, before_last, before_final, before_pack = outer_sums(dquery)
            waits = before_last
        dquery, *dkv = call(
            functools.partial(attend_back_kernel, chunks, first),
            count,
            [(these, query)]
            + [(these, chunk) for chunk in kv_all]
            + [(these, array) for array in (attn, dout, logs, cosine, sine)],
            [(one, (count,) + wide[1:], bf16)] + [(one, (count, rows, KV_PACKED), bf16)] * chunks,
            scalars=(blocks,),
            scratch=[
                pltpu.VMEM((length, KV_PACKED), bf16),
                pltpu.VMEM((KV_HEADS, 2 * GROUP * blk, PACK), bf16),
                pltpu.VMEM((KV_HEADS, PACK, 2 * GROUP * blk), bf16),
                pltpu.VMEM(tile_rows, f32),
                pltpu.VMEM(tile_rows, f32),
                pltpu.VMEM((KV_PACKED, length), f32),
                pltpu.VMEM((length, KV_PACKED), bf16),
            ],
            us=17.0 * count * load,
            after=waits,
        )
        dkv_own, trace = ring_scatter(
            [lambda k=k, dkv=dkv: dkv[k] for k in range(chunks)], first > 0
        )
        traces.append(trace)
        dinput, dall, gain_one_grad = call(
            final_kernel,
            count,
            [
                (these, x),
                (whole, gain_one),
                (one, dquery),
                (one, dkv_own),
                (these, dresid),
                (these, cosine),
                (these, sine),
                (whole, inward),
            ],
            [
                (one, (count,) + wide[1:], f32),
                (one, (count, rows, INNER), bf16),
                (one, (count, 1, MODEL_WIDTH), f32),
            ],
            us=2.0 * count,
            after=before_final if first == last else (),
        )
        dinputs.append(dinput)
        dalls.append(dall)
        gain_one_grads.append(jnp.sum(gain_one_grad, axis=0))
    input_gradient = give(jnp.concatenate(dinputs, axis=0))
    gains_grad = jnp.concatenate([sum(gain_one_grads), jnp.sum(gain_two_grad, axis=0)], axis=0)
    packs = (chunks, first_part.shape[0], LANES)
    first_packs = call(
        functools.partial(pack_first_kernel, q_cols, kv_cols, len(dalls)),
        1,
        [(whole, normed_one)] + [(whole, dall) for dall in dalls] + [(whole, gains_grad)],
        [(whole, packs, bf16), (whole, packs, bf16)],
        scalars=(where,),
        scratch=[pltpu.VMEM((INNER, MODEL_WIDTH), f32)],
        us=3.5,
        after=before_pack,
    )
    first_sum = rows_scatter(reduced_packs(*first_packs, False)[0][:, :MODEL_WIDTH])
    reduced = (
        first_sum[:q_cols],
        first_sum[q_cols : q_cols + kv_cols],
        first_sum[q_cols + kv_cols : q_cols + 2 * kv_cols],
        *outer_reduced,
    )
    gains_total = first_sum[q_cols + 2 * kv_cols : first_used].T
    rates = (
        (MODEL_WIDTH // 4) ** (-0.5),
        MODEL_WIDTH ** (-0.5),
        MODEL_WIDTH ** (-0.5),
        (MODEL_WIDTH // 32) ** (-0.5),
        MODEL_WIDTH ** (-0.5),
        MODEL_WIDTH ** (-0.5),
        (FF // 2) ** (-0.5),
    )
    firsts = (
        query_first,
        key_first_moment,
        value_first_moment,
        output_first,
        gate_first,
        up_first,
        down_first,
    )
    seconds = (
        query_second,
        key_second_moment,
        value_second_moment,
        output_second,
        gate_second,
        up_second,
        down_second,
    )
    results = [
        adam_update(
            masters[member], firsts[member], seconds[member], reduced[member].T, rates[member], DECAY
        )
        for member in range(7)
    ]
    results.append(adam_update(norm_gains, gains_first, gains_second, gains_total, GAIN_RATE, 0.0))
    new_weights = [result[0] for result in results]
    new_firsts = [result[1] for result in results]
    new_seconds = [result[2] for result in results]
    return tuple([block_output, input_gradient] + new_weights + new_firsts + new_seconds)


def solution(mesh):
    sequences = P("fsdp", "ctx", None)
    matrix = P("fsdp", "ctx")
    gains = P("fsdp", None)
    state = (matrix,) * 7 + (gains,)
    return jax.shard_map(
        body,
        mesh=mesh,
        in_specs=(sequences, sequences, P("fsdp", None)) + state * 3,
        out_specs=(sequences, sequences) + state * 3,
        check_vma=False,
    )
```

profile of v0, /device:TPU:0, one launch (start us, length us, event | category | flops | bytes accessed | tf_op | source)
XLA Modules:
  0.0 421.2 jit_solution(7975780154262941702)
XLA Ops:
  3.0 3.0 collective-permute-start.1
  14.9 2.1 collective-permute-done.2
  19.7 1.8 collective-permute-done.3
  24.2 3.3 collective-permute-done.7
  28.9 2.9 collective-permute-done.8
  39.7 3.3 shard_map.485.refs_2_.refs_7_
  43.0 6.3 %shard_map.486 = (bf16[3,256,576]{2,1,0:T(8,128)(2,1)}, bf16[3,4,3,192,128]{4,3,2,1,0:T(8,128)(2,1)}, bf16[3,256,384]{2,1,0:T(8,128)(2,1)}) custom-call(bf16[3,256,576]{2,1,0:T(8,128)(2,1)} %pad_maximum_fusion.refs_0_.refs_1_, f32[1,576]{1,0:T(1,128)} %get-tuple-element.297.refs_1_, bf16[960,576]{1,0:T(8,128)(2,1)} %shard_map.485.refs_2_.refs_7_, ...), custom_call_target="tpu_custom_call" | custom-call | flops 7151699968 | bytes 6023424 | tf_op jit(solution)/shard_map/pallas_call | solution.py:536
  53.9 11.7 %collective-permute-done.10.refs_3_ = bf16[3,256,384]{2,1,0:T(8,128)(2,1)S(1)} collective-permute-done((bf16[3,256,384]{2,1,0:T(8,128)(2,1)}, bf16[3,256,384]{2,1,0:T(8,128)(2,1)S(1)}, u32[]{:S(2)}, u32[]{:S(2)}) %collective-permute-start.10) | collective-permute-done | bytes 589856 | tf_op jit(solution)/shard_map/ppermute | solution.py:603
  68.4 3.5 collective-permute-done.18.refs_0_
  77.0 11.5 %collective-permute-done.20.refs_0_ = bf16[168,640]{1,0:T(8,128)(2,1)S(1)} collective-permute-done((bf16[168,640]{1,0:T(8,128)(2,1)}, bf16[168,640]{1,0:T(8,128)(2,1)S(1)}, u32[]{:S(2)}, u32[]{:S(2)}) %collective-permute-start.20) | collective-permute-done | bytes 215072 | tf_op jit(solution)/shard_map/ppermute | solution.py:600
  93.5 3.1 collective-permute-done.22.refs_0_
  100.8 2.8 collective-permute-done.24
  109.9 11.1 %collective-permute-done.15.refs_7_ = bf16[3,256,384]{2,1,0:T(8,128)(2,1)S(1)} collective-permute-done((bf16[3,256,384]{2,1,0:T(8,128)(2,1)}, bf16[3,256,384]{2,1,0:T(8,128)(2,1)S(1)}, u32[]{:S(2)}, u32[]{:S(2)}) %collective-permute-start.15) | collective-permute-done | bytes 589856 | tf_op jit(solution)/shard_map/ppermute | solution.py:600
  126.0 18.4 %collective-permute-done.25.refs_6_ = bf16[8,168,640]{2,1,0:T(8,128)(2,1)} collective-permute-done((bf16[8,168,640]{2,1,0:T(8,128)(2,1)}, bf16[8,168,640]{2,1,0:T(8,128)(2,1)}, u32[]{:S(2)}, u32[]{:S(2)}) %collective-permute-start.25) | collective-permute-done | bytes 1720352 | tf_op jit(solution)/shard_map/ppermute | solution.py:811
  144.4 33.4 %shard_map.487 = (bf16[3,256,576]{2,1,0:T(8,128)(2,1)}, f32[3,4,3,192,128]{4,3,2,1,0:T(8,128)}) custom-call(s32[3,32]{1,0:T(4,128)} %copy-done.75, bf16[3,4,3,192,128]{4,3,2,1,0:T(8,128)(2,1)} %get-tuple-element.79.refs_1_, bf16[3,256,384]{2,1,0:T(8,128)(2,1)} %get-tuple-element.80.refs_2_, bf16[3,256,384]{2,1,0:T(8,128)(2,1)} %copy-done.31, ...), custom_call_target="tpu_custom_call" | custom-call | flops 38065500160 | bytes 10911744 | tf_op jit(solution)/shard_map/pallas_call | solution.py:536
  179.6 26.0 %shard_map.491 = (f32[3,256,576]{2,1,0:T(8,128)}, bf16[3,256,576]{2,1,0:T(8,128)(2,1)}, bf16[3,256,1536]{2,1,0:T(8,128)(2,1)}, bf16[3,256,1536]{2,1,0:T(8,128)(2...) custom-call(s32[10]{0:T(128)} %pad_add_fusion.1.refs_0_, ...), custom_call_target="tpu_custom_call" | custom-call | flops 29991000064 | bytes 22815744 | tf_op jit(solution)/shard_map/pallas_call | solution.py:536
  205.6 29.8 %shard_map.492 = (bf16[2,256,576]{2,1,0:T(8,128)(2,1)}, bf16[2,256,384]{2,1,0:T(8,128)(2,1)}, bf16[2,256,384]{2,1,0:T(8,128)(2,1)}, bf16[2,256,384]{2,1,0:T(8,12...) custom-call(s32[3,32]{1,0:T(4,128)} %copy-done.75, ...), custom_call_target="tpu_custom_call" | custom-call | flops 39218999296 | bytes 16318464 | tf_op jit(solution)/shard_map/pallas_call | solution.py:536
  237.5 3.6 bitcast_convert_fusion.2
  241.1 1.8 bitcast_convert_fusion.3.refs_1_
  242.9 2.3 copy.211.refs_2_
  245.2 2.0 collective-permute-done.29
  252.4 3.5 bitcast_convert_fusion.1
  255.9 2.4 copy.212.refs_3_
  258.3 1.8 collective-permute-done.30
  264.9 4.5 %bitcast_convert_fusion.refs_4_ = bf16[576,1536]{1,0:T(8,128)(2,1)} fusion(bf16[3,256,1536]{2,1,0:T(8,128)(2,1)} %shard_map.496, bf16[3,128,576]{2,1,0:T(8,128)(2,1)S(1)} %collective-permute-done.17, bf16[3,128,576]{2,1,0:T(8,128)(2,1)S(1)} %copy.240), kind=kOutput, calls=%fused_computation.2 | convolution fusion | flops 1361608704 | bytes 5013504 | tf_op jit(solution)/shard_map/dot_general | solution.py:667
  269.4 1.9 collective-permute-done.31
  273.8 7.8 %shard_map.497 = (bf16[8,168,640]{2,1,0:T(8,128)(2,1)}, bf16[8,168,640]{2,1,0:T(8,128)(2,1)}, bf16[8,168,640]{2,1,0:T(8,128)(2,1)}, bf16[8,168,640]{2,1,0:T(8,128)(2,1)}) custom-call(s32[10]{0:T(128)} %pad_add_fusion.1.refs_0_, bf16[576,576]{1,0:T(8,128)(2,1)} %bitcast_convert_fusion.3.refs_1_, bf16[1536,576]{1,0:T(8,128)(2,1)} %copy.211.refs_2_, ...), custom_call_target="tpu_custom_call" | custom-call | flops 8881949696 | bytes 12853248 | tf_op jit(solution)/shard_map/pallas_call | solution.py:536
  290.3 3.1 collective-permute-done.32
  293.4 2.0 convert_add_fusion.refs_3_
  295.4 3.1 add_convert_fusion
  299.6 16.8 %shard_map.498 = (bf16[1,256,576]{2,1,0:T(8,128)(2,1)}, bf16[1,256,384]{2,1,0:T(8,128)(2,1)}, bf16[1,256,384]{2,1,0:T(8,128)(2,1)}, bf16[1,256,384]{2,1,0:T(8,12...) custom-call(s32[3,32]{1,0:T(4,128)} %copy-done.75, ...), custom_call_target="tpu_custom_call" | custom-call | flops 19609499648 | bytes 14450688 | tf_op jit(solution)/shard_map/pallas_call | solution.py:536
  317.6 4.9 %shard_map.493 = (f32[2,256,576]{2,1,0:T(8,128)}, bf16[2,256,1024]{2,1,0:T(8,128)(2,1)}, f32[2,1,576]{2,1,0:T(1,128)}) custom-call(bf16[3,256,576]{2,1,0:T(8,128)(2,1)} %pad_maximum_fusion.refs_0_.refs_1_, f32[1,576]{1,0:T(1,128)} %get-tuple-element.297.refs_1_, bf16[2,256,576]{2,1,0:T(8,128)(2,1)} %get-tuple-element.92.refs_2_, ...), custom_call_target="tpu_custom_call" | custom-call | flops 4614000128 | bytes 8157952 | tf_op jit(solution)/shard_map/pallas_call | solution.py:536
  327.2 3.7 collective-permute-done.41
  333.2 3.8 collective-permute-done.42
  340.5 4.3 %collective-permute-done.43 = bf16[1,256,384]{2,1,0:T(8,128)(2,1)S(1)} collective-permute-done((bf16[1,256,384]{2,1,0:T(8,128)(2,1)S(1)}, bf16[1,256,384]{2,1,0:T(8,128)(2,1)S(1)}, u32[]{:S(2)}, u32[]{:S(2)}) %collective-permute-start.43) | collective-permute-done | bytes 196640 | tf_op jit(solution)/shard_map/ppermute | solution.py:633
  347.0 2.3 collective-permute-done.49
  354.1 2.9 shard_map.500
  358.6 1.8 collective-permute-start.48
  361.3 3.2 collective-permute-done.48
  366.2 2.3 fusion
  368.5 5.0 %shard_map.499 = (bf16[8,64,640]{2,1,0:T(8,128)(2,1)}, bf16[8,64,640]{2,1,0:T(8,128)(2,1)}) custom-call(s32[9]{0:T(128)} %pad_add_fusion.2.refs_0_, bf16[3,256,576]{2,1,0:T(8,128)(2,1)} %get-tuple-element.123.refs_1_, bf16[2,256,1024]{2,1,0:T(8,128)(2,1)} %get-tuple-element.124.refs_2_, bf16[1,256,1024]{2,1,0:T(8,128)(2,1)} %get-tuple-element.239.refs_3_, ...), custom_call_target="tpu_custom_call" | custom-call | flops 4037250048 | bytes 3772928 | tf_op jit(solution)/shard_map/pallas_call | solution.py:536
  376.5 2.4 copy.217
  381.4 1.8 collective-permute-start.60
  384.5 1.8 collective-permute-start.52
  386.3 3.3 collective-permute-done.60
  393.1 1.8 collective-permute-start.53
  398.6 1.8 collective-permute-start.54
  416.6 1.9 collective-permute-done.59
  (409 shorter events, 139.4 us)
Async XLA Ops:
  3.0 9.0 %collective-permute-start.1 = (bf16[62,288]{1,0:T(8,128)(2,1)S(1)}, bf16[62,288]{1,0:T(8,128)(2,1)S(1)}, u32[]{:S(2)}, u32[]{:S(2)}) collective-permute-start(bf16[62,288]{1,0:T(8,128)(2,1)S(1)} %pad_maximum_fusion.4), channel_id=1, source_target_pairs={{0,1},{1,0},{2,3},{3,2},{4,5},{5,4},{6,7},{7,6},{8,9},{9,8},{10,11... | collective-permute-start | bytes 107144 | tf_op jit(solution)/shard_map/ppermute | solution.py:645
  7.9 30.7 %collective-permute-start = (bf16[3,128,576]{2,1,0:T(8,128)(2,1)S(1)}, bf16[3,128,576]{2,1,0:T(8,128)(2,1)S(1)}, u32[]{:S(2)}, u32[]{:S(2)}) collective-permute-start(bf16[3,128,576]{2,1,0:T(8,128)(2,1)S(1)} %copy.239), channel_id=1, source_target_pairs={{0,2},{2,0},{4,6},{6,4},{8,10},{10,8},{12,14},{14,12},{16,18},{18,... | collective-permute-start | bytes 1327112 | tf_op jit(solution)/shard_map/ppermute | solution.py:723
  21.5 6.8 %collective-permute-start.4 = (bf16[64,640]{1,0:T(8,128)(2,1)S(1)}, bf16[64,640]{1,0:T(8,128)(2,1)S(1)}, u32[]{:S(2)}, u32[]{:S(2)}) collective-permute-start(bf16[64,640]{1,0:T(8,128)(2,1)S(1)} %collective-permute-done.3), channel_id=1, source_target_pairs={{0,4},{2,6},{8,0},{10,2},{16,8},{18,10},{24,16},{26,18},{28,24},{3... | collective-permute-start | bytes 245768 | tf_op jit(solution)/shard_map/ppermute | solution.py:603
  49.3 16.3 %collective-permute-start.10 = (bf16[3,256,384]{2,1,0:T(8,128)(2,1)}, bf16[3,256,384]{2,1,0:T(8,128)(2,1)S(1)}, u32[]{:S(2)}, u32[]{:S(2)}) collective-permute-start(bf16[3,256,384]{2,1,0:T(8,128)(2,1)} %get-tuple-element.80.refs_2_), channel_id=1, source_target_pairs={{0,4},{2,6},{8,0},{10,2},{16,8},{18,10},{24,16},{26,18},{28,24},{3... | collective-permute-start | bytes 1769480 | tf_op jit(solution)/shard_map/ppermute | solution.py:603
  50.9 16.4 %collective-permute-start.13 = (bf16[3,256,384]{2,1,0:T(8,128)(2,1)}, bf16[3,256,384]{2,1,0:T(8,128)(2,1)S(1)}, u32[]{:S(2)}, u32[]{:S(2)}) collective-permute-start(bf16[3,256,384]{2,1,0:T(8,128)(2,1)} %get-tuple-element.80.refs_2_), channel_id=1, source_target_pairs={{0,8},{2,10},{8,16},{10,18},{16,24},{18,26},{24,28},{26,30},{28,20... | collective-permute-start | bytes 1769480 | tf_op jit(solution)/shard_map/ppermute | solution.py:600
  51.9 20.0 %collective-permute-start.18 = (bf16[168,640]{1,0:T(8,128)(2,1)S(1)}, bf16[168,640]{1,0:T(8,128)(2,1)S(1)}, u32[]{:S(2)}, u32[]{:S(2)}) collective-permute-start(bf16[168,640]{1,0:T(8,128)(2,1)S(1)} %pad_maximum_fusion.2), channel_id=1, source_target_pairs={{0,8},{2,10},{8,16},{10,18},{16,24},{18,26},{24,28},{26,30},{28,20... | collective-permute-start | bytes 645128 | tf_op jit(solution)/shard_map/ppermute | solution.py:600
  52.8 19.1 %collective-permute-start.19 = (bf16[168,640]{1,0:T(8,128)(2,1)S(1)}, bf16[168,640]{1,0:T(8,128)(2,1)S(1)}, u32[]{:S(2)}, u32[]{:S(2)}) collective-permute-start(bf16[168,640]{1,0:T(8,128)(2,1)S(1)} %pad_maximum_fusion.2), channel_id=1, source_target_pairs={{0,4},{2,6},{8,0},{10,2},{16,8},{18,10},{24,16},{26,18},{28,24},{3... | collective-permute-start | bytes 645128 | tf_op jit(solution)/shard_map/ppermute | solution.py:603
  65.7 31.1 %collective-permute-start.11 = (bf16[3,256,384]{2,1,0:T(8,128)(2,1)S(1)}, bf16[3,256,384]{2,1,0:T(8,128)(2,1)}, u32[]{:S(2)}, u32[]{:S(2)}) collective-permute-start(bf16[3,256,384]{2,1,0:T(8,128)(2,1)S(1)} %collective-permute-done.10.refs_3_), channel_id=1, source_target_pairs={{0,4},{2,6},{8,0},{10,2},{16,8},{18,10},{24,16},{26,18},{28,24},{3... | collective-permute-start | bytes 1769480 | tf_op jit(solution)/shard_map/ppermute | solution.py:603
  67.3 29.5 %collective-permute-start.14 = (bf16[3,256,384]{2,1,0:T(8,128)(2,1)S(1)}, bf16[3,256,384]{2,1,0:T(8,128)(2,1)}, u32[]{:S(2)}, u32[]{:S(2)}) collective-permute-start(bf16[3,256,384]{2,1,0:T(8,128)(2,1)S(1)} %collective-permute-done.13.refs_9_.refs_2_), channel_id=1, source_target_pairs={{0,8},{2,10},{8,16},{10,18},{16,24},{18,26},{24,28},{26,30},{28,20... | collective-permute-start | bytes 1769480 | tf_op jit(solution)/shard_map/ppermute | solution.py:600
  73.3 15.2 %collective-permute-start.20 = (bf16[168,640]{1,0:T(8,128)(2,1)}, bf16[168,640]{1,0:T(8,128)(2,1)S(1)}, u32[]{:S(2)}, u32[]{:S(2)}) collective-permute-start(bf16[168,640]{1,0:T(8,128)(2,1)} %get-tuple-element.84), channel_id=1, source_target_pairs={{0,8},{2,10},{8,16},{10,18},{16,24},{18,26},{24,28},{26,30},{28,20... | collective-permute-start | bytes 645128 | tf_op jit(solution)/shard_map/ppermute | solution.py:600
  73.7 14.7 %collective-permute-start.21 = (bf16[168,640]{1,0:T(8,128)(2,1)}, bf16[168,640]{1,0:T(8,128)(2,1)S(1)}, u32[]{:S(2)}, u32[]{:S(2)}) collective-permute-start(bf16[168,640]{1,0:T(8,128)(2,1)} %get-tuple-element.83), channel_id=1, source_target_pairs={{0,4},{2,6},{8,0},{10,2},{16,8},{18,10},{24,16},{26,18},{28,24},{3... | collective-permute-start | bytes 645128 | tf_op jit(solution)/shard_map/ppermute | solution.py:603
  89.8 6.8 %collective-permute-start.22 = (bf16[168,640]{1,0:T(8,128)(2,1)}, bf16[168,640]{1,0:T(8,128)(2,1)S(1)}, u32[]{:S(2)}, u32[]{:S(2)}) collective-permute-start(bf16[168,640]{1,0:T(8,128)(2,1)} %get-tuple-element.86), channel_id=1, source_target_pairs={{0,8},{2,10},{8,16},{10,18},{16,24},{18,26},{24,28},{26,30},{28,20... | collective-permute-start | bytes 645128 | tf_op jit(solution)/shard_map/ppermute | solution.py:600
  90.3 6.5 %collective-permute-start.23 = (bf16[168,640]{1,0:T(8,128)(2,1)}, bf16[168,640]{1,0:T(8,128)(2,1)S(1)}, u32[]{:S(2)}, u32[]{:S(2)}) collective-permute-start(bf16[168,640]{1,0:T(8,128)(2,1)} %get-tuple-element.85), channel_id=1, source_target_pairs={{0,4},{2,6},{8,0},{10,2},{16,8},{18,10},{24,16},{26,18},{28,24},{3... | collective-permute-start | bytes 645128 | tf_op jit(solution)/shard_map/ppermute | solution.py:603
  97.5 6.1 %collective-permute-start.24 = (bf16[168,640]{1,0:T(8,128)(2,1)}, bf16[168,640]{1,0:T(8,128)(2,1)S(1)}, u32[]{:S(2)}, u32[]{:S(2)}) collective-permute-start(bf16[168,640]{1,0:T(8,128)(2,1)} %get-tuple-element.87), channel_id=1, source_target_pairs={{0,4},{2,6},{8,0},{10,2},{16,8},{18,10},{24,16},{26,18},{28,24},{3... | collective-permute-start | bytes 645128 | tf_op jit(solution)/shard_map/ppermute | solution.py:603
  107.3 37.0 %collective-permute-start.25 = (bf16[8,168,640]{2,1,0:T(8,128)(2,1)}, bf16[8,168,640]{2,1,0:T(8,128)(2,1)}, u32[]{:S(2)}, u32[]{:S(2)}) collective-permute-start(bf16[8,168,640]{2,1,0:T(8,128)(2,1)} %bitcast_dynamic-update-slice_fusion.refs_5_), channel_id=1, source_target_pairs={{0,1},{1,0},{2,3},{3,2},{4,5},{5,4},{6,7},{7,6},{8,9},{9,8},{10,11... | collective-permute-start | bytes 5160968 | tf_op jit(solution)/shard_map/ppermute | solution.py:811
  107.8 13.2 %collective-permute-start.15 = (bf16[3,256,384]{2,1,0:T(8,128)(2,1)}, bf16[3,256,384]{2,1,0:T(8,128)(2,1)S(1)}, u32[]{:S(2)}, u32[]{:S(2)}) collective-permute-start(bf16[3,256,384]{2,1,0:T(8,128)(2,1)} %collective-permute-done.14.refs_8_.refs_2_), channel_id=1, source_target_pairs={{0,8},{2,10},{8,16},{10,18},{16,24},{18,26},{24,28},{26,30},{28,20... | collective-permute-start | bytes 1769480 | tf_op jit(solution)/shard_map/ppermute | solution.py:600
  108.9 35.4 %collective-permute-start.12 = (bf16[3,256,384]{2,1,0:T(8,128)(2,1)}, bf16[3,256,384]{2,1,0:T(8,128)(2,1)}, u32[]{:S(2)}, u32[]{:S(2)}) collective-permute-start(bf16[3,256,384]{2,1,0:T(8,128)(2,1)} %collective-permute-done.11.refs_4_.refs_3_), channel_id=1, source_target_pairs={{0,4},{2,6},{8,0},{10,2},{16,8},{18,10},{24,16},{26,18},{28,24},{3... | collective-permute-start | bytes 1769480 | tf_op jit(solution)/shard_map/ppermute | solution.py:603
  121.0 23.4 %collective-permute-start.16 = (bf16[3,256,384]{2,1,0:T(8,128)(2,1)S(1)}, bf16[3,256,384]{2,1,0:T(8,128)(2,1)}, u32[]{:S(2)}, u32[]{:S(2)}) collective-permute-start(bf16[3,256,384]{2,1,0:T(8,128)(2,1)S(1)} %collective-permute-done.15.refs_7_), channel_id=1, source_target_pairs={{0,8},{2,10},{8,16},{10,18},{16,24},{18,26},{24,28},{26,30},{28,20... | collective-permute-start | bytes 1769480 | tf_op jit(solution)/shard_map/ppermute | solution.py:600
  125.8 52.0 %collective-permute-start.26 = (bf16[8,168,640]{2,1,0:T(8,128)(2,1)S(1)}, bf16[8,168,640]{2,1,0:T(8,128)(2,1)S(1)}, u32[]{:S(2)}, u32[]{:S(2)}) collective-permute-start(bf16[8,168,640]{2,1,0:T(8,128)(2,1)S(1)} %copy-done.68), channel_id=1, source_target_pairs={{0,2},{2,0},{4,6},{6,4},{8,10},{10,8},{12,14},{14,12},{16,18},{18,... | collective-permute-start | bytes 5160968 | tf_op jit(solution)/shard_map/ppermute | solution.py:823
  144.4 33.5 %collective-permute-start.27 = (bf16[8,168,640]{2,1,0:T(8,128)(2,1)}, bf16[8,168,640]{2,1,0:T(8,128)(2,1)S(1)}, u32[]{:S(2)}, u32[]{:S(2)}) collective-permute-start(bf16[8,168,640]{2,1,0:T(8,128)(2,1)} %collective-permute-done.25.refs_6_), channel_id=1, source_target_pairs={{0,2},{2,0},{4,6},{6,4},{8,10},{10,8},{12,14},{14,12},{16,18},{18,... | collective-permute-start | bytes 5160968 | tf_op jit(solution)/shard_map/ppermute | solution.py:823
  235.4 11.8 %collective-permute-start.29 = (bf16[2,256,384]{2,1,0:T(8,128)(2,1)}, bf16[2,256,384]{2,1,0:T(8,128)(2,1)S(1)}, u32[]{:S(2)}, u32[]{:S(2)}) collective-permute-start(bf16[2,256,384]{2,1,0:T(8,128)(2,1)} %get-tuple-element.94), channel_id=1, source_target_pairs={{0,8},{2,10},{8,16},{10,18},{16,24},{18,26},{24,28},{26,30},{28,20... | collective-permute-start | bytes 1179656 | tf_op jit(solution)/shard_map/ppermute | solution.py:633
  236.1 13.6 %collective-permute-start.33 = (bf16[2,256,384]{2,1,0:T(8,128)(2,1)}, bf16[2,256,384]{2,1,0:T(8,128)(2,1)}, u32[]{:S(2)}, u32[]{:S(2)}) collective-permute-start(bf16[2,256,384]{2,1,0:T(8,128)(2,1)} %get-tuple-element.98), channel_id=1, source_target_pairs={{0,4},{2,6},{8,0},{10,2},{16,8},{18,10},{24,16},{26,18},{28,24},{3... | collective-permute-start | bytes 1179656 | tf_op jit(solution)/shard_map/ppermute | solution.py:633
  249.1 11.0 %collective-permute-start.30 = (bf16[2,256,384]{2,1,0:T(8,128)(2,1)S(1)}, bf16[2,256,384]{2,1,0:T(8,128)(2,1)}, u32[]{:S(2)}, u32[]{:S(2)}) collective-permute-start(bf16[2,256,384]{2,1,0:T(8,128)(2,1)S(1)} %add_convert_fusion.5.refs_1_), channel_id=1, source_target_pairs={{0,8},{2,10},{8,16},{10,18},{16,24},{18,26},{24,28},{26,30},{28,20... | collective-permute-start | bytes 1179656 | tf_op jit(solution)/shard_map/ppermute | solution.py:633
  251.0 11.0 %collective-permute-start.34 = (bf16[2,256,384]{2,1,0:T(8,128)(2,1)S(1)}, bf16[2,256,384]{2,1,0:T(8,128)(2,1)}, u32[]{:S(2)}, u32[]{:S(2)}) collective-permute-start(bf16[2,256,384]{2,1,0:T(8,128)(2,1)S(1)} %add_convert_fusion.2.refs_2_), channel_id=1, source_target_pairs={{0,4},{2,6},{8,0},{10,2},{16,8},{18,10},{24,16},{26,18},{28,24},{3... | collective-permute-start | bytes 1179656 | tf_op jit(solution)/shard_map/ppermute | solution.py:633
  261.3 10.0 %collective-permute-start.31 = (bf16[2,256,384]{2,1,0:T(8,128)(2,1)S(1)}, bf16[2,256,384]{2,1,0:T(8,128)(2,1)S(1)}, u32[]{:S(2)}, u32[]{:S(2)}) collective-permute-start(bf16[2,256,384]{2,1,0:T(8,128)(2,1)S(1)} %add_convert_fusion.4.refs_1_), channel_id=1, source_target_pairs={{0,8},{2,10},{8,16},{10,18},{16,24},{18,26},{24,28},{26,30},{28,20... | collective-permute-start | bytes 1179656 | tf_op jit(solution)/shard_map/ppermute | solution.py:633
  263.2 9.9 %collective-permute-start.35 = (bf16[2,256,384]{2,1,0:T(8,128)(2,1)S(1)}, bf16[2,256,384]{2,1,0:T(8,128)(2,1)S(1)}, u32[]{:S(2)}, u32[]{:S(2)}) collective-permute-start(bf16[2,256,384]{2,1,0:T(8,128)(2,1)S(1)} %add_convert_fusion.1.refs_2_), channel_id=1, source_target_pairs={{0,4},{2,6},{8,0},{10,2},{16,8},{18,10},{24,16},{26,18},{28,24},{3... | collective-permute-start | bytes 1179656 | tf_op jit(solution)/shard_map/ppermute | solution.py:633
  281.6 13.8 %collective-permute-start.37 = (bf16[8,168,640]{2,1,0:T(8,128)(2,1)}, bf16[8,168,640]{2,1,0:T(8,128)(2,1)}, u32[]{:S(2)}, u32[]{:S(2)}) collective-permute-start(bf16[8,168,640]{2,1,0:T(8,128)(2,1)} %get-tuple-element.111), channel_id=1, source_target_pairs={{0,2},{2,0},{4,6},{6,4},{8,10},{10,8},{12,14},{14,12},{16,18},{18,... | collective-permute-start | bytes 5160968 | tf_op jit(solution)/shard_map/ppermute | solution.py:911
  281.7 17.9 %collective-permute-start.36 = (bf16[8,168,640]{2,1,0:T(8,128)(2,1)}, bf16[8,168,640]{2,1,0:T(8,128)(2,1)}, u32[]{:S(2)}, u32[]{:S(2)}) collective-permute-start(bf16[8,168,640]{2,1,0:T(8,128)(2,1)} %get-tuple-element.110), channel_id=1, source_target_pairs={{0,2},{2,0},{4,6},{6,4},{8,10},{10,8},{12,14},{14,12},{16,18},{18,... | collective-permute-start | bytes 5160968 | tf_op jit(solution)/shard_map/ppermute | solution.py:911
  282.2 11.2 %collective-permute-start.32 = (bf16[2,256,384]{2,1,0:T(8,128)(2,1)S(1)}, bf16[2,256,384]{2,1,0:T(8,128)(2,1)}, u32[]{:S(2)}, u32[]{:S(2)}) collective-permute-start(bf16[2,256,384]{2,1,0:T(8,128)(2,1)S(1)} %copy-done.36), channel_id=1, source_target_pairs={{0,8},{2,10},{8,16},{10,18},{16,24},{18,26},{24,28},{26,30},{28,20... | collective-permute-start | bytes 1179656 | tf_op jit(solution)/shard_map/ppermute | solution.py:633
  290.3 83.3 %collective-permute-start.28 = (f32[3,128,576]{1,2,0:T(8,128)}, f32[3,128,576]{1,2,0:T(8,128)}, u32[]{:S(2)}, u32[]{:S(2)}) collective-permute-start(f32[3,128,576]{1,2,0:T(8,128)} %copy.201), channel_id=1, source_target_pairs={{0,2},{2,0},{4,6},{6,4},{8,10},{10,8},{12,14},{14,12},{16,18},{18,... | collective-permute-start | bytes 2654216 | tf_op jit(solution)/shard_map/ppermute | solution.py:727
  298.5 39.4 %collective-permute-start.45 = (bf16[8,168,640]{2,1,0:T(8,128)(2,1)}, bf16[8,168,640]{2,1,0:T(8,128)(2,1)S(1)}, u32[]{:S(2)}, u32[]{:S(2)}) collective-permute-start(bf16[8,168,640]{2,1,0:T(8,128)(2,1)} %add_convert_fusion), channel_id=1, source_target_pairs={{0,1},{1,0},{2,3},{3,2},{4,5},{5,4},{6,7},{7,6},{8,9},{9,8},{10,11... | collective-permute-start | bytes 5160968 | tf_op jit(solution)/shard_map/ppermute | solution.py:913
  316.4 9.5 %collective-permute-start.38 = (bf16[1,256,384]{2,1,0:T(8,128)(2,1)}, bf16[1,256,384]{2,1,0:T(8,128)(2,1)S(1)}, u32[]{:S(2)}, u32[]{:S(2)}) collective-permute-start(bf16[1,256,384]{2,1,0:T(8,128)(2,1)} %get-tuple-element.114), channel_id=1, source_target_pairs={{0,8},{2,10},{8,16},{10,18},{16,24},{18,26},{24,28},{26,30},{28,20... | collective-permute-start | bytes 589832 | tf_op jit(solution)/shard_map/ppermute | solution.py:633
  324.8 6.2 %collective-permute-start.41 = (bf16[1,256,384]{2,1,0:T(8,128)(2,1)}, bf16[1,256,384]{2,1,0:T(8,128)(2,1)S(1)}, u32[]{:S(2)}, u32[]{:S(2)}) collective-permute-start(bf16[1,256,384]{2,1,0:T(8,128)(2,1)} %get-tuple-element.117), channel_id=1, source_target_pairs={{0,4},{2,6},{8,0},{10,2},{16,8},{18,10},{24,16},{26,18},{28,24},{3... | collective-permute-start | bytes 589832 | tf_op jit(solution)/shard_map/ppermute | solution.py:633
  326.0 5.9 %collective-permute-start.39 = (bf16[1,256,384]{2,1,0:T(8,128)(2,1)S(1)}, bf16[1,256,384]{2,1,0:T(8,128)(2,1)S(1)}, u32[]{:S(2)}, u32[]{:S(2)}) collective-permute-start(bf16[1,256,384]{2,1,0:T(8,128)(2,1)S(1)} %add_convert_fusion.12), channel_id=1, source_target_pairs={{0,8},{2,10},{8,16},{10,18},{16,24},{18,26},{24,28},{26,30},{28,20... | collective-permute-start | bytes 589832 | tf_op jit(solution)/shard_map/ppermute | solution.py:633
  331.0 6.0 %collective-permute-start.42 = (bf16[1,256,384]{2,1,0:T(8,128)(2,1)S(1)}, bf16[1,256,384]{2,1,0:T(8,128)(2,1)S(1)}, u32[]{:S(2)}, u32[]{:S(2)}) collective-permute-start(bf16[1,256,384]{2,1,0:T(8,128)(2,1)S(1)} %add_convert_fusion.10), channel_id=1, source_target_pairs={{0,4},{2,6},{8,0},{10,2},{16,8},{18,10},{24,16},{26,18},{28,24},{3... | collective-permute-start | bytes 589832 | tf_op jit(solution)/shard_map/ppermute | solution.py:633
  332.0 19.6 %collective-permute-start.40 = (bf16[1,256,384]{2,1,0:T(8,128)(2,1)S(1)}, bf16[1,256,384]{2,1,0:T(8,128)(2,1)S(1)}, u32[]{:S(2)}, u32[]{:S(2)}) collective-permute-start(bf16[1,256,384]{2,1,0:T(8,128)(2,1)S(1)} %add_convert_fusion.11), channel_id=1, source_target_pairs={{0,8},{2,10},{8,16},{10,18},{16,24},{18,26},{24,28},{26,30},{28,20... | collective-permute-start | bytes 589832 | tf_op jit(solution)/shard_map/ppermute | solution.py:633
  337.1 7.8 %collective-permute-start.43 = (bf16[1,256,384]{2,1,0:T(8,128)(2,1)S(1)}, bf16[1,256,384]{2,1,0:T(8,128)(2,1)S(1)}, u32[]{:S(2)}, u32[]{:S(2)}) collective-permute-start(bf16[1,256,384]{2,1,0:T(8,128)(2,1)S(1)} %add_convert_fusion.9), channel_id=1, source_target_pairs={{0,4},{2,6},{8,0},{10,2},{16,8},{18,10},{24,16},{26,18},{28,24},{3... | collective-permute-start | bytes 589832 | tf_op jit(solution)/shard_map/ppermute | solution.py:633
  339.5 9.8 %collective-permute-start.49 = (bf16[168,640]{1,0:T(8,128)(2,1)S(1)}, bf16[168,640]{1,0:T(8,128)(2,1)S(1)}, u32[]{:S(2)}, u32[]{:S(2)}) collective-permute-start(bf16[168,640]{1,0:T(8,128)(2,1)S(1)} %get-tuple-element.272), channel_id=1, source_target_pairs={{0,4},{2,6},{8,0},{10,2},{16,8},{18,10},{24,16},{26,18},{28,24},{3... | collective-permute-start | bytes 645128 | tf_op jit(solution)/shard_map/ppermute | solution.py:633
  344.9 8.3 %collective-permute-start.44 = (bf16[1,256,384]{2,1,0:T(8,128)(2,1)S(1)}, bf16[1,256,384]{2,1,0:T(8,128)(2,1)S(1)}, u32[]{:S(2)}, u32[]{:S(2)}) collective-permute-start(bf16[1,256,384]{2,1,0:T(8,128)(2,1)S(1)} %add_convert_fusion.8), channel_id=1, source_target_pairs={{0,4},{2,6},{8,0},{10,2},{16,8},{18,10},{24,16},{26,18},{28,24},{3... | collective-permute-start | bytes 589832 | tf_op jit(solution)/shard_map/ppermute | solution.py:633
  345.8 11.1 %collective-permute-start.47 = (bf16[168,640]{1,0:T(8,128)(2,1)S(1)}, bf16[168,640]{1,0:T(8,128)(2,1)}, u32[]{:S(2)}, u32[]{:S(2)}) collective-permute-start(bf16[168,640]{1,0:T(8,128)(2,1)S(1)} %get-tuple-element.273), channel_id=1, source_target_pairs={{0,8},{2,10},{8,16},{10,18},{16,24},{18,26},{24,28},{26,30},{28,20... | collective-permute-start | bytes 645128 | tf_op jit(solution)/shard_map/ppermute | solution.py:633
  350.5 6.5 %collective-permute-start.50 = (bf16[168,640]{1,0:T(8,128)(2,1)S(1)}, bf16[168,640]{1,0:T(8,128)(2,1)}, u32[]{:S(2)}, u32[]{:S(2)}) collective-permute-start(bf16[168,640]{1,0:T(8,128)(2,1)S(1)} %fusion.3), channel_id=1, source_target_pairs={{0,4},{2,6},{8,0},{10,2},{16,8},{18,10},{24,16},{26,18},{28,24},{3... | collective-permute-start | bytes 645128 | tf_op jit(solution)/shard_map/ppermute | solution.py:633
  373.5 10.0 %collective-permute-start.51 = (bf16[8,64,640]{2,1,0:T(8,128)(2,1)}, bf16[8,64,640]{2,1,0:T(8,128)(2,1)}, u32[]{:S(2)}, u32[]{:S(2)}) collective-permute-start(bf16[8,64,640]{2,1,0:T(8,128)(2,1)} %get-tuple-element.131), channel_id=1, source_target_pairs={{0,2},{2,0},{4,6},{6,4},{8,10},{10,8},{12,14},{14,12},{16,18},{18,... | collective-permute-start | bytes 1966088 | tf_op jit(solution)/shard_map/ppermute | solution.py:884
  380.1 35.3 %collective-permute-start.46 = (f32[3,128,576]{1,2,0:T(8,128)}, f32[3,128,576]{1,2,0:T(8,128)}, u32[]{:S(2)}, u32[]{:S(2)}) collective-permute-start(f32[3,128,576]{1,2,0:T(8,128)} %copy.218), channel_id=1, source_target_pairs={{0,2},{2,0},{4,6},{6,4},{8,10},{10,8},{12,14},{14,12},{16,18},{18,... | collective-permute-start | bytes 2654216 | tf_op jit(solution)/shard_map/ppermute | solution.py:727
  381.4 8.1 %collective-permute-start.60 = (bf16[168,640]{1,0:T(8,128)(2,1)S(1)}, bf16[168,640]{1,0:T(8,128)(2,1)S(1)}, u32[]{:S(2)}, u32[]{:S(2)}) collective-permute-start(bf16[168,640]{1,0:T(8,128)(2,1)S(1)} %copy-done.46), channel_id=1, source_target_pairs={{0,8},{2,10},{8,16},{10,18},{16,24},{18,26},{24,28},{26,30},{28,20... | collective-permute-start | bytes 645128 | tf_op jit(solution)/shard_map/ppermute | solution.py:633
  383.2 7.4 %collective-permute-start.62 = (bf16[168,640]{1,0:T(8,128)(2,1)S(1)}, bf16[168,640]{1,0:T(8,128)(2,1)S(1)}, u32[]{:S(2)}, u32[]{:S(2)}) collective-permute-start(bf16[168,640]{1,0:T(8,128)(2,1)S(1)} %copy-done.45), channel_id=1, source_target_pairs={{0,4},{2,6},{8,0},{10,2},{16,8},{18,10},{24,16},{26,18},{28,24},{3... | collective-permute-start | bytes 645128 | tf_op jit(solution)/shard_map/ppermute | solution.py:633
  384.5 7.7 %collective-permute-start.52 = (bf16[64,640]{1,0:T(8,128)(2,1)S(1)}, bf16[64,640]{1,0:T(8,128)(2,1)S(1)}, u32[]{:S(2)}, u32[]{:S(2)}) collective-permute-start(bf16[64,640]{1,0:T(8,128)(2,1)S(1)} %get-tuple-element.282), channel_id=1, source_target_pairs={{0,8},{2,10},{8,16},{10,18},{16,24},{18,26},{24,28},{26,30},{28,20... | collective-permute-start | bytes 245768 | tf_op jit(solution)/shard_map/ppermute | solution.py:633
  405.9 7.5 %collective-permute-start.55 = (bf16[64,640]{1,0:T(8,128)(2,1)S(1)}, bf16[64,640]{1,0:T(8,128)(2,1)S(1)}, u32[]{:S(2)}, u32[]{:S(2)}) collective-permute-start(bf16[64,640]{1,0:T(8,128)(2,1)S(1)} %get-tuple-element.278), channel_id=1, source_target_pairs={{0,8},{2,10},{8,16},{10,18},{16,24},{18,26},{24,28},{26,30},{28,20... | collective-permute-start | bytes 245768 | tf_op jit(solution)/shard_map/ppermute | solution.py:633
  407.1 6.3 %collective-permute-start.58 = (bf16[64,640]{1,0:T(8,128)(2,1)S(1)}, bf16[64,640]{1,0:T(8,128)(2,1)S(1)}, u32[]{:S(2)}, u32[]{:S(2)}) collective-permute-start(bf16[64,640]{1,0:T(8,128)(2,1)S(1)} %get-tuple-element.279), channel_id=1, source_target_pairs={{0,4},{2,6},{8,0},{10,2},{16,8},{18,10},{24,16},{26,18},{28,24},{3... | collective-permute-start | bytes 245768 | tf_op jit(solution)/shard_map/ppermute | solution.py:633
  (100 other events, 802.8 us)
where the time goes:
time: 428 us; the launch traced here: 421 us
  Pallas kernels  133 us (31%)
  waiting for transfers between devices  116 us (27%)
  starting transfers between devices  60.6 us (14%)
  local copies, waits for them, and re-layouts  55.3 us (13%)
  other arithmetic  40.5 us (9%)
  matrix products  13.4 us (3%)
    pallas_call x9, Pallas kernels, call(): pl.pallas_call(body_of, grid_spec=pltpu.PrefetchScalarGridSpec(num_scalar...  133 us
    ppermute x28, waiting for transfers between devices, ring_scatter(): got = lax.ppermute(moving[way], 'ctx', ring_pairs(chips, sign))  40.5 us
    ppermute x11, waiting for transfers between devices, ring_gather(): ahead = lax.ppermute(ahead, 'ctx', ring_pairs(chips, 1))  35.4 us
    unnamed x201, local copies, waits for them, and re-layouts  31.6 us
    ppermute x28, starting transfers between devices, ring_scatter(): got = lax.ppermute(moving[way], 'ctx', ring_pairs(chips, sign))  31.2 us
    ppermute x10, waiting for transfers between devices, ring_gather(): behind = lax.ppermute(behind, 'ctx', ring_pairs(chips, -1))  18.6 us
    ppermute x1, waiting for transfers between devices, body(): cross = lax.ppermute(same, 'fsdp', planes)  18.4 us
    ppermute x10, starting transfers between devices, ring_gather(): behind = lax.ppermute(behind, 'ctx', ring_pairs(chips, -1))  14.5 us
  transfers between devices with their start and end apart: 63, of which 32 were waited for; matrix products, arithmetic and copies ran while one was open for 22% of the time, Pallas kernels for 14%

commit v1 on v0

--- a/solution.py
+++ b/solution.py
@@ -171,58 +171,32 @@
                 )
 
 
-def unpack_second(place_ref, part_refs, pack_ref, sems, out_w_ref, gate_w_ref, up_w_ref, down_w_ref):
-    ctx = pack_ref.shape[1]
-    f_cols, o_cols, half = FF // ctx, MODEL_WIDTH // ctx, MODEL_WIDTH // 2
-    copies = []
-    for part, part_ref in enumerate(part_refs):
-        core = jnp.abs(place_ref[0] - part // 2)
-        plane = jnp.abs(place_ref[1] - part % 2)
-        for k in range(part_ref.shape[0]):
-            index = 2 * place_ref[2 + k] + core
-            copies.append(
-                pltpu.make_async_copy(
-                    part_ref.at[k], pack_ref.at[plane, index], sems.at[part, k]
-                )
-            )
-    for copy in copies:
-        copy.start()
-    for copy in copies:
-        copy.wait()
+def unpack_second(pack_ref, out_w_ref, gate_w_ref, up_w_ref, down_w_ref):
+    ctx = pack_ref.shape[0]
+    f_cols, o_cols = FF // ctx, MODEL_WIDTH // ctx
     for c in range(ctx):
         here = slice(c * f_cols, (c + 1) * f_cols)
-        low, high = pack_ref[0, c, :f_cols, :], pack_ref[1, c, :f_cols, :]
-        gate_w_ref[here, :] = jnp.concatenate([low[:, :half], high[:, :half]], axis=1)
-        up_w_ref[here, :] = jnp.concatenate(
-            [low[:, half:MODEL_WIDTH], high[:, half:MODEL_WIDTH]], axis=1
-        )
-
-    def natural(plane, base, lanes):
-        pieces = [
-            pack_ref[plane, c, base : base + o_cols, lanes].astype(f32) for c in range(ctx)
-        ]
+        gate_w_ref[here, :] = pack_ref[c, :f_cols, :MODEL_WIDTH]
+        up_w_ref[here, :] = pack_ref[c, f_cols : 2 * f_cols, :MODEL_WIDTH]
+
+    def natural(base, size):
+        pieces = [pack_ref[c, base : base + o_cols, :size].astype(f32) for c in range(ctx)]
         return jnp.concatenate(pieces, axis=0).astype(bf16)
 
-    base = f_cols + o_cols
-    for plane in range(2):
-        begin = plane * (FF // 2)
-        down_w_ref[:, begin : begin + LANES] = natural(plane, f_cols, slice(0, LANES))
-        down_w_ref[:, begin + LANES : begin + FF // 2] = natural(plane, base, slice(0, REST))
-    out_w_ref[...] = jnp.concatenate(
-        [natural(plane, base, slice(REST, REST + half)) for plane in range(2)], axis=1
-    )
+    base = 2 * f_cols
+    out_w_ref[...] = natural(base, MODEL_WIDTH)
+    for begin in range(0, FF, LANES):
+        base += o_cols
+        size = min(LANES, FF - begin)
+        down_w_ref[:, begin : begin + size] = natural(base, size)
 
 
 def middle_kernel(
-    place_ref,
     x_ref,
     attn_ref,
     cot_ref,
     gain_ref,
-    part_a_ref,
-    part_b_ref,
-    part_c_ref,
-    part_d_ref,
+    pack_ref,
     block_ref,
     normed_ref,
     hidden_ref,
@@ -236,15 +210,10 @@
     gate_w_ref,
     up_w_ref,
     down_w_ref,
-    pack_ref,
-    sems,
 ):
     @pl.when(pl.program_id(0) == 0)
     def _():
-        parts = (part_a_ref, part_b_ref, part_c_ref, part_d_ref)
-        unpack_second(
-            place_ref, parts, pack_ref, sems, out_w_ref, gate_w_ref, up_w_ref, down_w_ref
-        )
+        unpack_second(pack_ref, out_w_ref, gate_w_ref, up_w_ref, down_w_ref)
 
     attn = attn_ref[0]
     cot = cot_ref[0]
@@ -459,42 +428,22 @@
         other_ref[g, begin : begin + 2, :width] = gains_ref[...].astype(bf16)
 
 
-def pack_second_kernel(
-    place_ref, out_g_ref, gate_g_ref, up_g_ref, down_g_ref, a_ref, b_ref, c_ref, d_ref, pack_ref, sems
-):
-    ctx = pack_ref.shape[1]
-    f_cols, o_cols, half = FF // ctx, MODEL_WIDTH // ctx, MODEL_WIDTH // 2
-    base = f_cols + o_cols
-    for plane in range(2):
-        lanes = slice(plane * half, (plane + 1) * half)
+def pack_second_kernel(out_g_ref, gate_g_ref, up_g_ref, down_g_ref, pack_ref):
+    ctx = pack_ref.shape[0]
+    f_cols, o_cols = FF // ctx, MODEL_WIDTH // ctx
+    for c in range(ctx):
+        here = slice(c * f_cols, (c + 1) * f_cols)
+        pack_ref[c, :f_cols, :MODEL_WIDTH] = gate_g_ref[here, :]
+        pack_ref[c, f_cols : 2 * f_cols, :MODEL_WIDTH] = up_g_ref[here, :]
+    base = 2 * f_cols
+    parts = [out_g_ref[...]]
+    parts += [down_g_ref[:, begin : min(begin + LANES, FF)] for begin in range(0, FF, LANES)]
+    for part in parts:
+        wide = part.astype(f32)
         for c in range(ctx):
-            here = slice(c * f_cols, (c + 1) * f_cols)
-            pack_ref[plane, c, :f_cols, :MODEL_WIDTH] = jnp.concatenate(
-                [gate_g_ref[here, lanes], up_g_ref[here, lanes]], axis=1
-            )
-        begin = plane * (FF // 2)
-        first = down_g_ref[:, begin : begin + LANES].astype(f32)
-        rest = down_g_ref[:, begin + LANES : begin + FF // 2]
-        second = jnp.concatenate([rest, out_g_ref[:, lanes]], axis=1).astype(f32)
-        for c in range(ctx):
-            here = slice(c * o_cols, (c + 1) * o_cols)
-            pack_ref[plane, c, f_cols:base, :] = first[here].astype(bf16)
-            pack_ref[plane, c, base : base + o_cols, : REST + half] = second[here].astype(bf16)
-    copies = []
-    for part, part_ref in enumerate((a_ref, b_ref, c_ref, d_ref)):
-        core = jnp.abs(place_ref[0] - part // 2)
-        plane = jnp.abs(place_ref[1] - part % 2)
-        for k in range(part_ref.shape[0]):
-            index = 2 * place_ref[2 + k] + core
-            copies.append(
-                pltpu.make_async_copy(
-                    pack_ref.at[plane, index], part_ref.at[k], sems.at[part, k]
-                )
-            )
-    for copy in copies:
-        copy.start()
-    for copy in copies:
-        copy.wait()
+            piece = wide[c * o_cols : (c + 1) * o_cols].astype(bf16)
+            pack_ref[c, base : base + o_cols, : part.shape[1]] = piece
+        base += o_cols
 
 
 def one(shape):
@@ -617,12 +566,14 @@
     return total
 
 
-def ring_scatter(terms, flip):
+def ring_scatter(terms, flip, pin=()):
     chips = lax.axis_size("ctx") // 2
     steps = (chips // 2, (chips - 1) // 2)
     if flip:
         steps = steps[::-1]
     moving = [terms[steps[0]]().astype(bf16), terms[-steps[1] % chips]().astype(bf16)]
+    if pin:
+        moving = list(join(moving, *pin))
     trace = []
     for t in range(max(steps)):
         for way in range(2):
@@ -735,10 +686,6 @@
     slots = (jnp.array(position_of, jnp.int32) - position) % chunks
     where = jnp.concatenate([core[None].astype(jnp.int32), slots])
     reached = jnp.array(ring, jnp.int32)[(position + jnp.arange(chunks)) % chunks]
-    two_planes = lax.axis_size("fsdp") == 2
-    plane = lax.axis_index("fsdp") if two_planes else jnp.zeros((), jnp.int32)
-    place = jnp.concatenate([core[None].astype(jnp.int32), plane[None].astype(jnp.int32), reached])
-    planes = [(0, 1), (1, 0)]
 
     turned_low = [matrix.astype(bf16).T for matrix in masters]
     q_cols, kv_cols = QUERY_WIDTH // ctx, KEY_WIDTH // ctx
@@ -762,20 +709,14 @@
         scalars=(where,),
         us=3.3,
     )
-    half = MODEL_WIDTH // 2
-
-    def second_part(gate, up, output, down):
-        return jnp.concatenate(
-            [
-                widen(jnp.concatenate([gate, up], axis=1)),
-                down[:, :LANES],
-                widen(jnp.concatenate([down[:, LANES:], output], axis=1)),
-            ],
-            axis=0,
-        )
-
-    def later(part):
-        return lax.optimization_barrier((part, first_other))[0]
+    down_part = rows_gather(turned_low[6])
+    second_part = jnp.concatenate(
+        [widen(rows_gather(jnp.concatenate(turned_low[4:6] + turned_low[3:4], axis=0)))]
+        + [widen(down_part[:, begin : begin + LANES]) for begin in range(0, FF, LANES)],
+        axis=0,
+    )
+    (second_part,) = join([second_part], first_other)
+    second_all = lax.all_gather(second_part, "ctx", axis=0, tiled=False)
 
     x = take(tokens)
     cot = take(cotangent)
@@ -805,23 +746,6 @@
     tile_rows = (KV_HEADS, GROUP * blk, PACK)
     kv_trace = []
     kv_all = ring_gather(kv, False, trace=kv_trace)
-    outer = (turned_low[4], turned_low[5], turned_low[3], turned_low[6])
-    if two_planes:
-        same = jnp.stack(ring_gather(later(second_part(*outer)), True, {1: [inward], 2: kv_trace[0], 3: kv_trace[1]}), axis=0)
-        cross = lax.ppermute(same, "fsdp", planes)
-    else:
-        outer = [rows_gather(part) for part in outer]
-        same, cross = [
-            jnp.stack(
-                ring_gather(
-                    second_part(*[jnp.split(part, 2, axis=1)[side] for part in outer]), True
-                ),
-                axis=0,
-            )
-            for side in range(2)
-        ]
-    second_parts = [same, cross] + [lax.ppermute(part, "ctx", partners) for part in (same, cross)]
-
     attn, logs = call(
         functools.partial(attend_kernel, chunks),
         seqs,
@@ -855,8 +779,8 @@
             (one, attn),
             (one, cot),
             (whole, gain_two),
-        ]
-        + [(anywhere, part) for part in second_parts],
+            (whole, second_all),
+        ],
         [
             (one, wide, f32),
             (one, wide, bf16),
@@ -873,10 +797,7 @@
             pltpu.VMEM((FF, MODEL_WIDTH), bf16),
             pltpu.VMEM((FF, MODEL_WIDTH), bf16),
             pltpu.VMEM((MODEL_WIDTH, FF), bf16),
-            pltpu.VMEM((2, ctx) + same.shape[1:], bf16),
-            pltpu.SemaphoreType.DMA((4, chunks)),
         ],
-        scalars=(place,),
         us=26.0,
     )
     block_output = give(block_local)
@@ -890,7 +811,7 @@
         dattn_, dgate_ = join([dattn, dgate], earlier)
         (dup_,) = join([dup], *behind[0])
         (hidden_,) = join([hidden], *behind[1])
-        packs = call(
+        (second_pack,) = call(
             pack_second_kernel,
             1,
             [
@@ -899,42 +820,24 @@
                 (whole, weight_grad(dup_, normed_two).astype(bf16)),
                 (whole, weight_grad(cot, hidden_).astype(bf16)),
             ],
-            [(anywhere, same.shape, bf16)] * 4,
-            scalars=(place,),
-            scratch=[
-                pltpu.VMEM((2, ctx) + same.shape[1:], bf16),
-                pltpu.SemaphoreType.DMA((4, chunks)),
-            ],
-            us=7.7,
+            [(whole, second_all.shape, bf16)],
+            us=6.3,
             after=behind[2],
         )
-        got = [lax.ppermute(part, "ctx", partners) for part in packs[2:]]
-        if two_planes:
-            sent = lax.ppermute(plus(packs[1], got[1]).astype(bf16), "fsdp", planes)
-            terms = [lambda k=k: plus(packs[0][k], got[0][k], sent[k]) for k in range(chunks)]
-            sums, trace = ring_scatter(terms, True)
-            sums, before_last, before_final = [sums], got, [sent]
-        else:
-            sums = [
-                ring_scatter(
-                    [lambda k=k, i=i: plus(packs[i][k], got[i][k]) for k in range(chunks)], True
-                )[0]
-                for i in range(2)
-            ]
-            before_last, before_final, trace = got, [], [[], []]
-        base = f_cols + o_cols
-        result = []
-        for pick in (
-            lambda part: part[base:, REST : REST + half],
-            lambda part: part[:f_cols, :half],
-            lambda part: part[:f_cols, half:MODEL_WIDTH],
-            lambda part: jnp.concatenate([part[f_cols:base], part[base:, :REST]], axis=1),
-        ):
-            if two_planes:
-                result.append(pick(sums[0]))
-            else:
-                result.append(rows_scatter(jnp.concatenate([pick(part) for part in sums], axis=1)))
-        return result, before_last, before_final, trace[1]
+        second_sum = lax.psum_scatter(second_pack, "ctx", scatter_dimension=0, tiled=False)
+        base = 2 * f_cols + o_cols
+        down_sum = rows_scatter(
+            jnp.concatenate(
+                [
+                    second_sum[base + i * o_cols : base + (i + 1) * o_cols, : min(LANES, FF - begin)]
+                    for i, begin in enumerate(range(0, FF, LANES))
+                ],
+                axis=1,
+            ).astype(f32)
+        )
+        second_sum = rows_scatter(second_sum[:base, :MODEL_WIDTH].astype(f32))
+        outer = (second_sum[2 * f_cols :], second_sum[:f_cols], second_sum[f_cols : 2 * f_cols])
+        return second_pack, outer + (down_sum,)
 
     dinputs, dalls, gain_one_grads, traces = [], [], [], []
     last = seqs - 1
@@ -942,8 +845,8 @@
         these = since(first)
         waits = []
         if first == last:
-            outer_reduced, before_last, before_final, before_pack = outer_sums(dquery)
-            waits = before_last
+            second_pack, outer_reduced = outer_sums(dquery)
+            waits = [second_pack]
         dquery, *dkv = call(
             functools.partial(attend_back_kernel, chunks, first),
             count,
@@ -965,7 +868,9 @@
             after=waits,
         )
         dkv_own, trace = ring_scatter(
-            [lambda k=k, dkv=dkv: dkv[k] for k in range(chunks)], first > 0
+            [lambda k=k, dkv=dkv: dkv[k] for k in range(chunks)],
+            first > 0,
+            traces[-1][-1] if traces else (),
         )
         traces.append(trace)
         dinput, dall, gain_one_grad = call(
@@ -987,7 +892,6 @@
                 (one, (count, 1, MODEL_WIDTH), f32),
             ],
             us=2.0 * count,
-            after=before_final if first == last else (),
         )
         dinputs.append(dinput)
         dalls.append(dall)
@@ -1003,7 +907,6 @@
         scalars=(where,),
         scratch=[pltpu.VMEM((INNER, MODEL_WIDTH), f32)],
         us=3.5,
-        after=before_pack,
     )
     first_sum = rows_scatter(reduced_packs(*first_packs, False)[0][:, :MODEL_WIDTH])
     reduced = (

time: 428 us -> 426 us (level)
  local copies, waits for them, and re-layouts: 55.3 us -> 41.1 us
  between operations: 2.2 us -> 15.4 us
  waiting for transfers between devices: 116 us -> 124 us
    ppermute x11 -> x8, waiting for transfers between devices: 35.4 us -> 73.1 us  [ring_gather(): ahead = lax.ppermute(ahead, 'ctx', ring_pairs(chips, 1))]
    ppermute x6 -> x0, waiting for transfers between devices: 18.4 us -> none  [the longest x1 18.4 us: body(): cross = lax.ppermute(same, 'fsdp', planes)]
    unnamed x201 -> x154, local copies, waits for them, and re-layouts: 31.6 us -> 15.3 us
    ppermute x10 -> x6, waiting for transfers between devices: 18.6 us -> 7.08 us  [ring_gather(): behind = lax.ppermute(behind, 'ctx', ring_pairs(chips, -1))]
    ppermute x11 -> x8, starting transfers between devices: 7.81 us -> 14.9 us  [ring_gather(): ahead = lax.ppermute(ahead, 'ctx', ring_pairs(chips, 1))]
    ppermute x28 -> x21, starting transfers between devices: 31.2 us -> 25 us  [ring_scatter(): got = lax.ppermute(moving[way], 'ctx', ring_pairs(chips, sign))]
    ppermute x10 -> x6, starting transfers between devices: 14.5 us -> 8.71 us  [ring_gather(): behind = lax.ppermute(behind, 'ctx', ring_pairs(chips, -1))]
    ppermute x28 -> x21, waiting for transfers between devices: 40.5 us -> 35.6 us  [ring_scatter(): got = lax.ppermute(moving[way], 'ctx', ring_pairs(chips, sign))]
  transfers between devices with their start and end apart: 63 -> 49, of which waited for: 32 -> 26; matrix products, arithmetic and copies ran while one was open for 22% -> 18% of each run, Pallas kernels for 14% -> 17%
where the time goes in v1:
time: 426 us; the launch traced here: 419 us
  Pallas kernels  130 us (31%)
  waiting for transfers between devices  124 us (29%)
  starting transfers between devices  58.6 us (14%)
  local copies, waits for them, and re-layouts  41.1 us (10%)
  other arithmetic  36.6 us (9%)
  between operations  15.4 us (4%)
  matrix products  13.5 us (3%)
    pallas_call x9, Pallas kernels, call(): pl.pallas_call(body_of, grid_spec=pltpu.PrefetchScalarGridSpec(num_scalar...  130 us
    ppermute x8, waiting for transfers between devices, ring_gather(): ahead = lax.ppermute(ahead, 'ctx', ring_pairs(chips, 1))  73.1 us
    ppermute x21, waiting for transfers between devices, ring_scatter(): got = lax.ppermute(moving[way], 'ctx', ring_pairs(chips, sign))  35.6 us
    ppermute x21, starting transfers between devices, ring_scatter(): got = lax.ppermute(moving[way], 'ctx', ring_pairs(chips, sign))  25 us
    unnamed x154, local copies, waits for them, and re-layouts  15.3 us
    ppermute x8, starting transfers between devices, ring_gather(): ahead = lax.ppermute(ahead, 'ctx', ring_pairs(chips, 1))  14.9 us
    dot_general x4, matrix products, weight_grad(): lax.dot_general(left, right, (((0, 1), (0, 1)), ((), ())), preferred_elem...  13.5 us
    convert_element_type x13, other arithmetic, ring_scatter(): got = plus(got, terms[sign * left % chips]()).astype(bf16)  11 us
  transfers between devices with their start and end apart: 49, of which 26 were waited for; matrix products, arithmetic and copies ran while one was open for 18% of the time, Pallas kernels for 17%

profile of v1, /device:TPU:0, one launch (start us, length us, event | category | flops | bytes accessed | tf_op | source)
XLA Modules:
  0.0 419.3 jit_solution(10109071963294552807)
XLA Ops:
  9.6 3.0 collective-permute-start.1
  16.7 2.0 collective-permute-start.19
  20.9 2.4 collective-permute-done.2
  25.4 2.7 collective-permute-done.3
  30.4 3.9 collective-permute-done.7
  34.9 3.9 collective-permute-done.8
  52.9 3.4 shard_map.485.refs_2_.refs_7_
  56.3 6.3 %shard_map.486 = (bf16[3,256,576]{2,1,0:T(8,128)(2,1)}, bf16[3,4,3,192,128]{4,3,2,1,0:T(8,128)(2,1)}, bf16[3,256,384]{2,1,0:T(8,128)(2,1)}) custom-call(bf16[3,256,576]{2,1,0:T(8,128)(2,1)} %pad_maximum_fusion.refs_0_, f32[1,576]{1,0:T(1,128)} %get-tuple-element.279.refs_1_, bf16[960,576]{1,0:T(8,128)(2,1)} %shard_map.485.refs_2_.refs_7_, ...), custom_call_target="tpu_custom_call" | custom-call | flops 7151699968 | bytes 6023424 | tf_op jit(solution)/shard_map/pallas_call | solution.py:485
  64.6 16.9 %collective-permute-done.13.refs_9_ = bf16[3,256,384]{2,1,0:T(8,128)(2,1)S(1)} collective-permute-done((bf16[3,256,384]{2,1,0:T(8,128)(2,1)}, bf16[3,256,384]{2,1,0:T(8,128)(2,1)S(1)}, u32[]{:S(2)}, u32[]{:S(2)}) %collective-permute-start.13) | collective-permute-done | bytes 589856 | tf_op jit(solution)/shard_map/ppermute | solution.py:549
  81.5 3.9 collective-permute-start.14
  87.7 23.0 %collective-permute-done.14.refs_8_ = bf16[3,256,384]{2,1,0:T(8,128)(2,1)S(1)} collective-permute-done((bf16[3,256,384]{2,1,0:T(8,128)(2,1)S(1)}, bf16[3,256,384]{2,1,0:T(8,128)(2,1)S(1)}, u32[]{:S(2)}, u32[]{:S(2)}) %collective-permute-start.14) | collective-permute-done | bytes 589856 | tf_op jit(solution)/shard_map/ppermute | solution.py:549
  110.7 7.9 %collective-permute-start.15 = (bf16[3,256,384]{2,1,0:T(8,128)(2,1)S(1)}, bf16[3,256,384]{2,1,0:T(8,128)(2,1)}, u32[]{:S(2)}, u32[]{:S(2)}) collective-permute-start(bf16[3,256,384]{2,1,0:T(8,128)(2,1)S(1)} %collective-permute-done.14.refs_8_), channel_id=1, source_target_pairs={{0,8},{2,10},{8,16},{10,18},{16,24},{18,26},{24,28},{26,30},{28,20... | collective-permute-start | bytes 1769480 | tf_op jit(solution)/shard_map/ppermute | solution.py:549
  121.1 13.5 %collective-permute-done.15.refs_7_ = bf16[3,256,384]{2,1,0:T(8,128)(2,1)} collective-permute-done((bf16[3,256,384]{2,1,0:T(8,128)(2,1)S(1)}, bf16[3,256,384]{2,1,0:T(8,128)(2,1)}, u32[]{:S(2)}, u32[]{:S(2)}) %collective-permute-start.15) | collective-permute-done | bytes 589856 | tf_op jit(solution)/shard_map/ppermute | solution.py:549
  138.0 11.7 %collective-permute-done.16.refs_6_ = bf16[3,256,384]{2,1,0:T(8,128)(2,1)} collective-permute-done((bf16[3,256,384]{2,1,0:T(8,128)(2,1)}, bf16[3,256,384]{2,1,0:T(8,128)(2,1)}, u32[]{:S(2)}, u32[]{:S(2)}) %collective-permute-start.16) | collective-permute-done | bytes 589856 | tf_op jit(solution)/shard_map/ppermute | solution.py:549
  149.7 33.4 %shard_map.487 = (bf16[3,256,576]{2,1,0:T(8,128)(2,1)}, f32[3,4,3,192,128]{4,3,2,1,0:T(8,128)}) custom-call(s32[3,32]{1,0:T(4,128)} %copy-done.54, bf16[3,4,3,192,128]{4,3,2,1,0:T(8,128)(2,1)} %get-tuple-element.70.refs_1_, bf16[3,256,384]{2,1,0:T(8,128)(2,1)} %get-tuple-element.71.refs_2_, bf16[3,256,384]{2,1,0:T(8,128)(2,1)} %copy-done.61, ...), custom_call_target="tpu_custom_call" | custom-call | flops 38065500160 | bytes 10911744 | tf_op jit(solution)/shard_map/pallas_call | solution.py:485
  183.1 24.0 %shard_map.489 = (f32[3,256,576]{2,1,0:T(8,128)}, bf16[3,256,576]{2,1,0:T(8,128)(2,1)}, bf16[3,256,1536]{2,1,0:T(8,128)(2,1)}, bf16[3,256,1536]{2,1,0:T(8,128)(2...) custom-call(bf16[3,256,576]{2,1,0:T(8,128)(2,1)} %pad_maximum_fusion, ...), custom_call_target="tpu_custom_call" | custom-call | flops 29991000064 | bytes 22815744 | tf_op jit(solution)/shard_map/pallas_call | solution.py:485
  207.2 30.0 %shard_map.490 = (bf16[2,256,576]{2,1,0:T(8,128)(2,1)}, bf16[2,256,384]{2,1,0:T(8,128)(2,1)}, bf16[2,256,384]{2,1,0:T(8,128)(2,1)}, bf16[2,256,384]{2,1,0:T(8,12...) custom-call(s32[3,32]{1,0:T(4,128)} %copy-done.54, ...), custom_call_target="tpu_custom_call" | custom-call | flops 39218999296 | bytes 16318464 | tf_op jit(solution)/shard_map/pallas_call | solution.py:485
  239.3 3.6 bitcast_convert_fusion.2
  242.9 1.8 bitcast_convert_fusion.3.refs_0_
  244.8 2.3 copy.208.refs_1_
  252.3 3.5 bitcast_convert_fusion.1
  255.8 2.3 copy.209.refs_2_
  262.8 4.5 %bitcast_convert_fusion.refs_3_ = bf16[576,1536]{1,0:T(8,128)(2,1)} fusion(bf16[3,256,1536]{2,1,0:T(8,128)(2,1)} %shard_map.494, bf16[3,128,576]{2,1,0:T(8,128)(2,1)S(1)} %collective-permute-done.17, bf16[3,128,576]{2,1,0:T(8,128)(2,1)S(1)} %copy.237), kind=kOutput, calls=%fused_computation.2 | convolution fusion | flops 1361608704 | bytes 5013504 | tf_op jit(solution)/shard_map/dot_general | solution.py:618
  270.3 6.3 %shard_map.495.refs_15_ = bf16[16,336,640]{2,1,0:T(8,128)(2,1)} custom-call(bf16[576,576]{1,0:T(8,128)(2,1)} %bitcast_convert_fusion.3.refs_0_, bf16[1536,576]{1,0:T(8,128)(2,1)} %copy.208.refs_1_, bf16[1536,576]{1,0:T(8,128)(2,1)} %copy.209.refs_2_, bf16[576,1536]{1,0:T(8,128)(2,1)} %bitcast_convert_fusion.refs_3_, ...), custom_call_target="tpu_custom_call" | custom-call | flops 7267049984 | bytes 12853248 | tf_op jit(solution)/shard_map/pallas_call | solution.py:485
  278.4 16.9 %shard_map.496 = (bf16[1,256,576]{2,1,0:T(8,128)(2,1)}, bf16[1,256,384]{2,1,0:T(8,128)(2,1)}, bf16[1,256,384]{2,1,0:T(8,128)(2,1)}, bf16[1,256,384]{2,1,0:T(8,12...) custom-call(s32[3,32]{1,0:T(4,128)} %copy-done.54, ...), custom_call_target="tpu_custom_call" | custom-call | flops 19609499648 | bytes 14450688 | tf_op jit(solution)/shard_map/pallas_call | solution.py:485
  298.1 2.1 convert_add_fusion.refs_3_
  300.1 3.8 collective-permute-done.31
  306.2 10.3 %collective-permute-done.32 = bf16[1,256,384]{2,1,0:T(8,128)(2,1)S(1)} collective-permute-done((bf16[1,256,384]{2,1,0:T(8,128)(2,1)S(1)}, bf16[1,256,384]{2,1,0:T(8,128)(2,1)S(1)}, u32[]{:S(2)}, u32[]{:S(2)}) %collective-permute-start.32) | collective-permute-done | bytes 196640 | tf_op jit(solution)/shard_map/ppermute | solution.py:584
  316.7 2.9 collective-permute-start.30
  319.6 9.8 %collective-permute-done.33 = bf16[1,256,384]{2,1,0:T(8,128)(2,1)S(1)} collective-permute-done((bf16[1,256,384]{2,1,0:T(8,128)(2,1)S(1)}, bf16[1,256,384]{2,1,0:T(8,128)(2,1)S(1)}, u32[]{:S(2)}, u32[]{:S(2)}) %collective-permute-start.33) | collective-permute-done | bytes 196640 | tf_op jit(solution)/shard_map/ppermute | solution.py:584
  330.4 4.9 %shard_map.491 = (f32[2,256,576]{2,1,0:T(8,128)}, bf16[2,256,1024]{2,1,0:T(8,128)(2,1)}, f32[2,1,576]{2,1,0:T(1,128)}) custom-call(bf16[3,256,576]{2,1,0:T(8,128)(2,1)} %pad_maximum_fusion.refs_0_, f32[1,576]{1,0:T(1,128)} %get-tuple-element.279.refs_1_, bf16[2,256,576]{2,1,0:T(8,128)(2,1)} %get-tuple-element.76.refs_2_, ...), custom_call_target="tpu_custom_call" | custom-call | flops 4614000128 | bytes 8157952 | tf_op jit(solution)/shard_map/pallas_call | solution.py:485
  337.6 3.8 collective-permute-done.34
  342.6 3.2 shard_map.499
  346.4 5.1 %shard_map.498 = (bf16[8,64,640]{2,1,0:T(8,128)(2,1)}, bf16[8,64,640]{2,1,0:T(8,128)(2,1)}) custom-call(s32[9]{0:T(128)} %pad_add_fusion.1.refs_0_, bf16[3,256,576]{2,1,0:T(8,128)(2,1)} %get-tuple-element.106.refs_1_, bf16[2,256,1024]{2,1,0:T(8,128)(2,1)} %get-tuple-element.107.refs_2_, bf16[1,256,1024]{2,1,0:T(8,128)(2,1)} %get-tuple-element.221.refs_3_, ...), custom_call_target="tpu_custom_call" | custom-call | flops 4037250048 | bytes 3772928 | tf_op jit(solution)/shard_map/pallas_call | solution.py:485
  352.1 2.6 fusion.43
  354.7 2.4 copy.197
  360.9 1.9 collective-permute-start.41
  362.9 2.1 collective-permute-done.37
  366.6 2.2 collective-permute-start.38
  369.9 2.6 copy.215
  372.5 1.8 fusion.9
  374.3 1.9 collective-permute-start.39
  376.2 2.1 collective-permute-start.42
  385.0 2.1 collective-permute-done.40
  389.9 1.8 collective-permute-start.44
  398.9 1.8 collective-permute-start.46
  401.2 2.0 collective-permute-done.46
  404.1 2.4 collective-permute-done.45
  (334 shorter events, 95.0 us)
Async XLA Ops:
  7.2 175.9 %all-gather.3.cloned.1.call-start = ((), (), s32[]{:S(2)}) async-start(), calls=%async_computation.2 | async-start | bytes 7311360 | tf_op jit(solution)/shard_map/all_gather | solution.py:719
  9.6 9.1 %collective-permute-start.1 = (bf16[62,288]{1,0:T(8,128)(2,1)S(1)}, bf16[62,288]{1,0:T(8,128)(2,1)S(1)}, u32[]{:S(2)}, u32[]{:S(2)}) collective-permute-start(bf16[62,288]{1,0:T(8,128)(2,1)S(1)} %pad_maximum_fusion.5), channel_id=1, source_target_pairs={{0,1},{1,0},{2,3},{3,2},{4,5},{5,4},{6,7},{7,6},{8,9},{9,8},{10,11... | collective-permute-start | bytes 107144 | tf_op jit(solution)/shard_map/ppermute | solution.py:596
  15.7 23.3 %collective-permute-start.18 = (bf16[228,288]{1,0:T(8,128)(2,1)S(1)}, bf16[228,288]{1,0:T(8,128)(2,1)S(1)}, u32[]{:S(2)}, u32[]{:S(2)}) collective-permute-start(bf16[228,288]{1,0:T(8,128)(2,1)S(1)} %pad_maximum_fusion.3), channel_id=1, source_target_pairs={{0,1},{1,0},{2,3},{3,2},{4,5},{5,4},{6,7},{7,6},{8,9},{9,8},{10,11... | collective-permute-start | bytes 393992 | tf_op jit(solution)/shard_map/ppermute | solution.py:596
  16.7 22.2 %collective-permute-start.19 = (bf16[36,768]{1,0:T(8,128)(2,1)S(1)}, bf16[36,768]{1,0:T(8,128)(2,1)S(1)}, u32[]{:S(2)}, u32[]{:S(2)}) collective-permute-start(bf16[36,768]{1,0:T(8,128)(2,1)S(1)} %convert_bitcast_fusion.2), channel_id=1, source_target_pairs={{0,1},{1,0},{2,3},{3,2},{4,5},{5,4},{6,7},{7,6},{8,9},{9,8},{10,11... | collective-permute-start | bytes 165896 | tf_op jit(solution)/shard_map/ppermute | solution.py:596
  18.9 4.5 %collective-permute-start.2 = (bf16[64,640]{1,0:T(8,128)(2,1)S(1)}, bf16[64,640]{1,0:T(8,128)(2,1)S(1)}, u32[]{:S(2)}, u32[]{:S(2)}) collective-permute-start(bf16[64,640]{1,0:T(8,128)(2,1)S(1)} %pad.52), channel_id=1, source_target_pairs={{0,4},{2,6},{8,0},{10,2},{16,8},{18,10},{24,16},{26,18},{28,24},{3... | collective-permute-start | bytes 245768 | tf_op jit(solution)/shard_map/ppermute | solution.py:552
  20.4 4.4 %collective-permute-start.5 = (bf16[64,640]{1,0:T(8,128)(2,1)S(1)}, bf16[64,640]{1,0:T(8,128)(2,1)S(1)}, u32[]{:S(2)}, u32[]{:S(2)}) collective-permute-start(bf16[64,640]{1,0:T(8,128)(2,1)S(1)} %pad.52), channel_id=1, source_target_pairs={{0,8},{2,10},{8,16},{10,18},{16,24},{18,26},{24,28},{26,30},{28,20... | collective-permute-start | bytes 245768 | tf_op jit(solution)/shard_map/ppermute | solution.py:549
  23.3 4.7 %collective-permute-start.3 = (bf16[64,640]{1,0:T(8,128)(2,1)S(1)}, bf16[64,640]{1,0:T(8,128)(2,1)S(1)}, u32[]{:S(2)}, u32[]{:S(2)}) collective-permute-start(bf16[64,640]{1,0:T(8,128)(2,1)S(1)} %collective-permute-done.2), channel_id=1, source_target_pairs={{0,4},{2,6},{8,0},{10,2},{16,8},{18,10},{24,16},{26,18},{28,24},{3... | collective-permute-start | bytes 245768 | tf_op jit(solution)/shard_map/ppermute | solution.py:552
  24.8 5.0 %collective-permute-start.6 = (bf16[64,640]{1,0:T(8,128)(2,1)S(1)}, bf16[64,640]{1,0:T(8,128)(2,1)S(1)}, u32[]{:S(2)}, u32[]{:S(2)}) collective-permute-start(bf16[64,640]{1,0:T(8,128)(2,1)S(1)} %collective-permute-done.5), channel_id=1, source_target_pairs={{0,8},{2,10},{8,16},{10,18},{16,24},{18,26},{24,28},{26,30},{28,20... | collective-permute-start | bytes 245768 | tf_op jit(solution)/shard_map/ppermute | solution.py:549
  28.1 6.8 %collective-permute-start.4 = (bf16[64,640]{1,0:T(8,128)(2,1)S(1)}, bf16[64,640]{1,0:T(8,128)(2,1)S(1)}, u32[]{:S(2)}, u32[]{:S(2)}) collective-permute-start(bf16[64,640]{1,0:T(8,128)(2,1)S(1)} %collective-permute-done.3), channel_id=1, source_target_pairs={{0,4},{2,6},{8,0},{10,2},{16,8},{18,10},{24,16},{26,18},{28,24},{3... | collective-permute-start | bytes 245768 | tf_op jit(solution)/shard_map/ppermute | solution.py:552
  29.8 4.5 %collective-permute-start.7 = (bf16[64,640]{1,0:T(8,128)(2,1)S(1)}, bf16[64,640]{1,0:T(8,128)(2,1)S(1)}, u32[]{:S(2)}, u32[]{:S(2)}) collective-permute-start(bf16[64,640]{1,0:T(8,128)(2,1)S(1)} %collective-permute-done.6), channel_id=1, source_target_pairs={{0,8},{2,10},{8,16},{10,18},{16,24},{18,26},{24,28},{26,30},{28,20... | collective-permute-start | bytes 245768 | tf_op jit(solution)/shard_map/ppermute | solution.py:549
  34.3 4.4 %collective-permute-start.8 = (bf16[64,640]{1,0:T(8,128)(2,1)S(1)}, bf16[64,640]{1,0:T(8,128)(2,1)S(1)}, u32[]{:S(2)}, u32[]{:S(2)}) collective-permute-start(bf16[64,640]{1,0:T(8,128)(2,1)S(1)} %collective-permute-done.7), channel_id=1, source_target_pairs={{0,8},{2,10},{8,16},{10,18},{16,24},{18,26},{24,28},{26,30},{28,20... | collective-permute-start | bytes 245768 | tf_op jit(solution)/shard_map/ppermute | solution.py:549
  38.9 2.2 collective-permute-start.9
  41.9 354.3 %reduce-scatter.2.cloned.1.call-start = ((), (), s32[]{:S(2)}) async-start(), calls=%async_computation.1 | async-start | bytes 7311360 | tf_op jit(solution)/shard_map/reduce_scatter | solution.py:827
  43.6 8.3 %collective-permute-start = (bf16[3,128,576]{2,1,0:T(8,128)(2,1)S(1)}, bf16[3,128,576]{2,1,0:T(8,128)(2,1)S(1)}, u32[]{:S(2)}, u32[]{:S(2)}) collective-permute-start(bf16[3,128,576]{2,1,0:T(8,128)(2,1)S(1)} %copy.236), channel_id=1, source_target_pairs={{0,2},{2,0},{4,6},{6,4},{8,10},{10,8},{12,14},{14,12},{16,18},{18,... | collective-permute-start | bytes 1327112 | tf_op jit(solution)/shard_map/ppermute | solution.py:674
  62.5 19.0 %collective-permute-start.13 = (bf16[3,256,384]{2,1,0:T(8,128)(2,1)}, bf16[3,256,384]{2,1,0:T(8,128)(2,1)S(1)}, u32[]{:S(2)}, u32[]{:S(2)}) collective-permute-start(bf16[3,256,384]{2,1,0:T(8,128)(2,1)} %get-tuple-element.71.refs_2_), channel_id=1, source_target_pairs={{0,8},{2,10},{8,16},{10,18},{16,24},{18,26},{24,28},{26,30},{28,20... | collective-permute-start | bytes 1769480 | tf_op jit(solution)/shard_map/ppermute | solution.py:549
  63.1 23.3 %collective-permute-start.10 = (bf16[3,256,384]{2,1,0:T(8,128)(2,1)}, bf16[3,256,384]{2,1,0:T(8,128)(2,1)S(1)}, u32[]{:S(2)}, u32[]{:S(2)}) collective-permute-start(bf16[3,256,384]{2,1,0:T(8,128)(2,1)} %get-tuple-element.71.refs_2_), channel_id=1, source_target_pairs={{0,4},{2,6},{8,0},{10,2},{16,8},{18,10},{24,16},{26,18},{28,24},{3... | collective-permute-start | bytes 1769480 | tf_op jit(solution)/shard_map/ppermute | solution.py:552
  81.5 29.2 %collective-permute-start.14 = (bf16[3,256,384]{2,1,0:T(8,128)(2,1)S(1)}, bf16[3,256,384]{2,1,0:T(8,128)(2,1)S(1)}, u32[]{:S(2)}, u32[]{:S(2)}) collective-permute-start(bf16[3,256,384]{2,1,0:T(8,128)(2,1)S(1)} %collective-permute-done.13.refs_9_), channel_id=1, source_target_pairs={{0,8},{2,10},{8,16},{10,18},{16,24},{18,26},{24,28},{26,30},{28,20... | collective-permute-start | bytes 1769480 | tf_op jit(solution)/shard_map/ppermute | solution.py:549
  86.4 33.2 %collective-permute-start.11 = (bf16[3,256,384]{2,1,0:T(8,128)(2,1)S(1)}, bf16[3,256,384]{2,1,0:T(8,128)(2,1)}, u32[]{:S(2)}, u32[]{:S(2)}) collective-permute-start(bf16[3,256,384]{2,1,0:T(8,128)(2,1)S(1)} %collective-permute-done.10.refs_3_), channel_id=1, source_target_pairs={{0,4},{2,6},{8,0},{10,2},{16,8},{18,10},{24,16},{26,18},{28,24},{3... | collective-permute-start | bytes 1769480 | tf_op jit(solution)/shard_map/ppermute | solution.py:552
  110.7 23.8 %collective-permute-start.15 = (bf16[3,256,384]{2,1,0:T(8,128)(2,1)S(1)}, bf16[3,256,384]{2,1,0:T(8,128)(2,1)}, u32[]{:S(2)}, u32[]{:S(2)}) collective-permute-start(bf16[3,256,384]{2,1,0:T(8,128)(2,1)S(1)} %collective-permute-done.14.refs_8_), channel_id=1, source_target_pairs={{0,8},{2,10},{8,16},{10,18},{16,24},{18,26},{24,28},{26,30},{28,20... | collective-permute-start | bytes 1769480 | tf_op jit(solution)/shard_map/ppermute | solution.py:549
  119.6 18.4 %collective-permute-start.12 = (bf16[3,256,384]{2,1,0:T(8,128)(2,1)}, bf16[3,256,384]{2,1,0:T(8,128)(2,1)}, u32[]{:S(2)}, u32[]{:S(2)}) collective-permute-start(bf16[3,256,384]{2,1,0:T(8,128)(2,1)} %collective-permute-done.11.refs_4_), channel_id=1, source_target_pairs={{0,4},{2,6},{8,0},{10,2},{16,8},{18,10},{24,16},{26,18},{28,24},{3... | collective-permute-start | bytes 1769480 | tf_op jit(solution)/shard_map/ppermute | solution.py:552
  134.6 15.1 %collective-permute-start.16 = (bf16[3,256,384]{2,1,0:T(8,128)(2,1)}, bf16[3,256,384]{2,1,0:T(8,128)(2,1)}, u32[]{:S(2)}, u32[]{:S(2)}) collective-permute-start(bf16[3,256,384]{2,1,0:T(8,128)(2,1)} %collective-permute-done.15.refs_7_), channel_id=1, source_target_pairs={{0,8},{2,10},{8,16},{10,18},{16,24},{18,26},{24,28},{26,30},{28,20... | collective-permute-start | bytes 1769480 | tf_op jit(solution)/shard_map/ppermute | solution.py:549
  237.2 9.9 %collective-permute-start.21 = (bf16[2,256,384]{2,1,0:T(8,128)(2,1)}, bf16[2,256,384]{2,1,0:T(8,128)(2,1)S(1)}, u32[]{:S(2)}, u32[]{:S(2)}) collective-permute-start(bf16[2,256,384]{2,1,0:T(8,128)(2,1)} %get-tuple-element.78), channel_id=1, source_target_pairs={{0,8},{2,10},{8,16},{10,18},{16,24},{18,26},{24,28},{26,30},{28,20... | collective-permute-start | bytes 1179656 | tf_op jit(solution)/shard_map/ppermute | solution.py:584
  237.6 11.9 %collective-permute-start.25 = (bf16[2,256,384]{2,1,0:T(8,128)(2,1)}, bf16[2,256,384]{2,1,0:T(8,128)(2,1)}, u32[]{:S(2)}, u32[]{:S(2)}) collective-permute-start(bf16[2,256,384]{2,1,0:T(8,128)(2,1)} %get-tuple-element.82), channel_id=1, source_target_pairs={{0,4},{2,6},{8,0},{10,2},{16,8},{18,10},{24,16},{26,18},{28,24},{3... | collective-permute-start | bytes 1179656 | tf_op jit(solution)/shard_map/ppermute | solution.py:584
  248.9 9.2 %collective-permute-start.22 = (bf16[2,256,384]{2,1,0:T(8,128)(2,1)S(1)}, bf16[2,256,384]{2,1,0:T(8,128)(2,1)}, u32[]{:S(2)}, u32[]{:S(2)}) collective-permute-start(bf16[2,256,384]{2,1,0:T(8,128)(2,1)S(1)} %add_convert_fusion.4.refs_1_), channel_id=1, source_target_pairs={{0,8},{2,10},{8,16},{10,18},{16,24},{18,26},{24,28},{26,30},{28,20... | collective-permute-start | bytes 1179656 | tf_op jit(solution)/shard_map/ppermute | solution.py:584
  250.7 9.2 %collective-permute-start.26 = (bf16[2,256,384]{2,1,0:T(8,128)(2,1)S(1)}, bf16[2,256,384]{2,1,0:T(8,128)(2,1)}, u32[]{:S(2)}, u32[]{:S(2)}) collective-permute-start(bf16[2,256,384]{2,1,0:T(8,128)(2,1)S(1)} %add_convert_fusion.1.refs_2_), channel_id=1, source_target_pairs={{0,4},{2,6},{8,0},{10,2},{16,8},{18,10},{24,16},{26,18},{28,24},{3... | collective-permute-start | bytes 1179656 | tf_op jit(solution)/shard_map/ppermute | solution.py:584
  259.3 8.4 %collective-permute-start.23 = (bf16[2,256,384]{2,1,0:T(8,128)(2,1)S(1)}, bf16[2,256,384]{2,1,0:T(8,128)(2,1)S(1)}, u32[]{:S(2)}, u32[]{:S(2)}) collective-permute-start(bf16[2,256,384]{2,1,0:T(8,128)(2,1)S(1)} %add_convert_fusion.3.refs_1_), channel_id=1, source_target_pairs={{0,8},{2,10},{8,16},{10,18},{16,24},{18,26},{24,28},{26,30},{28,20... | collective-permute-start | bytes 1179656 | tf_op jit(solution)/shard_map/ppermute | solution.py:584
  261.1 8.4 %collective-permute-start.27 = (bf16[2,256,384]{2,1,0:T(8,128)(2,1)S(1)}, bf16[2,256,384]{2,1,0:T(8,128)(2,1)S(1)}, u32[]{:S(2)}, u32[]{:S(2)}) collective-permute-start(bf16[2,256,384]{2,1,0:T(8,128)(2,1)S(1)} %add_convert_fusion.refs_2_), channel_id=1, source_target_pairs={{0,4},{2,6},{8,0},{10,2},{16,8},{18,10},{24,16},{26,18},{28,24},{3... | collective-permute-start | bytes 1179656 | tf_op jit(solution)/shard_map/ppermute | solution.py:584
  277.6 17.7 %collective-permute-start.24 = (bf16[2,256,384]{2,1,0:T(8,128)(2,1)S(1)}, bf16[2,256,384]{2,1,0:T(8,128)(2,1)S(1)}, u32[]{:S(2)}, u32[]{:S(2)}) collective-permute-start(bf16[2,256,384]{2,1,0:T(8,128)(2,1)S(1)} %copy-done.25), channel_id=1, source_target_pairs={{0,8},{2,10},{8,16},{10,18},{16,24},{18,26},{24,28},{26,30},{28,20... | collective-permute-start | bytes 1179656 | tf_op jit(solution)/shard_map/ppermute | solution.py:584
  296.0 9.2 %collective-permute-start.28 = (bf16[1,256,384]{2,1,0:T(8,128)(2,1)}, bf16[1,256,384]{2,1,0:T(8,128)(2,1)S(1)}, u32[]{:S(2)}, u32[]{:S(2)}) collective-permute-start(bf16[1,256,384]{2,1,0:T(8,128)(2,1)} %get-tuple-element.98), channel_id=1, source_target_pairs={{0,8},{2,10},{8,16},{10,18},{16,24},{18,26},{24,28},{26,30},{28,20... | collective-permute-start | bytes 589832 | tf_op jit(solution)/shard_map/ppermute | solution.py:584
  297.1 6.8 %collective-permute-start.31 = (bf16[1,256,384]{2,1,0:T(8,128)(2,1)}, bf16[1,256,384]{2,1,0:T(8,128)(2,1)S(1)}, u32[]{:S(2)}, u32[]{:S(2)}) collective-permute-start(bf16[1,256,384]{2,1,0:T(8,128)(2,1)} %get-tuple-element.101), channel_id=1, source_target_pairs={{0,4},{2,6},{8,0},{10,2},{16,8},{18,10},{24,16},{26,18},{28,24},{3... | collective-permute-start | bytes 589832 | tf_op jit(solution)/shard_map/ppermute | solution.py:584
  304.0 12.5 %collective-permute-start.32 = (bf16[1,256,384]{2,1,0:T(8,128)(2,1)S(1)}, bf16[1,256,384]{2,1,0:T(8,128)(2,1)S(1)}, u32[]{:S(2)}, u32[]{:S(2)}) collective-permute-start(bf16[1,256,384]{2,1,0:T(8,128)(2,1)S(1)} %add_convert_fusion.7), channel_id=1, source_target_pairs={{0,4},{2,6},{8,0},{10,2},{16,8},{18,10},{24,16},{26,18},{28,24},{3... | collective-permute-start | bytes 589832 | tf_op jit(solution)/shard_map/ppermute | solution.py:584
  305.3 11.4 %collective-permute-start.29 = (bf16[1,256,384]{2,1,0:T(8,128)(2,1)S(1)}, bf16[1,256,384]{2,1,0:T(8,128)(2,1)S(1)}, u32[]{:S(2)}, u32[]{:S(2)}) collective-permute-start(bf16[1,256,384]{2,1,0:T(8,128)(2,1)S(1)} %add_convert_fusion.9), channel_id=1, source_target_pairs={{0,8},{2,10},{8,16},{10,18},{16,24},{18,26},{24,28},{26,30},{28,20... | collective-permute-start | bytes 589832 | tf_op jit(solution)/shard_map/ppermute | solution.py:584
  316.6 12.8 %collective-permute-start.33 = (bf16[1,256,384]{2,1,0:T(8,128)(2,1)S(1)}, bf16[1,256,384]{2,1,0:T(8,128)(2,1)S(1)}, u32[]{:S(2)}, u32[]{:S(2)}) collective-permute-start(bf16[1,256,384]{2,1,0:T(8,128)(2,1)S(1)} %add_convert_fusion.6), channel_id=1, source_target_pairs={{0,4},{2,6},{8,0},{10,2},{16,8},{18,10},{24,16},{26,18},{28,24},{3... | collective-permute-start | bytes 589832 | tf_op jit(solution)/shard_map/ppermute | solution.py:584
  316.7 20.8 %collective-permute-start.30 = (bf16[1,256,384]{2,1,0:T(8,128)(2,1)S(1)}, bf16[1,256,384]{2,1,0:T(8,128)(2,1)}, u32[]{:S(2)}, u32[]{:S(2)}) collective-permute-start(bf16[1,256,384]{2,1,0:T(8,128)(2,1)S(1)} %add_convert_fusion.8), channel_id=1, source_target_pairs={{0,8},{2,10},{8,16},{10,18},{16,24},{18,26},{24,28},{26,30},{28,20... | collective-permute-start | bytes 589832 | tf_op jit(solution)/shard_map/ppermute | solution.py:584
  330.2 11.2 %collective-permute-start.34 = (bf16[1,256,384]{2,1,0:T(8,128)(2,1)}, bf16[1,256,384]{2,1,0:T(8,128)(2,1)}, u32[]{:S(2)}, u32[]{:S(2)}) collective-permute-start(bf16[1,256,384]{2,1,0:T(8,128)(2,1)} %add_convert_fusion.5), channel_id=1, source_target_pairs={{0,4},{2,6},{8,0},{10,2},{16,8},{18,10},{24,16},{26,18},{28,24},{3... | collective-permute-start | bytes 589832 | tf_op jit(solution)/shard_map/ppermute | solution.py:584
  351.6 7.3 %collective-permute-start.36 = (bf16[8,64,640]{2,1,0:T(8,128)(2,1)}, bf16[8,64,640]{2,1,0:T(8,128)(2,1)}, u32[]{:S(2)}, u32[]{:S(2)}) collective-permute-start(bf16[8,64,640]{2,1,0:T(8,128)(2,1)} %get-tuple-element.113), channel_id=1, source_target_pairs={{0,2},{2,0},{4,6},{6,4},{8,10},{10,8},{12,14},{14,12},{16,18},{18,... | collective-permute-start | bytes 1966088 | tf_op jit(solution)/shard_map/ppermute | solution.py:805
  358.3 20.0 %collective-permute-start.20 = (f32[3,128,576]{1,2,0:T(8,128)}, f32[3,128,576]{1,2,0:T(8,128)}, u32[]{:S(2)}, u32[]{:S(2)}) collective-permute-start(f32[3,128,576]{1,2,0:T(8,128)} %copy.198), channel_id=1, source_target_pairs={{0,2},{2,0},{4,6},{6,4},{8,10},{10,8},{12,14},{14,12},{16,18},{18,... | collective-permute-start | bytes 2654216 | tf_op jit(solution)/shard_map/ppermute | solution.py:678
  360.6 4.4 %collective-permute-start.37 = (bf16[64,640]{1,0:T(8,128)(2,1)S(1)}, bf16[64,640]{1,0:T(8,128)(2,1)S(1)}, u32[]{:S(2)}, u32[]{:S(2)}) collective-permute-start(bf16[64,640]{1,0:T(8,128)(2,1)S(1)} %get-tuple-element.258), channel_id=1, source_target_pairs={{0,8},{2,10},{8,16},{10,18},{16,24},{18,26},{24,28},{26,30},{28,20... | collective-permute-start | bytes 245768 | tf_op jit(solution)/shard_map/ppermute | solution.py:584
  360.9 11.5 %collective-permute-start.41 = (bf16[64,640]{1,0:T(8,128)(2,1)}, bf16[64,640]{1,0:T(8,128)(2,1)}, u32[]{:S(2)}, u32[]{:S(2)}) collective-permute-start(bf16[64,640]{1,0:T(8,128)(2,1)} %get-tuple-element.259), channel_id=1, source_target_pairs={{0,4},{2,6},{8,0},{10,2},{16,8},{18,10},{24,16},{26,18},{28,24},{3... | collective-permute-start | bytes 245768 | tf_op jit(solution)/shard_map/ppermute | solution.py:584
  366.6 5.9 %collective-permute-start.38 = (bf16[64,640]{1,0:T(8,128)(2,1)}, bf16[64,640]{1,0:T(8,128)(2,1)}, u32[]{:S(2)}, u32[]{:S(2)}) collective-permute-start(bf16[64,640]{1,0:T(8,128)(2,1)} %fusion.10), channel_id=1, source_target_pairs={{0,8},{2,10},{8,16},{10,18},{16,24},{18,26},{24,28},{26,30},{28,20... | collective-permute-start | bytes 245768 | tf_op jit(solution)/shard_map/ppermute | solution.py:584
  372.4 19.3 %collective-permute-start.35 = (f32[3,128,576]{1,2,0:T(8,128)}, f32[3,128,576]{1,2,0:T(8,128)}, u32[]{:S(2)}, u32[]{:S(2)}) collective-permute-start(f32[3,128,576]{1,2,0:T(8,128)} %copy.215), channel_id=1, source_target_pairs={{0,2},{2,0},{4,6},{6,4},{8,10},{10,8},{12,14},{14,12},{16,18},{18,... | collective-permute-start | bytes 2654216 | tf_op jit(solution)/shard_map/ppermute | solution.py:678
  374.3 6.8 %collective-permute-start.39 = (bf16[64,640]{1,0:T(8,128)(2,1)}, bf16[64,640]{1,0:T(8,128)(2,1)S(1)}, u32[]{:S(2)}, u32[]{:S(2)}) collective-permute-start(bf16[64,640]{1,0:T(8,128)(2,1)} %get-tuple-element.256), channel_id=1, source_target_pairs={{0,8},{2,10},{8,16},{10,18},{16,24},{18,26},{24,28},{26,30},{28,20... | collective-permute-start | bytes 245768 | tf_op jit(solution)/shard_map/ppermute | solution.py:584
  376.2 5.3 %collective-permute-start.42 = (bf16[64,640]{1,0:T(8,128)(2,1)S(1)}, bf16[64,640]{1,0:T(8,128)(2,1)}, u32[]{:S(2)}, u32[]{:S(2)}) collective-permute-start(bf16[64,640]{1,0:T(8,128)(2,1)S(1)} %get-tuple-element.257), channel_id=1, source_target_pairs={{0,4},{2,6},{8,0},{10,2},{16,8},{18,10},{24,16},{26,18},{28,24},{3... | collective-permute-start | bytes 245768 | tf_op jit(solution)/shard_map/ppermute | solution.py:584
  382.6 4.5 %collective-permute-start.40 = (bf16[64,640]{1,0:T(8,128)(2,1)S(1)}, bf16[64,640]{1,0:T(8,128)(2,1)S(1)}, u32[]{:S(2)}, u32[]{:S(2)}) collective-permute-start(bf16[64,640]{1,0:T(8,128)(2,1)S(1)} %get-tuple-element.254), channel_id=1, source_target_pairs={{0,8},{2,10},{8,16},{10,18},{16,24},{18,26},{24,28},{26,30},{28,20... | collective-permute-start | bytes 245768 | tf_op jit(solution)/shard_map/ppermute | solution.py:584
  384.4 4.4 %collective-permute-start.43 = (bf16[64,640]{1,0:T(8,128)(2,1)S(1)}, bf16[64,640]{1,0:T(8,128)(2,1)S(1)}, u32[]{:S(2)}, u32[]{:S(2)}) collective-permute-start(bf16[64,640]{1,0:T(8,128)(2,1)S(1)} %get-tuple-element.255), channel_id=1, source_target_pairs={{0,4},{2,6},{8,0},{10,2},{16,8},{18,10},{24,16},{26,18},{28,24},{3... | collective-permute-start | bytes 245768 | tf_op jit(solution)/shard_map/ppermute | solution.py:584
  389.9 4.2 collective-permute-start.44
  398.9 4.3 %collective-permute-start.46 = (bf16[36,768]{1,0:T(8,128)(2,1)S(1)}, bf16[36,768]{1,0:T(8,128)(2,1)S(1)}, u32[]{:S(2)}, u32[]{:S(2)}) collective-permute-start(bf16[36,768]{1,0:T(8,128)(2,1)S(1)} %select_convert_fusion.1), channel_id=1, source_target_pairs={{0,1},{1,0},{2,3},{3,2},{4,5},{5,4},{6,7},{7,6},{8,9},{9,8},{10,11... | collective-permute-start | bytes 165896 | tf_op jit(solution)/shard_map/ppermute | solution.py:609
  400.9 5.5 %collective-permute-start.45 = (bf16[228,288]{1,0:T(8,128)(2,1)S(1)}, bf16[228,288]{1,0:T(8,128)(2,1)S(1)}, u32[]{:S(2)}, u32[]{:S(2)}) collective-permute-start(bf16[228,288]{1,0:T(8,128)(2,1)S(1)} %select_convert_fusion), channel_id=1, source_target_pairs={{0,1},{1,0},{2,3},{3,2},{4,5},{5,4},{6,7},{7,6},{8,9},{9,8},{10,11... | collective-permute-start | bytes 393992 | tf_op jit(solution)/shard_map/ppermute | solution.py:609
  (66 other events, 660.9 us)
Sparse Core Ops, SparseCore 0:
  42.0 75.6 all-gather.2
  276.7 96.5 reduce-scatter.1

commit v2 on v0

--- a/solution.py
+++ b/solution.py
@@ -617,12 +617,14 @@
     return total
 
 
-def ring_scatter(terms, flip):
+def ring_scatter(terms, flip, pin=()):
     chips = lax.axis_size("ctx") // 2
     steps = (chips // 2, (chips - 1) // 2)
     if flip:
         steps = steps[::-1]
     moving = [terms[steps[0]]().astype(bf16), terms[-steps[1] % chips]().astype(bf16)]
+    if pin:
+        moving = list(join(moving, *pin))
     trace = []
     for t in range(max(steps)):
         for way in range(2):
@@ -774,9 +776,6 @@
             axis=0,
         )
 
-    def later(part):
-        return lax.optimization_barrier((part, first_other))[0]
-
     x = take(tokens)
     cot = take(cotangent)
     order = lax.dynamic_slice_in_dim(pair_order, mine, seqs, 0)
@@ -807,7 +806,7 @@
     kv_all = ring_gather(kv, False, trace=kv_trace)
     outer = (turned_low[4], turned_low[5], turned_low[3], turned_low[6])
     if two_planes:
-        same = jnp.stack(ring_gather(later(second_part(*outer)), True, {1: [inward], 2: kv_trace[0], 3: kv_trace[1]}), axis=0)
+        same = jnp.stack(ring_gather(second_part(*outer), True, {2: [inward]}), axis=0)
         cross = lax.ppermute(same, "fsdp", planes)
     else:
         outer = [rows_gather(part) for part in outer]
@@ -965,7 +964,9 @@
             after=waits,
         )
         dkv_own, trace = ring_scatter(
-            [lambda k=k, dkv=dkv: dkv[k] for k in range(chunks)], first > 0
+            [lambda k=k, dkv=dkv: dkv[k] for k in range(chunks)],
+            first > 0,
+            traces[-1][-1] if traces else (),
         )
         traces.append(trace)
         dinput, dall, gain_one_grad = call(

time: 428 us -> 406 us (0.949)
  waiting for transfers between devices: 116 us -> 103 us
  local copies, waits for them, and re-layouts: 55.3 us -> 47.8 us
    ppermute x1, waiting for transfers between devices: 18.4 us -> 7.49 us  [body(): cross = lax.ppermute(same, 'fsdp', planes)]
    ppermute x11, waiting for transfers between devices: 35.4 us -> 26.5 us  [ring_gather(): ahead = lax.ppermute(ahead, 'ctx', ring_pairs(chips, 1))]
    unnamed x201 -> x202, local copies, waits for them, and re-layouts: 31.6 us -> 25 us
    ppermute x10, waiting for transfers between devices: 18.6 us -> 24.1 us  [ring_gather(): behind = lax.ppermute(behind, 'ctx', ring_pairs(chips, -1))]
    ppermute x11, starting transfers between devices: 7.81 us -> 13 us  [ring_gather(): ahead = lax.ppermute(ahead, 'ctx', ring_pairs(chips, 1))]
  transfers between devices with their start and end apart: 63 -> 63, of which waited for: 32 -> 30; matrix products, arithmetic and copies ran while one was open for 22% -> 22% of each run, Pallas kernels for 14% -> 17%
where the time goes in v2:
time: 406 us; the launch traced here: 400 us
  Pallas kernels  133 us (33%)
  waiting for transfers between devices  103 us (25%)
  starting transfers between devices  58.1 us (14%)
  local copies, waits for them, and re-layouts  47.8 us (12%)
  other arithmetic  41.4 us (10%)
  matrix products  13.4 us (3%)
    pallas_call x9, Pallas kernels, call(): pl.pallas_call(body_of, grid_spec=pltpu.PrefetchScalarGridSpec(num_scalar...  133 us
    ppermute x28, waiting for transfers between devices, ring_scatter(): got = lax.ppermute(moving[way], 'ctx', ring_pairs(chips, sign))  42.3 us
    ppermute x28, starting transfers between devices, ring_scatter(): got = lax.ppermute(moving[way], 'ctx', ring_pairs(chips, sign))  28.4 us
    ppermute x11, waiting for transfers between devices, ring_gather(): ahead = lax.ppermute(ahead, 'ctx', ring_pairs(chips, 1))  26.5 us
    unnamed x202, local copies, waits for them, and re-layouts  25 us
    ppermute x10, waiting for transfers between devices, ring_gather(): behind = lax.ppermute(behind, 'ctx', ring_pairs(chips, -1))  24.1 us
    convert_element_type x16, other arithmetic, ring_scatter(): got = plus(got, terms[sign * left % chips]()).astype(bf16)  13.5 us
    dot_general x4, matrix products, weight_grad(): lax.dot_general(left, right, (((0, 1), (0, 1)), ((), ())), preferred_elem...  13.4 us
  transfers between devices with their start and end apart: 63, of which 30 were waited for; matrix products, arithmetic and copies ran while one was open for 22% of the time, Pallas kernels for 17%

profile of v2, /device:TPU:0, one launch (start us, length us, event | category | flops | bytes accessed | tf_op | source)
XLA Modules:
  0.0 399.5 jit_solution(3258425814080130465)
XLA Ops:
  5.7 3.0 collective-permute-start.19
  8.8 2.0 collective-permute-start.1
  23.0 2.8 collective-permute-done.2
  27.9 2.4 collective-permute-done.3
  32.3 3.9 collective-permute-done.7
  37.1 3.6 collective-permute-done.8
  46.2 3.3 shard_map.485.refs_2_.refs_7_
  49.6 6.2 %shard_map.486 = (bf16[3,256,576]{2,1,0:T(8,128)(2,1)}, bf16[3,4,3,192,128]{4,3,2,1,0:T(8,128)(2,1)}, bf16[3,256,384]{2,1,0:T(8,128)(2,1)}) custom-call(bf16[3,256,576]{2,1,0:T(8,128)(2,1)} %pad_maximum_fusion.refs_0_.refs_1_, f32[1,576]{1,0:T(1,128)} %get-tuple-element.293.refs_1_, bf16[960,576]{1,0:T(8,128)(2,1)} %shard_map.485.refs_2_.refs_7_, ...), custom_call_target="tpu_custom_call" | custom-call | flops 7151699968 | bytes 6023424 | tf_op jit(solution)/shard_map/pallas_call | solution.py:536
  62.9 13.5 %collective-permute-done.22 = bf16[168,640]{1,0:T(8,128)(2,1)S(1)} collective-permute-done((bf16[168,640]{1,0:T(8,128)(2,1)}, bf16[168,640]{1,0:T(8,128)(2,1)S(1)}, u32[]{:S(2)}, u32[]{:S(2)}) %collective-permute-start.22) | collective-permute-done | bytes 215072 | tf_op jit(solution)/shard_map/ppermute | solution.py:603
  78.2 4.0 %collective-permute-done.23 = bf16[168,640]{1,0:T(8,128)(2,1)S(1)} collective-permute-done((bf16[168,640]{1,0:T(8,128)(2,1)S(1)}, bf16[168,640]{1,0:T(8,128)(2,1)S(1)}, u32[]{:S(2)}, u32[]{:S(2)}) %collective-permute-start.23) | collective-permute-done | bytes 215072 | tf_op jit(solution)/shard_map/ppermute | solution.py:603
  87.8 9.9 %collective-permute-done.14.refs_8_ = bf16[3,256,384]{2,1,0:T(8,128)(2,1)S(1)} collective-permute-done((bf16[3,256,384]{2,1,0:T(8,128)(2,1)S(1)}, bf16[3,256,384]{2,1,0:T(8,128)(2,1)S(1)}, u32[]{:S(2)}, u32[]{:S(2)}) %collective-permute-start.14) | collective-permute-done | bytes 589856 | tf_op jit(solution)/shard_map/ppermute | solution.py:600
  101.4 9.1 %collective-permute-done.15.refs_7_ = bf16[3,256,384]{2,1,0:T(8,128)(2,1)} collective-permute-done((bf16[3,256,384]{2,1,0:T(8,128)(2,1)S(1)}, bf16[3,256,384]{2,1,0:T(8,128)(2,1)}, u32[]{:S(2)}, u32[]{:S(2)}) %collective-permute-start.15) | collective-permute-done | bytes 589856 | tf_op jit(solution)/shard_map/ppermute | solution.py:600
  110.6 2.1 collective-permute-start.16
  116.2 7.5 %collective-permute-done.25.refs_6_ = bf16[8,168,640]{2,1,0:T(8,128)(2,1)} collective-permute-done((bf16[8,168,640]{2,1,0:T(8,128)(2,1)}, bf16[8,168,640]{2,1,0:T(8,128)(2,1)}, u32[]{:S(2)}, u32[]{:S(2)}) %collective-permute-start.25) | collective-permute-done | bytes 1720352 | tf_op jit(solution)/shard_map/ppermute | solution.py:810
  123.7 33.4 %shard_map.487 = (bf16[3,256,576]{2,1,0:T(8,128)(2,1)}, f32[3,4,3,192,128]{4,3,2,1,0:T(8,128)}) custom-call(s32[3,32]{1,0:T(4,128)} %copy-done.74, bf16[3,4,3,192,128]{4,3,2,1,0:T(8,128)(2,1)} %get-tuple-element.76.refs_1_, bf16[3,256,384]{2,1,0:T(8,128)(2,1)} %get-tuple-element.77.refs_2_, bf16[3,256,384]{2,1,0:T(8,128)(2,1)} %collective-permute-done.10.refs_3_, ...), custom_call_target="tpu_custom_call" | custom-call | flops 38065500160 | bytes 10911744 | tf_op jit(solution)/shard_map/pallas_call | solution.py:536
  158.4 25.9 %shard_map.489 = (f32[3,256,576]{2,1,0:T(8,128)}, bf16[3,256,576]{2,1,0:T(8,128)(2,1)}, bf16[3,256,1536]{2,1,0:T(8,128)(2,1)}, bf16[3,256,1536]{2,1,0:T(8,128)(2...) custom-call(s32[10]{0:T(128)} %pad_add_fusion.1.refs_0_, ...), custom_call_target="tpu_custom_call" | custom-call | flops 29991000064 | bytes 22815744 | tf_op jit(solution)/shard_map/pallas_call | solution.py:536
  184.4 29.8 %shard_map.490 = (bf16[2,256,576]{2,1,0:T(8,128)(2,1)}, bf16[2,256,384]{2,1,0:T(8,128)(2,1)}, bf16[2,256,384]{2,1,0:T(8,128)(2,1)}, bf16[2,256,384]{2,1,0:T(8,12...) custom-call(s32[3,32]{1,0:T(4,128)} %copy-done.74, ...), custom_call_target="tpu_custom_call" | custom-call | flops 39218999296 | bytes 16318464 | tf_op jit(solution)/shard_map/pallas_call | solution.py:536
  214.1 1.6 collective-permute-start.29
  216.2 3.6 bitcast_convert_fusion.2
  219.9 1.8 bitcast_convert_fusion.3.refs_1_
  221.7 2.3 copy.209.refs_2_
  224.0 2.0 collective-permute-done.29
  227.8 1.6 collective-permute-start.30
  231.3 3.5 bitcast_convert_fusion.1
  234.8 2.4 copy.210.refs_3_
  237.2 1.7 collective-permute-done.30
  244.6 4.5 %bitcast_convert_fusion.refs_4_ = bf16[576,1536]{1,0:T(8,128)(2,1)} fusion(bf16[3,256,1536]{2,1,0:T(8,128)(2,1)} %shard_map.494, bf16[3,128,576]{2,1,0:T(8,128)(2,1)S(1)} %copy-done.31, bf16[3,128,576]{2,1,0:T(8,128)(2,1)S(1)} %copy.238), kind=kOutput, calls=%fused_computation.2 | convolution fusion | flops 1361608704 | bytes 5013504 | tf_op jit(solution)/shard_map/dot_general | solution.py:669
  251.0 1.8 collective-permute-done.35.refs_6_.refs_3_
  253.5 7.8 %shard_map.495 = (bf16[8,168,640]{2,1,0:T(8,128)(2,1)}, bf16[8,168,640]{2,1,0:T(8,128)(2,1)}, bf16[8,168,640]{2,1,0:T(8,128)(2,1)}, bf16[8,168,640]{2,1,0:T(8,128)(2,1)}) custom-call(s32[10]{0:T(128)} %pad_add_fusion.1.refs_0_, bf16[576,576]{1,0:T(8,128)(2,1)} %bitcast_convert_fusion.3.refs_1_, bf16[1536,576]{1,0:T(8,128)(2,1)} %copy.209.refs_2_, ...), custom_call_target="tpu_custom_call" | custom-call | flops 8881949696 | bytes 12853248 | tf_op jit(solution)/shard_map/pallas_call | solution.py:536
  269.8 3.4 collective-permute-done.32.refs_2_
  273.3 2.0 convert_add_fusion.refs_3_
  275.3 3.1 add_convert_fusion
  278.9 16.8 %shard_map.496 = (bf16[1,256,576]{2,1,0:T(8,128)(2,1)}, bf16[1,256,384]{2,1,0:T(8,128)(2,1)}, bf16[1,256,384]{2,1,0:T(8,128)(2,1)}, bf16[1,256,384]{2,1,0:T(8,12...) custom-call(s32[3,32]{1,0:T(4,128)} %copy-done.74, ...), custom_call_target="tpu_custom_call" | custom-call | flops 19609499648 | bytes 14450688 | tf_op jit(solution)/shard_map/pallas_call | solution.py:536
  297.2 4.9 %shard_map.491 = (f32[2,256,576]{2,1,0:T(8,128)}, bf16[2,256,1024]{2,1,0:T(8,128)(2,1)}, f32[2,1,576]{2,1,0:T(1,128)}) custom-call(bf16[3,256,576]{2,1,0:T(8,128)(2,1)} %pad_maximum_fusion.refs_0_.refs_1_, f32[1,576]{1,0:T(1,128)} %get-tuple-element.293.refs_1_, bf16[2,256,576]{2,1,0:T(8,128)(2,1)} %get-tuple-element.84.refs_2_, ...), custom_call_target="tpu_custom_call" | custom-call | flops 4614000128 | bytes 8157952 | tf_op jit(solution)/shard_map/pallas_call | solution.py:536
  306.9 3.5 collective-permute-done.41
  312.7 3.8 collective-permute-done.42
  319.4 5.0 %collective-permute-done.43 = bf16[1,256,384]{2,1,0:T(8,128)(2,1)S(1)} collective-permute-done((bf16[1,256,384]{2,1,0:T(8,128)(2,1)S(1)}, bf16[1,256,384]{2,1,0:T(8,128)(2,1)S(1)}, u32[]{:S(2)}, u32[]{:S(2)}) %collective-permute-start.43) | collective-permute-done | bytes 196640 | tf_op jit(solution)/shard_map/ppermute | solution.py:635
  326.5 2.5 collective-permute-done.49
  330.6 2.5 collective-permute-done.44
  333.9 2.9 shard_map.499
  341.1 3.2 collective-permute-done.48
  345.7 2.2 fusion
  347.9 5.0 %shard_map.498 = (bf16[8,64,640]{2,1,0:T(8,128)(2,1)}, bf16[8,64,640]{2,1,0:T(8,128)(2,1)}) custom-call(s32[9]{0:T(128)} %pad_add_fusion.2.refs_0_, bf16[3,256,576]{2,1,0:T(8,128)(2,1)} %get-tuple-element.117.refs_1_, bf16[2,256,1024]{2,1,0:T(8,128)(2,1)} %get-tuple-element.118.refs_2_, bf16[1,256,1024]{2,1,0:T(8,128)(2,1)} %get-tuple-element.233.refs_3_, ...), custom_call_target="tpu_custom_call" | custom-call | flops 4037250048 | bytes 3772928 | tf_op jit(solution)/shard_map/pallas_call | solution.py:536
  355.9 2.4 copy.215
  361.0 2.0 collective-permute-start.62
  364.0 5.0 %collective-permute-done.60 = bf16[168,640]{1,0:T(8,128)(2,1)S(1)} collective-permute-done((bf16[168,640]{1,0:T(8,128)(2,1)S(1)}, bf16[168,640]{1,0:T(8,128)(2,1)S(1)}, u32[]{:S(2)}, u32[]{:S(2)}) %collective-permute-start.60) | collective-permute-done | bytes 215072 | tf_op jit(solution)/shard_map/ppermute | solution.py:635
  374.7 2.4 collective-permute-done.53
  384.4 1.9 collective-permute-start.58
  (409 shorter events, 125.8 us)
Async XLA Ops:
  5.7 35.8 %collective-permute-start.19 = (bf16[168,640]{1,0:T(8,128)(2,1)}, bf16[168,640]{1,0:T(8,128)(2,1)S(1)}, u32[]{:S(2)}, u32[]{:S(2)}) collective-permute-start(bf16[168,640]{1,0:T(8,128)(2,1)} %get-tuple-element.261), channel_id=1, source_target_pairs={{0,8},{2,10},{8,16},{10,18},{16,24},{18,26},{24,28},{26,30},{28,20... | collective-permute-start | bytes 645128 | tf_op jit(solution)/shard_map/ppermute | solution.py:600
  8.7 33.6 %collective-permute-start.18 = (bf16[168,640]{1,0:T(8,128)(2,1)}, bf16[168,640]{1,0:T(8,128)(2,1)S(1)}, u32[]{:S(2)}, u32[]{:S(2)}) collective-permute-start(bf16[168,640]{1,0:T(8,128)(2,1)} %get-tuple-element.261), channel_id=1, source_target_pairs={{0,4},{2,6},{8,0},{10,2},{16,8},{18,10},{24,16},{26,18},{28,24},{3... | collective-permute-start | bytes 645128 | tf_op jit(solution)/shard_map/ppermute | solution.py:603
  8.8 11.2 %collective-permute-start.1 = (bf16[62,288]{1,0:T(8,128)(2,1)S(1)}, bf16[62,288]{1,0:T(8,128)(2,1)}, u32[]{:S(2)}, u32[]{:S(2)}) collective-permute-start(bf16[62,288]{1,0:T(8,128)(2,1)S(1)} %pad_maximum_fusion.4), channel_id=1, source_target_pairs={{0,1},{1,0},{2,3},{3,2},{4,5},{5,4},{6,7},{7,6},{8,9},{9,8},{10,11... | collective-permute-start | bytes 107144 | tf_op jit(solution)/shard_map/ppermute | solution.py:647
  12.4 31.8 %collective-permute-start = (bf16[3,128,576]{2,1,0:T(8,128)(2,1)S(1)}, bf16[3,128,576]{2,1,0:T(8,128)(2,1)S(1)}, u32[]{:S(2)}, u32[]{:S(2)}) collective-permute-start(bf16[3,128,576]{2,1,0:T(8,128)(2,1)S(1)} %copy.237), channel_id=1, source_target_pairs={{0,2},{2,0},{4,6},{6,4},{8,10},{10,8},{12,14},{14,12},{16,18},{18,... | collective-permute-start | bytes 1327112 | tf_op jit(solution)/shard_map/ppermute | solution.py:725
  30.2 6.8 %collective-permute-start.4 = (bf16[64,640]{1,0:T(8,128)(2,1)S(1)}, bf16[64,640]{1,0:T(8,128)(2,1)S(1)}, u32[]{:S(2)}, u32[]{:S(2)}) collective-permute-start(bf16[64,640]{1,0:T(8,128)(2,1)S(1)} %collective-permute-done.3), channel_id=1, source_target_pairs={{0,4},{2,6},{8,0},{10,2},{16,8},{18,10},{24,16},{26,18},{28,24},{3... | collective-permute-start | bytes 245768 | tf_op jit(solution)/shard_map/ppermute | solution.py:603
  41.5 16.3 %collective-permute-start.20 = (bf16[168,640]{1,0:T(8,128)(2,1)S(1)}, bf16[168,640]{1,0:T(8,128)(2,1)S(1)}, u32[]{:S(2)}, u32[]{:S(2)}) collective-permute-start(bf16[168,640]{1,0:T(8,128)(2,1)S(1)} %collective-permute-done.19), channel_id=1, source_target_pairs={{0,8},{2,10},{8,16},{10,18},{16,24},{18,26},{24,28},{26,30},{28,20... | collective-permute-start | bytes 645128 | tf_op jit(solution)/shard_map/ppermute | solution.py:600
  42.4 15.5 %collective-permute-start.21 = (bf16[168,640]{1,0:T(8,128)(2,1)S(1)}, bf16[168,640]{1,0:T(8,128)(2,1)S(1)}, u32[]{:S(2)}, u32[]{:S(2)}) collective-permute-start(bf16[168,640]{1,0:T(8,128)(2,1)S(1)} %collective-permute-done.18), channel_id=1, source_target_pairs={{0,4},{2,6},{8,0},{10,2},{16,8},{18,10},{24,16},{26,18},{28,24},{3... | collective-permute-start | bytes 645128 | tf_op jit(solution)/shard_map/ppermute | solution.py:603
  55.8 28.5 %collective-permute-start.13 = (bf16[3,256,384]{2,1,0:T(8,128)(2,1)}, bf16[3,256,384]{2,1,0:T(8,128)(2,1)S(1)}, u32[]{:S(2)}, u32[]{:S(2)}) collective-permute-start(bf16[3,256,384]{2,1,0:T(8,128)(2,1)} %get-tuple-element.77.refs_2_), channel_id=1, source_target_pairs={{0,8},{2,10},{8,16},{10,18},{16,24},{18,26},{24,28},{26,30},{28,20... | collective-permute-start | bytes 1769480 | tf_op jit(solution)/shard_map/ppermute | solution.py:600
  56.7 30.5 %collective-permute-start.10 = (bf16[3,256,384]{2,1,0:T(8,128)(2,1)}, bf16[3,256,384]{2,1,0:T(8,128)(2,1)}, u32[]{:S(2)}, u32[]{:S(2)}) collective-permute-start(bf16[3,256,384]{2,1,0:T(8,128)(2,1)} %get-tuple-element.77.refs_2_), channel_id=1, source_target_pairs={{0,4},{2,6},{8,0},{10,2},{16,8},{18,10},{24,16},{26,18},{28,24},{3... | collective-permute-start | bytes 1769480 | tf_op jit(solution)/shard_map/ppermute | solution.py:603
  59.2 17.1 %collective-permute-start.22 = (bf16[168,640]{1,0:T(8,128)(2,1)}, bf16[168,640]{1,0:T(8,128)(2,1)S(1)}, u32[]{:S(2)}, u32[]{:S(2)}) collective-permute-start(bf16[168,640]{1,0:T(8,128)(2,1)} %get-tuple-element.79), channel_id=1, source_target_pairs={{0,4},{2,6},{8,0},{10,2},{16,8},{18,10},{24,16},{26,18},{28,24},{3... | collective-permute-start | bytes 645128 | tf_op jit(solution)/shard_map/ppermute | solution.py:603
  60.8 22.1 %collective-permute-start.24 = (bf16[168,640]{1,0:T(8,128)(2,1)}, bf16[168,640]{1,0:T(8,128)(2,1)S(1)}, u32[]{:S(2)}, u32[]{:S(2)}) collective-permute-start(bf16[168,640]{1,0:T(8,128)(2,1)} %get-tuple-element.80), channel_id=1, source_target_pairs={{0,8},{2,10},{8,16},{10,18},{16,24},{18,26},{24,28},{26,30},{28,20... | collective-permute-start | bytes 645128 | tf_op jit(solution)/shard_map/ppermute | solution.py:600
  76.3 5.9 %collective-permute-start.23 = (bf16[168,640]{1,0:T(8,128)(2,1)S(1)}, bf16[168,640]{1,0:T(8,128)(2,1)S(1)}, u32[]{:S(2)}, u32[]{:S(2)}) collective-permute-start(bf16[168,640]{1,0:T(8,128)(2,1)S(1)} %collective-permute-done.22), channel_id=1, source_target_pairs={{0,4},{2,6},{8,0},{10,2},{16,8},{18,10},{24,16},{26,18},{28,24},{3... | collective-permute-start | bytes 645128 | tf_op jit(solution)/shard_map/ppermute | solution.py:603
  84.3 13.4 %collective-permute-start.14 = (bf16[3,256,384]{2,1,0:T(8,128)(2,1)S(1)}, bf16[3,256,384]{2,1,0:T(8,128)(2,1)S(1)}, u32[]{:S(2)}, u32[]{:S(2)}) collective-permute-start(bf16[3,256,384]{2,1,0:T(8,128)(2,1)S(1)} %collective-permute-done.13.refs_9_), channel_id=1, source_target_pairs={{0,8},{2,10},{8,16},{10,18},{16,24},{18,26},{24,28},{26,30},{28,20... | collective-permute-start | bytes 1769480 | tf_op jit(solution)/shard_map/ppermute | solution.py:600
  86.7 37.0 %collective-permute-start.25 = (bf16[8,168,640]{2,1,0:T(8,128)(2,1)}, bf16[8,168,640]{2,1,0:T(8,128)(2,1)}, u32[]{:S(2)}, u32[]{:S(2)}) collective-permute-start(bf16[8,168,640]{2,1,0:T(8,128)(2,1)} %bitcast_dynamic-update-slice_fusion.refs_5_), channel_id=1, source_target_pairs={{0,1},{1,0},{2,3},{3,2},{4,5},{5,4},{6,7},{7,6},{8,9},{9,8},{10,11... | collective-permute-start | bytes 5160968 | tf_op jit(solution)/shard_map/ppermute | solution.py:810
  87.2 13.6 %collective-permute-start.11 = (bf16[3,256,384]{2,1,0:T(8,128)(2,1)}, bf16[3,256,384]{2,1,0:T(8,128)(2,1)S(1)}, u32[]{:S(2)}, u32[]{:S(2)}) collective-permute-start(bf16[3,256,384]{2,1,0:T(8,128)(2,1)} %collective-permute-done.10.refs_3_), channel_id=1, source_target_pairs={{0,4},{2,6},{8,0},{10,2},{16,8},{18,10},{24,16},{26,18},{28,24},{3... | collective-permute-start | bytes 1769480 | tf_op jit(solution)/shard_map/ppermute | solution.py:603
  97.7 12.8 %collective-permute-start.15 = (bf16[3,256,384]{2,1,0:T(8,128)(2,1)S(1)}, bf16[3,256,384]{2,1,0:T(8,128)(2,1)}, u32[]{:S(2)}, u32[]{:S(2)}) collective-permute-start(bf16[3,256,384]{2,1,0:T(8,128)(2,1)S(1)} %collective-permute-done.14.refs_8_), channel_id=1, source_target_pairs={{0,8},{2,10},{8,16},{10,18},{16,24},{18,26},{24,28},{26,30},{28,20... | collective-permute-start | bytes 1769480 | tf_op jit(solution)/shard_map/ppermute | solution.py:600
  100.8 22.9 %collective-permute-start.12 = (bf16[3,256,384]{2,1,0:T(8,128)(2,1)S(1)}, bf16[3,256,384]{2,1,0:T(8,128)(2,1)}, u32[]{:S(2)}, u32[]{:S(2)}) collective-permute-start(bf16[3,256,384]{2,1,0:T(8,128)(2,1)S(1)} %collective-permute-done.11.refs_4_), channel_id=1, source_target_pairs={{0,4},{2,6},{8,0},{10,2},{16,8},{18,10},{24,16},{26,18},{28,24},{3... | collective-permute-start | bytes 1769480 | tf_op jit(solution)/shard_map/ppermute | solution.py:603
  110.6 13.1 %collective-permute-start.16 = (bf16[3,256,384]{2,1,0:T(8,128)(2,1)}, bf16[3,256,384]{2,1,0:T(8,128)(2,1)}, u32[]{:S(2)}, u32[]{:S(2)}) collective-permute-start(bf16[3,256,384]{2,1,0:T(8,128)(2,1)} %collective-permute-done.15.refs_7_), channel_id=1, source_target_pairs={{0,8},{2,10},{8,16},{10,18},{16,24},{18,26},{24,28},{26,30},{28,20... | collective-permute-start | bytes 1769480 | tf_op jit(solution)/shard_map/ppermute | solution.py:600
  116.0 41.2 %collective-permute-start.26 = (bf16[8,168,640]{2,1,0:T(8,128)(2,1)S(1)}, bf16[8,168,640]{2,1,0:T(8,128)(2,1)S(1)}, u32[]{:S(2)}, u32[]{:S(2)}) collective-permute-start(bf16[8,168,640]{2,1,0:T(8,128)(2,1)S(1)} %copy-done.65), channel_id=1, source_target_pairs={{0,2},{2,0},{4,6},{6,4},{8,10},{10,8},{12,14},{14,12},{16,18},{18,... | collective-permute-start | bytes 5160968 | tf_op jit(solution)/shard_map/ppermute | solution.py:822
  123.7 33.5 %collective-permute-start.27 = (bf16[8,168,640]{2,1,0:T(8,128)(2,1)}, bf16[8,168,640]{2,1,0:T(8,128)(2,1)}, u32[]{:S(2)}, u32[]{:S(2)}) collective-permute-start(bf16[8,168,640]{2,1,0:T(8,128)(2,1)} %collective-permute-done.25.refs_6_), channel_id=1, source_target_pairs={{0,2},{2,0},{4,6},{6,4},{8,10},{10,8},{12,14},{14,12},{16,18},{18,... | collective-permute-start | bytes 5160968 | tf_op jit(solution)/shard_map/ppermute | solution.py:822
  214.1 11.8 %collective-permute-start.29 = (bf16[2,256,384]{2,1,0:T(8,128)(2,1)}, bf16[2,256,384]{2,1,0:T(8,128)(2,1)S(1)}, u32[]{:S(2)}, u32[]{:S(2)}) collective-permute-start(bf16[2,256,384]{2,1,0:T(8,128)(2,1)} %get-tuple-element.86), channel_id=1, source_target_pairs={{0,8},{2,10},{8,16},{10,18},{16,24},{18,26},{24,28},{26,30},{28,20... | collective-permute-start | bytes 1179656 | tf_op jit(solution)/shard_map/ppermute | solution.py:635
  215.8 13.7 %collective-permute-start.33 = (bf16[2,256,384]{2,1,0:T(8,128)(2,1)}, bf16[2,256,384]{2,1,0:T(8,128)(2,1)}, u32[]{:S(2)}, u32[]{:S(2)}) collective-permute-start(bf16[2,256,384]{2,1,0:T(8,128)(2,1)} %get-tuple-element.90), channel_id=1, source_target_pairs={{0,4},{2,6},{8,0},{10,2},{16,8},{18,10},{24,16},{26,18},{28,24},{3... | collective-permute-start | bytes 1179656 | tf_op jit(solution)/shard_map/ppermute | solution.py:635
  227.8 11.0 %collective-permute-start.30 = (bf16[2,256,384]{2,1,0:T(8,128)(2,1)S(1)}, bf16[2,256,384]{2,1,0:T(8,128)(2,1)}, u32[]{:S(2)}, u32[]{:S(2)}) collective-permute-start(bf16[2,256,384]{2,1,0:T(8,128)(2,1)S(1)} %add_convert_fusion.5.refs_1_), channel_id=1, source_target_pairs={{0,8},{2,10},{8,16},{10,18},{16,24},{18,26},{24,28},{26,30},{28,20... | collective-permute-start | bytes 1179656 | tf_op jit(solution)/shard_map/ppermute | solution.py:635
  230.6 11.1 %collective-permute-start.34 = (bf16[2,256,384]{2,1,0:T(8,128)(2,1)S(1)}, bf16[2,256,384]{2,1,0:T(8,128)(2,1)}, u32[]{:S(2)}, u32[]{:S(2)}) collective-permute-start(bf16[2,256,384]{2,1,0:T(8,128)(2,1)S(1)} %add_convert_fusion.2.refs_2_), channel_id=1, source_target_pairs={{0,4},{2,6},{8,0},{10,2},{16,8},{18,10},{24,16},{26,18},{28,24},{3... | collective-permute-start | bytes 1179656 | tf_op jit(solution)/shard_map/ppermute | solution.py:635
  240.1 10.0 %collective-permute-start.31 = (bf16[2,256,384]{2,1,0:T(8,128)(2,1)S(1)}, bf16[2,256,384]{2,1,0:T(8,128)(2,1)S(1)}, u32[]{:S(2)}, u32[]{:S(2)}) collective-permute-start(bf16[2,256,384]{2,1,0:T(8,128)(2,1)S(1)} %add_convert_fusion.4.refs_1_), channel_id=1, source_target_pairs={{0,8},{2,10},{8,16},{10,18},{16,24},{18,26},{24,28},{26,30},{28,20... | collective-permute-start | bytes 1179656 | tf_op jit(solution)/shard_map/ppermute | solution.py:635
  242.8 10.0 %collective-permute-start.35 = (bf16[2,256,384]{2,1,0:T(8,128)(2,1)S(1)}, bf16[2,256,384]{2,1,0:T(8,128)(2,1)S(1)}, u32[]{:S(2)}, u32[]{:S(2)}) collective-permute-start(bf16[2,256,384]{2,1,0:T(8,128)(2,1)S(1)} %add_convert_fusion.1.refs_2_), channel_id=1, source_target_pairs={{0,4},{2,6},{8,0},{10,2},{16,8},{18,10},{24,16},{26,18},{28,24},{3... | collective-permute-start | bytes 1179656 | tf_op jit(solution)/shard_map/ppermute | solution.py:635
  261.3 14.0 %collective-permute-start.37 = (bf16[8,168,640]{2,1,0:T(8,128)(2,1)}, bf16[8,168,640]{2,1,0:T(8,128)(2,1)}, u32[]{:S(2)}, u32[]{:S(2)}) collective-permute-start(bf16[8,168,640]{2,1,0:T(8,128)(2,1)} %get-tuple-element.103), channel_id=1, source_target_pairs={{0,2},{2,0},{4,6},{6,4},{8,10},{10,8},{12,14},{14,12},{16,18},{18,... | collective-permute-start | bytes 5160968 | tf_op jit(solution)/shard_map/ppermute | solution.py:910
  261.3 17.5 %collective-permute-start.36 = (bf16[8,168,640]{2,1,0:T(8,128)(2,1)}, bf16[8,168,640]{2,1,0:T(8,128)(2,1)}, u32[]{:S(2)}, u32[]{:S(2)}) collective-permute-start(bf16[8,168,640]{2,1,0:T(8,128)(2,1)} %get-tuple-element.102), channel_id=1, source_target_pairs={{0,2},{2,0},{4,6},{6,4},{8,10},{10,8},{12,14},{14,12},{16,18},{18,... | collective-permute-start | bytes 5160968 | tf_op jit(solution)/shard_map/ppermute | solution.py:910
  261.8 11.4 %collective-permute-start.32 = (bf16[2,256,384]{2,1,0:T(8,128)(2,1)}, bf16[2,256,384]{2,1,0:T(8,128)(2,1)}, u32[]{:S(2)}, u32[]{:S(2)}) collective-permute-start(bf16[2,256,384]{2,1,0:T(8,128)(2,1)} %add_convert_fusion.3.refs_5_), channel_id=1, source_target_pairs={{0,8},{2,10},{8,16},{10,18},{16,24},{18,26},{24,28},{26,30},{28,20... | collective-permute-start | bytes 1179656 | tf_op jit(solution)/shard_map/ppermute | solution.py:635
  269.8 83.3 %collective-permute-start.28 = (f32[3,128,576]{1,2,0:T(8,128)}, f32[3,128,576]{1,2,0:T(8,128)}, u32[]{:S(2)}, u32[]{:S(2)}) collective-permute-start(f32[3,128,576]{1,2,0:T(8,128)} %copy.199), channel_id=1, source_target_pairs={{0,2},{2,0},{4,6},{6,4},{8,10},{10,8},{12,14},{14,12},{16,18},{18,... | collective-permute-start | bytes 2654216 | tf_op jit(solution)/shard_map/ppermute | solution.py:729
  278.4 38.9 %collective-permute-start.45 = (bf16[8,168,640]{2,1,0:T(8,128)(2,1)}, bf16[8,168,640]{2,1,0:T(8,128)(2,1)S(1)}, u32[]{:S(2)}, u32[]{:S(2)}) collective-permute-start(bf16[8,168,640]{2,1,0:T(8,128)(2,1)} %add_convert_fusion), channel_id=1, source_target_pairs={{0,1},{1,0},{2,3},{3,2},{4,5},{5,4},{6,7},{7,6},{8,9},{9,8},{10,11... | collective-permute-start | bytes 5160968 | tf_op jit(solution)/shard_map/ppermute | solution.py:912
  295.7 9.6 %collective-permute-start.38 = (bf16[1,256,384]{2,1,0:T(8,128)(2,1)}, bf16[1,256,384]{2,1,0:T(8,128)(2,1)S(1)}, u32[]{:S(2)}, u32[]{:S(2)}) collective-permute-start(bf16[1,256,384]{2,1,0:T(8,128)(2,1)} %get-tuple-element.108), channel_id=1, source_target_pairs={{0,8},{2,10},{8,16},{10,18},{16,24},{18,26},{24,28},{26,30},{28,20... | collective-permute-start | bytes 589832 | tf_op jit(solution)/shard_map/ppermute | solution.py:635
  304.4 6.0 %collective-permute-start.41 = (bf16[1,256,384]{2,1,0:T(8,128)(2,1)S(1)}, bf16[1,256,384]{2,1,0:T(8,128)(2,1)S(1)}, u32[]{:S(2)}, u32[]{:S(2)}) collective-permute-start(bf16[1,256,384]{2,1,0:T(8,128)(2,1)S(1)} %copy-done.44), channel_id=1, source_target_pairs={{0,4},{2,6},{8,0},{10,2},{16,8},{18,10},{24,16},{26,18},{28,24},{3... | collective-permute-start | bytes 589832 | tf_op jit(solution)/shard_map/ppermute | solution.py:635
  310.5 6.0 %collective-permute-start.42 = (bf16[1,256,384]{2,1,0:T(8,128)(2,1)S(1)}, bf16[1,256,384]{2,1,0:T(8,128)(2,1)S(1)}, u32[]{:S(2)}, u32[]{:S(2)}) collective-permute-start(bf16[1,256,384]{2,1,0:T(8,128)(2,1)S(1)} %add_convert_fusion.10), channel_id=1, source_target_pairs={{0,4},{2,6},{8,0},{10,2},{16,8},{18,10},{24,16},{26,18},{28,24},{3... | collective-permute-start | bytes 589832 | tf_op jit(solution)/shard_map/ppermute | solution.py:635
  311.1 19.5 %collective-permute-start.40 = (bf16[1,256,384]{2,1,0:T(8,128)(2,1)S(1)}, bf16[1,256,384]{2,1,0:T(8,128)(2,1)S(1)}, u32[]{:S(2)}, u32[]{:S(2)}) collective-permute-start(bf16[1,256,384]{2,1,0:T(8,128)(2,1)S(1)} %add_convert_fusion.11), channel_id=1, source_target_pairs={{0,8},{2,10},{8,16},{10,18},{16,24},{18,26},{24,28},{26,30},{28,20... | collective-permute-start | bytes 589832 | tf_op jit(solution)/shard_map/ppermute | solution.py:635
  316.5 7.8 %collective-permute-start.43 = (bf16[1,256,384]{2,1,0:T(8,128)(2,1)S(1)}, bf16[1,256,384]{2,1,0:T(8,128)(2,1)S(1)}, u32[]{:S(2)}, u32[]{:S(2)}) collective-permute-start(bf16[1,256,384]{2,1,0:T(8,128)(2,1)S(1)} %add_convert_fusion.9), channel_id=1, source_target_pairs={{0,4},{2,6},{8,0},{10,2},{16,8},{18,10},{24,16},{26,18},{28,24},{3... | collective-permute-start | bytes 589832 | tf_op jit(solution)/shard_map/ppermute | solution.py:635
  318.9 10.1 %collective-permute-start.49 = (bf16[168,640]{1,0:T(8,128)(2,1)S(1)}, bf16[168,640]{1,0:T(8,128)(2,1)S(1)}, u32[]{:S(2)}, u32[]{:S(2)}) collective-permute-start(bf16[168,640]{1,0:T(8,128)(2,1)S(1)} %get-tuple-element.268), channel_id=1, source_target_pairs={{0,4},{2,6},{8,0},{10,2},{16,8},{18,10},{24,16},{26,18},{28,24},{3... | collective-permute-start | bytes 645128 | tf_op jit(solution)/shard_map/ppermute | solution.py:635
  324.4 8.7 %collective-permute-start.44 = (bf16[1,256,384]{2,1,0:T(8,128)(2,1)S(1)}, bf16[1,256,384]{2,1,0:T(8,128)(2,1)S(1)}, u32[]{:S(2)}, u32[]{:S(2)}) collective-permute-start(bf16[1,256,384]{2,1,0:T(8,128)(2,1)S(1)} %add_convert_fusion.8), channel_id=1, source_target_pairs={{0,4},{2,6},{8,0},{10,2},{16,8},{18,10},{24,16},{26,18},{28,24},{3... | collective-permute-start | bytes 589832 | tf_op jit(solution)/shard_map/ppermute | solution.py:635
  324.9 11.9 %collective-permute-start.47 = (bf16[168,640]{1,0:T(8,128)(2,1)S(1)}, bf16[168,640]{1,0:T(8,128)(2,1)}, u32[]{:S(2)}, u32[]{:S(2)}) collective-permute-start(bf16[168,640]{1,0:T(8,128)(2,1)S(1)} %get-tuple-element.269), channel_id=1, source_target_pairs={{0,8},{2,10},{8,16},{10,18},{16,24},{18,26},{24,28},{26,30},{28,20... | collective-permute-start | bytes 645128 | tf_op jit(solution)/shard_map/ppermute | solution.py:635
  330.1 6.7 %collective-permute-start.50 = (bf16[168,640]{1,0:T(8,128)(2,1)S(1)}, bf16[168,640]{1,0:T(8,128)(2,1)}, u32[]{:S(2)}, u32[]{:S(2)}) collective-permute-start(bf16[168,640]{1,0:T(8,128)(2,1)S(1)} %fusion.3), channel_id=1, source_target_pairs={{0,4},{2,6},{8,0},{10,2},{16,8},{18,10},{24,16},{26,18},{28,24},{3... | collective-permute-start | bytes 645128 | tf_op jit(solution)/shard_map/ppermute | solution.py:635
  338.4 5.9 %collective-permute-start.48 = (bf16[168,640]{1,0:T(8,128)(2,1)S(1)}, bf16[168,640]{1,0:T(8,128)(2,1)S(1)}, u32[]{:S(2)}, u32[]{:S(2)}) collective-permute-start(bf16[168,640]{1,0:T(8,128)(2,1)S(1)} %get-tuple-element.267), channel_id=1, source_target_pairs={{0,8},{2,10},{8,16},{10,18},{16,24},{18,26},{24,28},{26,30},{28,20... | collective-permute-start | bytes 645128 | tf_op jit(solution)/shard_map/ppermute | solution.py:635
  352.9 10.0 %collective-permute-start.51 = (bf16[8,64,640]{2,1,0:T(8,128)(2,1)}, bf16[8,64,640]{2,1,0:T(8,128)(2,1)}, u32[]{:S(2)}, u32[]{:S(2)}) collective-permute-start(bf16[8,64,640]{2,1,0:T(8,128)(2,1)} %get-tuple-element.125), channel_id=1, source_target_pairs={{0,2},{2,0},{4,6},{6,4},{8,10},{10,8},{12,14},{14,12},{16,18},{18,... | collective-permute-start | bytes 1966088 | tf_op jit(solution)/shard_map/ppermute | solution.py:883
  359.6 34.5 %collective-permute-start.46 = (f32[3,128,576]{1,2,0:T(8,128)}, f32[3,128,576]{1,2,0:T(8,128)}, u32[]{:S(2)}, u32[]{:S(2)}) collective-permute-start(f32[3,128,576]{1,2,0:T(8,128)} %copy.216), channel_id=1, source_target_pairs={{0,2},{2,0},{4,6},{6,4},{8,10},{10,8},{12,14},{14,12},{16,18},{18,... | collective-permute-start | bytes 2654216 | tf_op jit(solution)/shard_map/ppermute | solution.py:729
  360.9 8.1 %collective-permute-start.60 = (bf16[168,640]{1,0:T(8,128)(2,1)S(1)}, bf16[168,640]{1,0:T(8,128)(2,1)S(1)}, u32[]{:S(2)}, u32[]{:S(2)}) collective-permute-start(bf16[168,640]{1,0:T(8,128)(2,1)S(1)} %copy-done.42), channel_id=1, source_target_pairs={{0,8},{2,10},{8,16},{10,18},{16,24},{18,26},{24,28},{26,30},{28,20... | collective-permute-start | bytes 645128 | tf_op jit(solution)/shard_map/ppermute | solution.py:635
  361.0 8.0 %collective-permute-start.62 = (bf16[168,640]{1,0:T(8,128)(2,1)S(1)}, bf16[168,640]{1,0:T(8,128)(2,1)S(1)}, u32[]{:S(2)}, u32[]{:S(2)}) collective-permute-start(bf16[168,640]{1,0:T(8,128)(2,1)S(1)} %copy-done.41), channel_id=1, source_target_pairs={{0,4},{2,6},{8,0},{10,2},{16,8},{18,10},{24,16},{26,18},{28,24},{3... | collective-permute-start | bytes 645128 | tf_op jit(solution)/shard_map/ppermute | solution.py:635
  363.9 7.7 %collective-permute-start.52 = (bf16[64,640]{1,0:T(8,128)(2,1)S(1)}, bf16[64,640]{1,0:T(8,128)(2,1)S(1)}, u32[]{:S(2)}, u32[]{:S(2)}) collective-permute-start(bf16[64,640]{1,0:T(8,128)(2,1)S(1)} %get-tuple-element.278), channel_id=1, source_target_pairs={{0,8},{2,10},{8,16},{10,18},{16,24},{18,26},{24,28},{26,30},{28,20... | collective-permute-start | bytes 245768 | tf_op jit(solution)/shard_map/ppermute | solution.py:635
  384.2 7.5 %collective-permute-start.55 = (bf16[64,640]{1,0:T(8,128)(2,1)S(1)}, bf16[64,640]{1,0:T(8,128)(2,1)S(1)}, u32[]{:S(2)}, u32[]{:S(2)}) collective-permute-start(bf16[64,640]{1,0:T(8,128)(2,1)S(1)} %get-tuple-element.274), channel_id=1, source_target_pairs={{0,8},{2,10},{8,16},{10,18},{16,24},{18,26},{24,28},{26,30},{28,20... | collective-permute-start | bytes 245768 | tf_op jit(solution)/shard_map/ppermute | solution.py:635
  384.4 7.3 %collective-permute-start.58 = (bf16[64,640]{1,0:T(8,128)(2,1)S(1)}, bf16[64,640]{1,0:T(8,128)(2,1)S(1)}, u32[]{:S(2)}, u32[]{:S(2)}) collective-permute-start(bf16[64,640]{1,0:T(8,128)(2,1)S(1)} %get-tuple-element.275), channel_id=1, source_target_pairs={{0,4},{2,6},{8,0},{10,2},{16,8},{18,10},{24,16},{26,18},{28,24},{3... | collective-permute-start | bytes 245768 | tf_op jit(solution)/shard_map/ppermute | solution.py:635
  (101 other events, 817.8 us)

commit v3 on v2

--- a/solution.py
+++ b/solution.py
@@ -588,26 +588,26 @@
     ]
 
 
-def ring_gather(mine, flip, pins=None, trace=None):
+def ring_gather(mine, flip, pins=None, trace=None, state=None, until=None):
     chips = lax.axis_size("ctx") // 2
     steps = (chips // 2, (chips - 1) // 2)
     if flip:
         steps = steps[::-1]
-    result = [mine] * chips
-    ahead = behind = mine
-    for t in range(1, max(steps) + 1):
+    begin, ahead, behind, result = state or (0, mine, mine, [mine] * chips)
+    result = list(result)
+    for t in range(begin + 1, (until or max(steps)) + 1):
+        if pins and t - 1 in pins and t - 1 <= min(steps):
+            ahead, behind = join([ahead, behind], *pins[t - 1])
+            result[-(t - 1) % chips], result[t - 1] = ahead, behind
         if t <= steps[0]:
             ahead = lax.ppermute(ahead, "ctx", ring_pairs(chips, 1))
             result[-t % chips] = ahead
         if t <= steps[1]:
             behind = lax.ppermute(behind, "ctx", ring_pairs(chips, -1))
             result[t] = behind
-        if pins and t in pins and t <= min(steps):
-            ahead, behind = join([ahead, behind], *pins[t])
-            result[-t % chips], result[t] = ahead, behind
         if trace is not None:
             trace.append([ahead, behind])
-    return result
+    return (until, ahead, behind, result) if until else result
 
 
 def plus(*terms):
@@ -746,8 +746,8 @@
     q_cols, kv_cols = QUERY_WIDTH // ctx, KEY_WIDTH // ctx
     o_cols, f_cols = MODEL_WIDTH // ctx, FF // ctx
 
-    def both_packs(pack, flip):
-        stack = jnp.stack(ring_gather(pack, flip), axis=0)
+    def both_packs(pack, flip, pins):
+        stack = jnp.stack(ring_gather(pack, flip, pins), axis=0)
         return stack, lax.ppermute(stack, "ctx", partners)
 
     first_part = rows_gather(jnp.concatenate(turned_low[:3] + [norm_gains.astype(bf16).T], axis=0))
@@ -755,15 +755,6 @@
     first_part = jnp.pad(first_part, ((0, -first_used % 16), (0, 0)))
     gains = first_part[q_cols + 2 * kv_cols : first_used].astype(f32)
     gain_one, gain_two = gains[0:1], gains[1:2]
-    first_own, first_other = both_packs(widen(first_part), False)
-    (inward,) = call(
-        functools.partial(unpack_first_kernel, q_cols, kv_cols),
-        1,
-        [(whole, first_own), (whole, first_other)],
-        [(whole, (KV_PACKED + QUERY_WIDTH, MODEL_WIDTH), bf16)],
-        scalars=(where,),
-        us=3.3,
-    )
     half = MODEL_WIDTH // 2
 
     def second_part(gate, up, output, down):
@@ -776,6 +767,32 @@
             axis=0,
         )
 
+    outer = (turned_low[4], turned_low[5], turned_low[3], turned_low[6])
+    second_trace = []
+    if two_planes:
+        part = join([second_part(*outer)], first_part)[0]
+        started = [ring_gather(part, True, trace=second_trace, until=2)]
+    else:
+        outer = [rows_gather(part) for part in outer]
+        started = [
+            ring_gather(
+                second_part(*[jnp.split(part, 2, axis=1)[side] for part in outer]),
+                True,
+                trace=second_trace,
+                until=2,
+            )
+            for side in range(2)
+        ]
+    first_own, first_other = both_packs(widen(first_part), False, {2: second_trace[0]})
+    (inward,) = call(
+        functools.partial(unpack_first_kernel, q_cols, kv_cols),
+        1,
+        [(whole, first_own), (whole, first_other)],
+        [(whole, (KV_PACKED + QUERY_WIDTH, MODEL_WIDTH), bf16)],
+        scalars=(where,),
+        us=3.3,
+        after=second_trace[0],
+    )
     x = take(tokens)
     cot = take(cotangent)
     order = lax.dynamic_slice_in_dim(pair_order, mine, seqs, 0)
@@ -799,28 +816,24 @@
         [(one, x), (whole, gain_one), (whole, inward), (one, cosine), (one, sine)],
         [(one, wide, bf16), (one, heads, bf16), (one, (seqs, rows, KV_PACKED), bf16)],
         us=6.2,
+        after=second_trace[1],
     )
     load = length / 2048
     tile_rows = (KV_HEADS, GROUP * blk, PACK)
     kv_trace = []
     kv_all = ring_gather(kv, False, trace=kv_trace)
-    outer = (turned_low[4], turned_low[5], turned_low[3], turned_low[6])
+    def later(part):
+        return join([part], first_part)[0]
+
     if two_planes:
-        same = jnp.stack(ring_gather(second_part(*outer), True, {2: [inward]}), axis=0)
+        same = jnp.stack(
+            ring_gather(None, True, {2: [inward], 3: kv_trace[1]}, None, started[0]), axis=0
+        )
         cross = lax.ppermute(same, "fsdp", planes)
     else:
-        outer = [rows_gather(part) for part in outer]
         same, cross = [
-            jnp.stack(
-                ring_gather(
-                    second_part(*[jnp.split(part, 2, axis=1)[side] for part in outer]), True
-                ),
-                axis=0,
-            )
-            for side in range(2)
+            jnp.stack(ring_gather(None, True, state=state), axis=0) for state in started
         ]
-    second_parts = [same, cross] + [lax.ppermute(part, "ctx", partners) for part in (same, cross)]
-
     attn, logs = call(
         functools.partial(attend_kernel, chunks),
         seqs,
@@ -835,6 +848,8 @@
         ],
         us=11.0 * seqs * load,
     )
+    (cross,) = join([cross], attn)
+    second_parts = [same, cross] + [lax.ppermute(part, "ctx", partners) for part in (same, cross)]
     ff_wide = (seqs, rows, FF)
     (
         block_local,

time: 406 us -> 415 us (1.022)
  local copies, waits for them, and re-layouts: 47.8 us -> 61.8 us
  waiting for transfers between devices: 103 us -> 95.8 us
    ppermute x10, waiting for transfers between devices: 24.1 us -> 8.43 us  [ring_gather(): behind = lax.ppermute(behind, 'ctx', ring_pairs(chips, -1))]
    ppermute x11, waiting for transfers between devices: 26.5 us -> 42 us  [ring_gather(): ahead = lax.ppermute(ahead, 'ctx', ring_pairs(chips, 1))]
    unnamed x202 -> x227, local copies, waits for them, and re-layouts: 25 us -> 35.6 us
    ppermute x1, waiting for transfers between devices: 7.49 us -> 0.01 us  [body(): cross = lax.ppermute(same, 'fsdp', planes)]
    ppermute x10, starting transfers between devices: 10.9 us -> 6.15 us  [ring_gather(): behind = lax.ppermute(behind, 'ctx', ring_pairs(chips, -1))]
    ppermute x11, starting transfers between devices: 13 us -> 17.5 us  [ring_gather(): ahead = lax.ppermute(ahead, 'ctx', ring_pairs(chips, 1))]
  transfers between devices with their start and end apart: 63 -> 63, of which waited for: 30 -> 33; matrix products, arithmetic and copies ran while one was open for 22% -> 25% of each run, Pallas kernels for 17% -> 16%
where the time goes in v3:
time: 415 us; the launch traced here: 408 us
  Pallas kernels  133 us (32%)
  waiting for transfers between devices  95.8 us (23%)
  local copies, waits for them, and re-layouts  61.8 us (15%)
  starting transfers between devices  59.4 us (14%)
  other arithmetic  42.4 us (10%)
  matrix products  13.4 us (3%)
    pallas_call x9, Pallas kernels, call(): pl.pallas_call(body_of, grid_spec=pltpu.PrefetchScalarGridSpec(num_scalar...  133 us
    ppermute x11, waiting for transfers between devices, ring_gather(): ahead = lax.ppermute(ahead, 'ctx', ring_pairs(chips, 1))  42 us
    ppermute x28, waiting for transfers between devices, ring_scatter(): got = lax.ppermute(moving[way], 'ctx', ring_pairs(chips, sign))  40.9 us
    unnamed x227, local copies, waits for them, and re-layouts  35.6 us
    ppermute x28, starting transfers between devices, ring_scatter(): got = lax.ppermute(moving[way], 'ctx', ring_pairs(chips, sign))  28.8 us
    ppermute x11, starting transfers between devices, ring_gather(): ahead = lax.ppermute(ahead, 'ctx', ring_pairs(chips, 1))  17.5 us
    convert_element_type x16, other arithmetic, ring_scatter(): got = plus(got, terms[sign * left % chips]()).astype(bf16)  13.5 us
    dot_general x4, matrix products, weight_grad(): lax.dot_general(left, right, (((0, 1), (0, 1)), ((), ())), preferred_elem...  13.4 us
  transfers between devices with their start and end apart: 63, of which 33 were waited for; matrix products, arithmetic and copies ran while one was open for 25% of the time, Pallas kernels for 16%

profile of v3, /device:TPU:0, one launch (start us, length us, event | category | flops | bytes accessed | tf_op | source)
XLA Modules:
  0.0 408.4 jit_solution(7261875066969340282)
XLA Ops:
  3.6 3.0 collective-permute-start.1
  22.5 3.1 collective-permute-done.3
  28.3 1.8 collective-permute-done.4.refs_0_
  36.6 2.1 collective-permute-done.9
  40.7 2.4 collective-permute-done.10
  54.7 3.4 shard_map.487.refs_2_.refs_7_
  61.1 6.3 %shard_map.488 = (bf16[3,256,576]{2,1,0:T(8,128)(2,1)}, bf16[3,4,3,192,128]{4,3,2,1,0:T(8,128)(2,1)}, bf16[3,256,384]{2,1,0:T(8,128)(2,1)}) custom-call(bf16[3,256,576]{2,1,0:T(8,128)(2,1)} %pad_maximum_fusion.refs_0_.refs_1_, f32[1,576]{1,0:T(1,128)} %get-tuple-element.299.refs_1_, bf16[960,576]{1,0:T(8,128)(2,1)} %shard_map.487.refs_2_.refs_7_, ...), custom_call_target="tpu_custom_call" | custom-call | flops 7151699968 | bytes 6023424 | tf_op jit(solution)/shard_map/pallas_call | solution.py:536
  69.4 12.9 %collective-permute-done.17.refs_9_ = bf16[3,256,384]{2,1,0:T(8,128)(2,1)} collective-permute-done((bf16[3,256,384]{2,1,0:T(8,128)(2,1)}, bf16[3,256,384]{2,1,0:T(8,128)(2,1)}, u32[]{:S(2)}, u32[]{:S(2)}) %collective-permute-start.17) | collective-permute-done | bytes 589856 | tf_op jit(solution)/shard_map/ppermute | solution.py:603
  87.8 11.0 %collective-permute-done.18.refs_8_.refs_2_ = bf16[3,256,384]{2,1,0:T(8,128)(2,1)S(1)} collective-permute-done((bf16[3,256,384]{2,1,0:T(8,128)(2,1)}, bf16[3,256,384]{2,1,0:T(8,128)(2,1)S(1)}, u32[]{:S(2)}, u32[]{:S(2)}) %collective-permute-start.18) | collective-permute-done | bytes 589856 | tf_op jit(solution)/shard_map/ppermute | solution.py:603
  100.4 1.6 bitcast_dynamic-update-slice_fusion.5
  109.0 4.4 %collective-permute-done.24 = bf16[168,640]{1,0:T(8,128)(2,1)S(1)} collective-permute-done((bf16[168,640]{1,0:T(8,128)(2,1)}, bf16[168,640]{1,0:T(8,128)(2,1)S(1)}, u32[]{:S(2)}, u32[]{:S(2)}) %collective-permute-start.24) | collective-permute-done | bytes 215072 | tf_op jit(solution)/shard_map/ppermute | solution.py:606
  114.1 2.0 collective-permute-start.20
  121.0 6.1 %collective-permute-done.20.refs_6_ = bf16[3,256,384]{2,1,0:T(8,128)(2,1)S(1)} collective-permute-done((bf16[3,256,384]{2,1,0:T(8,128)(2,1)}, bf16[3,256,384]{2,1,0:T(8,128)(2,1)S(1)}, u32[]{:S(2)}, u32[]{:S(2)}) %collective-permute-start.20) | collective-permute-done | bytes 589856 | tf_op jit(solution)/shard_map/ppermute | solution.py:603
  127.9 33.5 %shard_map.489 = (bf16[3,256,576]{2,1,0:T(8,128)(2,1)}, f32[3,4,3,192,128]{4,3,2,1,0:T(8,128)}) custom-call(s32[3,32]{1,0:T(4,128)} %copy-done.87, bf16[3,4,3,192,128]{4,3,2,1,0:T(8,128)(2,1)} %get-tuple-element.82.refs_1_, bf16[3,256,384]{2,1,0:T(8,128)(2,1)} %get-tuple-element.83.refs_2_, bf16[3,256,384]{2,1,0:T(8,128)(2,1)} %collective-permute-done.14.refs_3_, ...), custom_call_target="tpu_custom_call" | custom-call | flops 38065500160 | bytes 10911744 | tf_op jit(solution)/shard_map/pallas_call | solution.py:536
  164.4 2.6 collective-permute-done.21
  168.2 26.0 %shard_map.493 = (f32[3,256,576]{2,1,0:T(8,128)}, bf16[3,256,576]{2,1,0:T(8,128)(2,1)}, bf16[3,256,1536]{2,1,0:T(8,128)(2,1)}, bf16[3,256,1536]{2,1,0:T(8,128)(2...) custom-call(s32[10]{0:T(128)} %pad_add_fusion.1.refs_0_, ...), custom_call_target="tpu_custom_call" | custom-call | flops 29991000064 | bytes 22815744 | tf_op jit(solution)/shard_map/pallas_call | solution.py:536
  194.1 29.8 %shard_map.494 = (bf16[2,256,576]{2,1,0:T(8,128)(2,1)}, bf16[2,256,384]{2,1,0:T(8,128)(2,1)}, bf16[2,256,384]{2,1,0:T(8,128)(2,1)}, bf16[2,256,384]{2,1,0:T(8,12...) custom-call(s32[3,32]{1,0:T(4,128)} %copy-done.87, ...), custom_call_target="tpu_custom_call" | custom-call | flops 39218999296 | bytes 16318464 | tf_op jit(solution)/shard_map/pallas_call | solution.py:536
  226.0 3.6 bitcast_convert_fusion.2
  229.7 1.8 bitcast_convert_fusion.3.refs_1_
  231.4 2.3 copy.215.refs_2_
  237.2 1.6 collective-permute-start.30
  240.7 3.5 bitcast_convert_fusion.1
  244.2 2.4 copy.216.refs_3_
  249.0 1.7 collective-permute-start.31
  253.6 4.5 %bitcast_convert_fusion.refs_4_ = bf16[576,1536]{1,0:T(8,128)(2,1)} fusion(bf16[3,256,1536]{2,1,0:T(8,128)(2,1)} %shard_map.498, bf16[3,128,576]{2,1,0:T(8,128)(2,1)S(1)} %copy-done.44, bf16[3,128,576]{2,1,0:T(8,128)(2,1)S(1)} %copy.244), kind=kOutput, calls=%fused_computation.2 | convolution fusion | flops 1361608704 | bytes 5013504 | tf_op jit(solution)/shard_map/dot_general | solution.py:669
  259.5 1.8 collective-permute-done.35.refs_6_.refs_3_
  262.1 7.8 %shard_map.499 = (bf16[8,168,640]{2,1,0:T(8,128)(2,1)}, bf16[8,168,640]{2,1,0:T(8,128)(2,1)}, bf16[8,168,640]{2,1,0:T(8,128)(2,1)}, bf16[8,168,640]{2,1,0:T(8,128)(2,1)}) custom-call(s32[10]{0:T(128)} %pad_add_fusion.1.refs_0_, bf16[576,576]{1,0:T(8,128)(2,1)} %bitcast_convert_fusion.3.refs_1_, bf16[1536,576]{1,0:T(8,128)(2,1)} %copy.215.refs_2_, ...), custom_call_target="tpu_custom_call" | custom-call | flops 8881949696 | bytes 12853248 | tf_op jit(solution)/shard_map/pallas_call | solution.py:536
  278.5 3.4 collective-permute-done.32.refs_2_
  281.8 2.0 convert_add_fusion.refs_3_
  283.9 3.1 add_convert_fusion
  287.4 16.8 %shard_map.500 = (bf16[1,256,576]{2,1,0:T(8,128)(2,1)}, bf16[1,256,384]{2,1,0:T(8,128)(2,1)}, bf16[1,256,384]{2,1,0:T(8,128)(2,1)}, bf16[1,256,384]{2,1,0:T(8,12...) custom-call(s32[3,32]{1,0:T(4,128)} %copy-done.87, ...), custom_call_target="tpu_custom_call" | custom-call | flops 19609499648 | bytes 14450688 | tf_op jit(solution)/shard_map/pallas_call | solution.py:536
  304.2 1.7 collective-permute-start.38
  305.9 4.9 %shard_map.495 = (f32[2,256,576]{2,1,0:T(8,128)}, bf16[2,256,1024]{2,1,0:T(8,128)(2,1)}, f32[2,1,576]{2,1,0:T(1,128)}) custom-call(bf16[3,256,576]{2,1,0:T(8,128)(2,1)} %pad_maximum_fusion.refs_0_.refs_1_, f32[1,576]{1,0:T(1,128)} %get-tuple-element.299.refs_1_, bf16[2,256,576]{2,1,0:T(8,128)(2,1)} %get-tuple-element.92.refs_2_, ...), custom_call_target="tpu_custom_call" | custom-call | flops 4614000128 | bytes 8157952 | tf_op jit(solution)/shard_map/pallas_call | solution.py:536
  313.9 1.7 collective-permute-start.39
  315.6 3.5 collective-permute-done.41
  319.7 1.7 collective-permute-start.40
  321.4 3.8 collective-permute-done.42
  328.0 4.9 %collective-permute-done.43 = bf16[1,256,384]{2,1,0:T(8,128)(2,1)S(1)} collective-permute-done((bf16[1,256,384]{2,1,0:T(8,128)(2,1)S(1)}, bf16[1,256,384]{2,1,0:T(8,128)(2,1)S(1)}, u32[]{:S(2)}, u32[]{:S(2)}) %collective-permute-start.43) | collective-permute-done | bytes 196640 | tf_op jit(solution)/shard_map/ppermute | solution.py:635
  335.1 2.5 collective-permute-done.49
  339.2 2.5 collective-permute-done.44
  342.5 2.9 shard_map.503
  347.0 1.6 collective-permute-start.48
  349.7 3.2 collective-permute-done.48
  354.5 2.3 fusion
  356.8 5.0 %shard_map.502 = (bf16[8,64,640]{2,1,0:T(8,128)(2,1)}, bf16[8,64,640]{2,1,0:T(8,128)(2,1)}) custom-call(s32[9]{0:T(128)} %pad_add_fusion.2.refs_0_, bf16[3,256,576]{2,1,0:T(8,128)(2,1)} %get-tuple-element.125.refs_1_, bf16[2,256,1024]{2,1,0:T(8,128)(2,1)} %get-tuple-element.126.refs_2_, bf16[1,256,1024]{2,1,0:T(8,128)(2,1)} %get-tuple-element.241.refs_3_, ...), custom_call_target="tpu_custom_call" | custom-call | flops 4037250048 | bytes 3772928 | tf_op jit(solution)/shard_map/pallas_call | solution.py:536
  364.8 2.5 copy.221
  373.3 4.6 %collective-permute-done.60 = bf16[168,640]{1,0:T(8,128)(2,1)S(1)} collective-permute-done((bf16[168,640]{1,0:T(8,128)(2,1)S(1)}, bf16[168,640]{1,0:T(8,128)(2,1)S(1)}, u32[]{:S(2)}, u32[]{:S(2)}) %collective-permute-start.60) | collective-permute-done | bytes 215072 | tf_op jit(solution)/shard_map/ppermute | solution.py:635
  383.6 2.4 collective-permute-done.53
  (439 shorter events, 146.3 us)
Async XLA Ops:
  3.6 10.8 %collective-permute-start.1 = (bf16[62,288]{1,0:T(8,128)(2,1)}, bf16[62,288]{1,0:T(8,128)(2,1)}, u32[]{:S(2)}, u32[]{:S(2)}) collective-permute-start(bf16[62,288]{1,0:T(8,128)(2,1)} %pad_maximum_fusion.4), channel_id=1, source_target_pairs={{0,1},{1,0},{2,3},{3,2},{4,5},{5,4},{6,7},{7,6},{8,9},{9,8},{10,11... | collective-permute-start | bytes 107144 | tf_op jit(solution)/shard_map/ppermute | solution.py:647
  8.4 45.2 %collective-permute-start = (bf16[3,128,576]{2,1,0:T(8,128)(2,1)S(1)}, bf16[3,128,576]{2,1,0:T(8,128)(2,1)S(1)}, u32[]{:S(2)}, u32[]{:S(2)}) collective-permute-start(bf16[3,128,576]{2,1,0:T(8,128)(2,1)S(1)} %copy.243), channel_id=1, source_target_pairs={{0,2},{2,0},{4,6},{6,4},{8,10},{10,8},{12,14},{14,12},{16,18},{18,... | collective-permute-start | bytes 1327112 | tf_op jit(solution)/shard_map/ppermute | solution.py:725
  16.0 15.7 %collective-permute-start.6 = (bf16[168,640]{1,0:T(8,128)(2,1)}, bf16[168,640]{1,0:T(8,128)(2,1)S(1)}, u32[]{:S(2)}, u32[]{:S(2)}) collective-permute-start(bf16[168,640]{1,0:T(8,128)(2,1)} %shard_map.485), channel_id=1, source_target_pairs={{0,8},{2,10},{8,16},{10,18},{16,24},{18,26},{24,28},{26,30},{28,20... | collective-permute-start | bytes 645128 | tf_op jit(solution)/shard_map/ppermute | solution.py:603
  17.5 14.1 %collective-permute-start.7 = (bf16[168,640]{1,0:T(8,128)(2,1)}, bf16[168,640]{1,0:T(8,128)(2,1)S(1)}, u32[]{:S(2)}, u32[]{:S(2)}) collective-permute-start(bf16[168,640]{1,0:T(8,128)(2,1)} %shard_map.485), channel_id=1, source_target_pairs={{0,4},{2,6},{8,0},{10,2},{16,8},{18,10},{24,16},{26,18},{28,24},{3... | collective-permute-start | bytes 645128 | tf_op jit(solution)/shard_map/ppermute | solution.py:606
  18.9 6.7 %collective-permute-start.3 = (bf16[64,640]{1,0:T(8,128)(2,1)S(1)}, bf16[64,640]{1,0:T(8,128)(2,1)S(1)}, u32[]{:S(2)}, u32[]{:S(2)}) collective-permute-start(bf16[64,640]{1,0:T(8,128)(2,1)S(1)} %pad.17), channel_id=1, source_target_pairs={{0,8},{2,10},{8,16},{10,18},{16,24},{18,26},{24,28},{26,30},{28,20... | collective-permute-start | bytes 245768 | tf_op jit(solution)/shard_map/ppermute | solution.py:603
  20.5 6.7 %collective-permute-start.2 = (bf16[64,640]{1,0:T(8,128)(2,1)S(1)}, bf16[64,640]{1,0:T(8,128)(2,1)S(1)}, u32[]{:S(2)}, u32[]{:S(2)}) collective-permute-start(bf16[64,640]{1,0:T(8,128)(2,1)S(1)} %pad.17), channel_id=1, source_target_pairs={{0,4},{2,6},{8,0},{10,2},{16,8},{18,10},{24,16},{26,18},{28,24},{3... | collective-permute-start | bytes 245768 | tf_op jit(solution)/shard_map/ppermute | solution.py:606
  33.0 7.0 %collective-permute-start.8 = (bf16[64,640]{1,0:T(8,128)(2,1)}, bf16[64,640]{1,0:T(8,128)(2,1)S(1)}, u32[]{:S(2)}, u32[]{:S(2)}) collective-permute-start(bf16[64,640]{1,0:T(8,128)(2,1)} %get-tuple-element.80), channel_id=1, source_target_pairs={{0,4},{2,6},{8,0},{10,2},{16,8},{18,10},{24,16},{26,18},{28,24},{3... | collective-permute-start | bytes 245768 | tf_op jit(solution)/shard_map/ppermute | solution.py:606
  47.5 7.3 %collective-permute-start.11 = (bf16[8,64,640]{2,1,0:T(8,128)(2,1)}, bf16[8,64,640]{2,1,0:T(8,128)(2,1)}, u32[]{:S(2)}, u32[]{:S(2)}) collective-permute-start(bf16[8,64,640]{2,1,0:T(8,128)(2,1)} %bitcast_dynamic-update-slice_fusion.8.refs_1_), channel_id=1, source_target_pairs={{0,2},{2,0},{4,6},{6,4},{8,10},{10,8},{12,14},{14,12},{16,18},{18,... | collective-permute-start | bytes 1966088 | tf_op jit(solution)/shard_map/ppermute | solution.py:751
  51.6 7.7 %collective-permute-start.12 = (bf16[168,640]{1,0:T(8,128)(2,1)S(1)}, bf16[168,640]{1,0:T(8,128)(2,1)S(1)}, u32[]{:S(2)}, u32[]{:S(2)}) collective-permute-start(bf16[168,640]{1,0:T(8,128)(2,1)S(1)} %copy-done.29), channel_id=1, source_target_pairs={{0,8},{2,10},{8,16},{10,18},{16,24},{18,26},{24,28},{26,30},{28,20... | collective-permute-start | bytes 645128 | tf_op jit(solution)/shard_map/ppermute | solution.py:603
  53.0 7.4 %collective-permute-start.13 = (bf16[168,640]{1,0:T(8,128)(2,1)S(1)}, bf16[168,640]{1,0:T(8,128)(2,1)S(1)}, u32[]{:S(2)}, u32[]{:S(2)}) collective-permute-start(bf16[168,640]{1,0:T(8,128)(2,1)S(1)} %copy-done.32), channel_id=1, source_target_pairs={{0,4},{2,6},{8,0},{10,2},{16,8},{18,10},{24,16},{26,18},{28,24},{3... | collective-permute-start | bytes 645128 | tf_op jit(solution)/shard_map/ppermute | solution.py:606
  67.4 15.0 %collective-permute-start.17 = (bf16[3,256,384]{2,1,0:T(8,128)(2,1)}, bf16[3,256,384]{2,1,0:T(8,128)(2,1)}, u32[]{:S(2)}, u32[]{:S(2)}) collective-permute-start(bf16[3,256,384]{2,1,0:T(8,128)(2,1)} %get-tuple-element.83.refs_2_), channel_id=1, source_target_pairs={{0,8},{2,10},{8,16},{10,18},{16,24},{18,26},{24,28},{26,30},{28,20... | collective-permute-start | bytes 1769480 | tf_op jit(solution)/shard_map/ppermute | solution.py:603
  69.0 15.0 %collective-permute-start.14 = (bf16[3,256,384]{2,1,0:T(8,128)(2,1)}, bf16[3,256,384]{2,1,0:T(8,128)(2,1)}, u32[]{:S(2)}, u32[]{:S(2)}) collective-permute-start(bf16[3,256,384]{2,1,0:T(8,128)(2,1)} %get-tuple-element.83.refs_2_), channel_id=1, source_target_pairs={{0,4},{2,6},{8,0},{10,2},{16,8},{18,10},{24,16},{26,18},{28,24},{3... | collective-permute-start | bytes 1769480 | tf_op jit(solution)/shard_map/ppermute | solution.py:606
  82.3 16.5 %collective-permute-start.18 = (bf16[3,256,384]{2,1,0:T(8,128)(2,1)}, bf16[3,256,384]{2,1,0:T(8,128)(2,1)S(1)}, u32[]{:S(2)}, u32[]{:S(2)}) collective-permute-start(bf16[3,256,384]{2,1,0:T(8,128)(2,1)} %collective-permute-done.17.refs_9_), channel_id=1, source_target_pairs={{0,8},{2,10},{8,16},{10,18},{16,24},{18,26},{24,28},{26,30},{28,20... | collective-permute-start | bytes 1769480 | tf_op jit(solution)/shard_map/ppermute | solution.py:603
  83.9 19.5 %collective-permute-start.15 = (bf16[3,256,384]{2,1,0:T(8,128)(2,1)}, bf16[3,256,384]{2,1,0:T(8,128)(2,1)S(1)}, u32[]{:S(2)}, u32[]{:S(2)}) collective-permute-start(bf16[3,256,384]{2,1,0:T(8,128)(2,1)} %collective-permute-done.14.refs_3_), channel_id=1, source_target_pairs={{0,4},{2,6},{8,0},{10,2},{16,8},{18,10},{24,16},{26,18},{28,24},{3... | collective-permute-start | bytes 1769480 | tf_op jit(solution)/shard_map/ppermute | solution.py:606
  85.8 17.6 %collective-permute-start.22 = (bf16[168,640]{1,0:T(8,128)(2,1)}, bf16[168,640]{1,0:T(8,128)(2,1)S(1)}, u32[]{:S(2)}, u32[]{:S(2)}) collective-permute-start(bf16[168,640]{1,0:T(8,128)(2,1)} %get-tuple-element.86), channel_id=1, source_target_pairs={{0,8},{2,10},{8,16},{10,18},{16,24},{18,26},{24,28},{26,30},{28,20... | collective-permute-start | bytes 645128 | tf_op jit(solution)/shard_map/ppermute | solution.py:603
  87.4 16.1 %collective-permute-start.23 = (bf16[168,640]{1,0:T(8,128)(2,1)}, bf16[168,640]{1,0:T(8,128)(2,1)S(1)}, u32[]{:S(2)}, u32[]{:S(2)}) collective-permute-start(bf16[168,640]{1,0:T(8,128)(2,1)} %get-tuple-element.85), channel_id=1, source_target_pairs={{0,4},{2,6},{8,0},{10,2},{16,8},{18,10},{24,16},{26,18},{28,24},{3... | collective-permute-start | bytes 645128 | tf_op jit(solution)/shard_map/ppermute | solution.py:606
  98.8 15.3 %collective-permute-start.19 = (bf16[3,256,384]{2,1,0:T(8,128)(2,1)S(1)}, bf16[3,256,384]{2,1,0:T(8,128)(2,1)}, u32[]{:S(2)}, u32[]{:S(2)}) collective-permute-start(bf16[3,256,384]{2,1,0:T(8,128)(2,1)S(1)} %collective-permute-done.18.refs_8_.refs_2_), channel_id=1, source_target_pairs={{0,8},{2,10},{8,16},{10,18},{16,24},{18,26},{24,28},{26,30},{28,20... | collective-permute-start | bytes 1769480 | tf_op jit(solution)/shard_map/ppermute | solution.py:603
  105.0 8.4 %collective-permute-start.24 = (bf16[168,640]{1,0:T(8,128)(2,1)}, bf16[168,640]{1,0:T(8,128)(2,1)S(1)}, u32[]{:S(2)}, u32[]{:S(2)}) collective-permute-start(bf16[168,640]{1,0:T(8,128)(2,1)} %get-tuple-element.87), channel_id=1, source_target_pairs={{0,4},{2,6},{8,0},{10,2},{16,8},{18,10},{24,16},{26,18},{28,24},{3... | collective-permute-start | bytes 645128 | tf_op jit(solution)/shard_map/ppermute | solution.py:606
  105.8 15.2 %collective-permute-start.16 = (bf16[3,256,384]{2,1,0:T(8,128)(2,1)}, bf16[3,256,384]{2,1,0:T(8,128)(2,1)S(1)}, u32[]{:S(2)}, u32[]{:S(2)}) collective-permute-start(bf16[3,256,384]{2,1,0:T(8,128)(2,1)} %copy-done.40), channel_id=1, source_target_pairs={{0,4},{2,6},{8,0},{10,2},{16,8},{18,10},{24,16},{26,18},{28,24},{3... | collective-permute-start | bytes 1769480 | tf_op jit(solution)/shard_map/ppermute | solution.py:606
  114.1 12.9 %collective-permute-start.20 = (bf16[3,256,384]{2,1,0:T(8,128)(2,1)}, bf16[3,256,384]{2,1,0:T(8,128)(2,1)S(1)}, u32[]{:S(2)}, u32[]{:S(2)}) collective-permute-start(bf16[3,256,384]{2,1,0:T(8,128)(2,1)} %collective-permute-done.19.refs_7_), channel_id=1, source_target_pairs={{0,8},{2,10},{8,16},{10,18},{16,24},{18,26},{24,28},{26,30},{28,20... | collective-permute-start | bytes 1769480 | tf_op jit(solution)/shard_map/ppermute | solution.py:603
  119.2 42.2 %collective-permute-start.25 = (bf16[8,168,640]{2,1,0:T(8,128)(2,1)}, bf16[8,168,640]{2,1,0:T(8,128)(2,1)S(1)}, u32[]{:S(2)}, u32[]{:S(2)}) collective-permute-start(bf16[8,168,640]{2,1,0:T(8,128)(2,1)} %bitcast_dynamic-update-slice_fusion.refs_5_), channel_id=1, source_target_pairs={{0,1},{1,0},{2,3},{3,2},{4,5},{5,4},{6,7},{7,6},{8,9},{9,8},{10,11... | collective-permute-start | bytes 5160968 | tf_op jit(solution)/shard_map/ppermute | solution.py:832
  119.7 48.4 %collective-permute-start.26 = (bf16[8,168,640]{2,1,0:T(8,128)(2,1)}, bf16[8,168,640]{2,1,0:T(8,128)(2,1)}, u32[]{:S(2)}, u32[]{:S(2)}) collective-permute-start(bf16[8,168,640]{2,1,0:T(8,128)(2,1)} %bitcast_dynamic-update-slice_fusion.refs_5_), channel_id=1, source_target_pairs={{0,2},{2,0},{4,6},{6,4},{8,10},{10,8},{12,14},{14,12},{16,18},{18,... | collective-permute-start | bytes 5160968 | tf_op jit(solution)/shard_map/ppermute | solution.py:852
  223.9 11.4 %collective-permute-start.29 = (bf16[2,256,384]{2,1,0:T(8,128)(2,1)}, bf16[2,256,384]{2,1,0:T(8,128)(2,1)S(1)}, u32[]{:S(2)}, u32[]{:S(2)}) collective-permute-start(bf16[2,256,384]{2,1,0:T(8,128)(2,1)} %get-tuple-element.94), channel_id=1, source_target_pairs={{0,8},{2,10},{8,16},{10,18},{16,24},{18,26},{24,28},{26,30},{28,20... | collective-permute-start | bytes 1179656 | tf_op jit(solution)/shard_map/ppermute | solution.py:635
  225.5 13.3 %collective-permute-start.33 = (bf16[2,256,384]{2,1,0:T(8,128)(2,1)}, bf16[2,256,384]{2,1,0:T(8,128)(2,1)}, u32[]{:S(2)}, u32[]{:S(2)}) collective-permute-start(bf16[2,256,384]{2,1,0:T(8,128)(2,1)} %get-tuple-element.98), channel_id=1, source_target_pairs={{0,4},{2,6},{8,0},{10,2},{16,8},{18,10},{24,16},{26,18},{28,24},{3... | collective-permute-start | bytes 1179656 | tf_op jit(solution)/shard_map/ppermute | solution.py:635
  237.2 10.6 %collective-permute-start.30 = (bf16[2,256,384]{2,1,0:T(8,128)(2,1)S(1)}, bf16[2,256,384]{2,1,0:T(8,128)(2,1)}, u32[]{:S(2)}, u32[]{:S(2)}) collective-permute-start(bf16[2,256,384]{2,1,0:T(8,128)(2,1)S(1)} %add_convert_fusion.5.refs_1_), channel_id=1, source_target_pairs={{0,8},{2,10},{8,16},{10,18},{16,24},{18,26},{24,28},{26,30},{28,20... | collective-permute-start | bytes 1179656 | tf_op jit(solution)/shard_map/ppermute | solution.py:635
  240.0 10.7 %collective-permute-start.34 = (bf16[2,256,384]{2,1,0:T(8,128)(2,1)S(1)}, bf16[2,256,384]{2,1,0:T(8,128)(2,1)}, u32[]{:S(2)}, u32[]{:S(2)}) collective-permute-start(bf16[2,256,384]{2,1,0:T(8,128)(2,1)S(1)} %add_convert_fusion.2.refs_2_), channel_id=1, source_target_pairs={{0,4},{2,6},{8,0},{10,2},{16,8},{18,10},{24,16},{26,18},{28,24},{3... | collective-permute-start | bytes 1179656 | tf_op jit(solution)/shard_map/ppermute | solution.py:635
  249.0 9.6 %collective-permute-start.31 = (bf16[2,256,384]{2,1,0:T(8,128)(2,1)S(1)}, bf16[2,256,384]{2,1,0:T(8,128)(2,1)S(1)}, u32[]{:S(2)}, u32[]{:S(2)}) collective-permute-start(bf16[2,256,384]{2,1,0:T(8,128)(2,1)S(1)} %add_convert_fusion.4.refs_1_), channel_id=1, source_target_pairs={{0,8},{2,10},{8,16},{10,18},{16,24},{18,26},{24,28},{26,30},{28,20... | collective-permute-start | bytes 1179656 | tf_op jit(solution)/shard_map/ppermute | solution.py:635
  251.8 9.5 %collective-permute-start.35 = (bf16[2,256,384]{2,1,0:T(8,128)(2,1)S(1)}, bf16[2,256,384]{2,1,0:T(8,128)(2,1)S(1)}, u32[]{:S(2)}, u32[]{:S(2)}) collective-permute-start(bf16[2,256,384]{2,1,0:T(8,128)(2,1)S(1)} %add_convert_fusion.1.refs_2_), channel_id=1, source_target_pairs={{0,4},{2,6},{8,0},{10,2},{16,8},{18,10},{24,16},{26,18},{28,24},{3... | collective-permute-start | bytes 1179656 | tf_op jit(solution)/shard_map/ppermute | solution.py:635
  269.9 14.0 %collective-permute-start.37 = (bf16[8,168,640]{2,1,0:T(8,128)(2,1)}, bf16[8,168,640]{2,1,0:T(8,128)(2,1)}, u32[]{:S(2)}, u32[]{:S(2)}) collective-permute-start(bf16[8,168,640]{2,1,0:T(8,128)(2,1)} %get-tuple-element.111), channel_id=1, source_target_pairs={{0,2},{2,0},{4,6},{6,4},{8,10},{10,8},{12,14},{14,12},{16,18},{18,... | collective-permute-start | bytes 5160968 | tf_op jit(solution)/shard_map/ppermute | solution.py:925
  269.9 17.5 %collective-permute-start.36 = (bf16[8,168,640]{2,1,0:T(8,128)(2,1)}, bf16[8,168,640]{2,1,0:T(8,128)(2,1)}, u32[]{:S(2)}, u32[]{:S(2)}) collective-permute-start(bf16[8,168,640]{2,1,0:T(8,128)(2,1)} %get-tuple-element.110), channel_id=1, source_target_pairs={{0,2},{2,0},{4,6},{6,4},{8,10},{10,8},{12,14},{14,12},{16,18},{18,... | collective-permute-start | bytes 5160968 | tf_op jit(solution)/shard_map/ppermute | solution.py:925
  270.4 11.4 %collective-permute-start.32 = (bf16[2,256,384]{2,1,0:T(8,128)(2,1)}, bf16[2,256,384]{2,1,0:T(8,128)(2,1)}, u32[]{:S(2)}, u32[]{:S(2)}) collective-permute-start(bf16[2,256,384]{2,1,0:T(8,128)(2,1)} %add_convert_fusion.3.refs_5_), channel_id=1, source_target_pairs={{0,8},{2,10},{8,16},{10,18},{16,24},{18,26},{24,28},{26,30},{28,20... | collective-permute-start | bytes 1179656 | tf_op jit(solution)/shard_map/ppermute | solution.py:635
  278.5 83.5 %collective-permute-start.28 = (f32[3,128,576]{1,2,0:T(8,128)}, f32[3,128,576]{1,2,0:T(8,128)}, u32[]{:S(2)}, u32[]{:S(2)}) collective-permute-start(f32[3,128,576]{1,2,0:T(8,128)} %copy.205), channel_id=1, source_target_pairs={{0,2},{2,0},{4,6},{6,4},{8,10},{10,8},{12,14},{14,12},{16,18},{18,... | collective-permute-start | bytes 2654216 | tf_op jit(solution)/shard_map/ppermute | solution.py:729
  287.0 38.9 %collective-permute-start.45 = (bf16[8,168,640]{2,1,0:T(8,128)(2,1)}, bf16[8,168,640]{2,1,0:T(8,128)(2,1)S(1)}, u32[]{:S(2)}, u32[]{:S(2)}) collective-permute-start(bf16[8,168,640]{2,1,0:T(8,128)(2,1)} %add_convert_fusion), channel_id=1, source_target_pairs={{0,1},{1,0},{2,3},{3,2},{4,5},{5,4},{6,7},{7,6},{8,9},{9,8},{10,11... | collective-permute-start | bytes 5160968 | tf_op jit(solution)/shard_map/ppermute | solution.py:927
  304.2 9.6 %collective-permute-start.38 = (bf16[1,256,384]{2,1,0:T(8,128)(2,1)}, bf16[1,256,384]{2,1,0:T(8,128)(2,1)S(1)}, u32[]{:S(2)}, u32[]{:S(2)}) collective-permute-start(bf16[1,256,384]{2,1,0:T(8,128)(2,1)} %get-tuple-element.116), channel_id=1, source_target_pairs={{0,8},{2,10},{8,16},{10,18},{16,24},{18,26},{24,28},{26,30},{28,20... | collective-permute-start | bytes 589832 | tf_op jit(solution)/shard_map/ppermute | solution.py:635
  313.1 6.0 %collective-permute-start.41 = (bf16[1,256,384]{2,1,0:T(8,128)(2,1)S(1)}, bf16[1,256,384]{2,1,0:T(8,128)(2,1)S(1)}, u32[]{:S(2)}, u32[]{:S(2)}) collective-permute-start(bf16[1,256,384]{2,1,0:T(8,128)(2,1)S(1)} %copy-done.59), channel_id=1, source_target_pairs={{0,4},{2,6},{8,0},{10,2},{16,8},{18,10},{24,16},{26,18},{28,24},{3... | collective-permute-start | bytes 589832 | tf_op jit(solution)/shard_map/ppermute | solution.py:635
  319.7 19.6 %collective-permute-start.40 = (bf16[1,256,384]{2,1,0:T(8,128)(2,1)S(1)}, bf16[1,256,384]{2,1,0:T(8,128)(2,1)S(1)}, u32[]{:S(2)}, u32[]{:S(2)}) collective-permute-start(bf16[1,256,384]{2,1,0:T(8,128)(2,1)S(1)} %add_convert_fusion.11), channel_id=1, source_target_pairs={{0,8},{2,10},{8,16},{10,18},{16,24},{18,26},{24,28},{26,30},{28,20... | collective-permute-start | bytes 589832 | tf_op jit(solution)/shard_map/ppermute | solution.py:635
  325.2 7.7 %collective-permute-start.43 = (bf16[1,256,384]{2,1,0:T(8,128)(2,1)S(1)}, bf16[1,256,384]{2,1,0:T(8,128)(2,1)S(1)}, u32[]{:S(2)}, u32[]{:S(2)}) collective-permute-start(bf16[1,256,384]{2,1,0:T(8,128)(2,1)S(1)} %add_convert_fusion.9), channel_id=1, source_target_pairs={{0,4},{2,6},{8,0},{10,2},{16,8},{18,10},{24,16},{26,18},{28,24},{3... | collective-permute-start | bytes 589832 | tf_op jit(solution)/shard_map/ppermute | solution.py:635
  327.5 10.1 %collective-permute-start.49 = (bf16[168,640]{1,0:T(8,128)(2,1)S(1)}, bf16[168,640]{1,0:T(8,128)(2,1)S(1)}, u32[]{:S(2)}, u32[]{:S(2)}) collective-permute-start(bf16[168,640]{1,0:T(8,128)(2,1)S(1)} %get-tuple-element.274), channel_id=1, source_target_pairs={{0,4},{2,6},{8,0},{10,2},{16,8},{18,10},{24,16},{26,18},{28,24},{3... | collective-permute-start | bytes 645128 | tf_op jit(solution)/shard_map/ppermute | solution.py:635
  333.0 8.7 %collective-permute-start.44 = (bf16[1,256,384]{2,1,0:T(8,128)(2,1)S(1)}, bf16[1,256,384]{2,1,0:T(8,128)(2,1)S(1)}, u32[]{:S(2)}, u32[]{:S(2)}) collective-permute-start(bf16[1,256,384]{2,1,0:T(8,128)(2,1)S(1)} %add_convert_fusion.8), channel_id=1, source_target_pairs={{0,4},{2,6},{8,0},{10,2},{16,8},{18,10},{24,16},{26,18},{28,24},{3... | collective-permute-start | bytes 589832 | tf_op jit(solution)/shard_map/ppermute | solution.py:635
  333.5 11.9 %collective-permute-start.47 = (bf16[168,640]{1,0:T(8,128)(2,1)S(1)}, bf16[168,640]{1,0:T(8,128)(2,1)}, u32[]{:S(2)}, u32[]{:S(2)}) collective-permute-start(bf16[168,640]{1,0:T(8,128)(2,1)S(1)} %get-tuple-element.275), channel_id=1, source_target_pairs={{0,8},{2,10},{8,16},{10,18},{16,24},{18,26},{24,28},{26,30},{28,20... | collective-permute-start | bytes 645128 | tf_op jit(solution)/shard_map/ppermute | solution.py:635
  338.7 6.7 %collective-permute-start.50 = (bf16[168,640]{1,0:T(8,128)(2,1)S(1)}, bf16[168,640]{1,0:T(8,128)(2,1)}, u32[]{:S(2)}, u32[]{:S(2)}) collective-permute-start(bf16[168,640]{1,0:T(8,128)(2,1)S(1)} %fusion.3), channel_id=1, source_target_pairs={{0,4},{2,6},{8,0},{10,2},{16,8},{18,10},{24,16},{26,18},{28,24},{3... | collective-permute-start | bytes 645128 | tf_op jit(solution)/shard_map/ppermute | solution.py:635
  361.8 10.0 %collective-permute-start.51 = (bf16[8,64,640]{2,1,0:T(8,128)(2,1)}, bf16[8,64,640]{2,1,0:T(8,128)(2,1)}, u32[]{:S(2)}, u32[]{:S(2)}) collective-permute-start(bf16[8,64,640]{2,1,0:T(8,128)(2,1)} %get-tuple-element.133), channel_id=1, source_target_pairs={{0,2},{2,0},{4,6},{6,4},{8,10},{10,8},{12,14},{14,12},{16,18},{18,... | collective-permute-start | bytes 1966088 | tf_op jit(solution)/shard_map/ppermute | solution.py:898
  368.5 34.6 %collective-permute-start.46 = (f32[3,128,576]{1,2,0:T(8,128)}, f32[3,128,576]{1,2,0:T(8,128)}, u32[]{:S(2)}, u32[]{:S(2)}) collective-permute-start(f32[3,128,576]{1,2,0:T(8,128)} %copy.222), channel_id=1, source_target_pairs={{0,2},{2,0},{4,6},{6,4},{8,10},{10,8},{12,14},{14,12},{16,18},{18,... | collective-permute-start | bytes 2654216 | tf_op jit(solution)/shard_map/ppermute | solution.py:729
  369.7 8.1 %collective-permute-start.60 = (bf16[168,640]{1,0:T(8,128)(2,1)S(1)}, bf16[168,640]{1,0:T(8,128)(2,1)S(1)}, u32[]{:S(2)}, u32[]{:S(2)}) collective-permute-start(bf16[168,640]{1,0:T(8,128)(2,1)S(1)} %copy-done.57), channel_id=1, source_target_pairs={{0,8},{2,10},{8,16},{10,18},{16,24},{18,26},{24,28},{26,30},{28,20... | collective-permute-start | bytes 645128 | tf_op jit(solution)/shard_map/ppermute | solution.py:635
  370.2 7.7 %collective-permute-start.62 = (bf16[168,640]{1,0:T(8,128)(2,1)S(1)}, bf16[168,640]{1,0:T(8,128)(2,1)S(1)}, u32[]{:S(2)}, u32[]{:S(2)}) collective-permute-start(bf16[168,640]{1,0:T(8,128)(2,1)S(1)} %copy-done.56), channel_id=1, source_target_pairs={{0,4},{2,6},{8,0},{10,2},{16,8},{18,10},{24,16},{26,18},{28,24},{3... | collective-permute-start | bytes 645128 | tf_op jit(solution)/shard_map/ppermute | solution.py:635
  372.8 7.7 %collective-permute-start.52 = (bf16[64,640]{1,0:T(8,128)(2,1)S(1)}, bf16[64,640]{1,0:T(8,128)(2,1)S(1)}, u32[]{:S(2)}, u32[]{:S(2)}) collective-permute-start(bf16[64,640]{1,0:T(8,128)(2,1)S(1)} %get-tuple-element.284), channel_id=1, source_target_pairs={{0,8},{2,10},{8,16},{10,18},{16,24},{18,26},{24,28},{26,30},{28,20... | collective-permute-start | bytes 245768 | tf_op jit(solution)/shard_map/ppermute | solution.py:635
  393.1 7.5 %collective-permute-start.55 = (bf16[64,640]{1,0:T(8,128)(2,1)S(1)}, bf16[64,640]{1,0:T(8,128)(2,1)S(1)}, u32[]{:S(2)}, u32[]{:S(2)}) collective-permute-start(bf16[64,640]{1,0:T(8,128)(2,1)S(1)} %get-tuple-element.280), channel_id=1, source_target_pairs={{0,8},{2,10},{8,16},{10,18},{16,24},{18,26},{24,28},{26,30},{28,20... | collective-permute-start | bytes 245768 | tf_op jit(solution)/shard_map/ppermute | solution.py:635
  394.1 6.5 %collective-permute-start.58 = (bf16[64,640]{1,0:T(8,128)(2,1)S(1)}, bf16[64,640]{1,0:T(8,128)(2,1)S(1)}, u32[]{:S(2)}, u32[]{:S(2)}) collective-permute-start(bf16[64,640]{1,0:T(8,128)(2,1)S(1)} %get-tuple-element.281), channel_id=1, source_target_pairs={{0,4},{2,6},{8,0},{10,2},{16,8},{18,10},{24,16},{26,18},{28,24},{3... | collective-permute-start | bytes 245768 | tf_op jit(solution)/shard_map/ppermute | solution.py:635
  (113 other events, 868.8 us)
